TPU v7x, 256 devices: a whole 4x4x8 slice. The times are simulated.
256 devices in a mesh: dp: 64 (over y_hi, z, x), group: 4 (over y_lo, core).
Axes of the slice: x: 4, y: 4 (y_hi: 2, y_lo: 2; y = y_hi * 2 + y_lo), z: 8, core: 2. Of those that a mesh axis runs over, the one named last changes fastest.
Arguments:
- acts: bfloat16 [2, 16384, 256], P(None, 'dp'), may hold values from -16 to 16
- out_grads: bfloat16 [2, 16384, 16384], P(None, 'dp', 'group'), may hold values from -0.046875 to 0.046875
- master: float32 [2, 256, 16384], P(None, 'dp', 'group'), may hold values from -0.078125 to 0.078125
- m_codes: int32 [2, 256, 16384], P(None, 'dp', 'group'), may hold values from -127 to 127
- m_scale: float32 [2, 256, 8], P(None, 'dp', 'group'), may hold values from 0.1 to 1
- v_codes: int32 [2, 256, 16384], P(None, 'dp', 'group'), may hold values from 1 to 255
- v_scale: float32 [2, 256, 8], P(None, 'dp', 'group'), may hold values from 0.001 to 0.02
Outputs:
- new_master: float32 [2, 256, 16384], P(None, 'dp', 'group')
- m_state: float32 [2, 256, 16384], P(None, 'dp', 'group')
- m_absmax: float32 [2, 256, 8], P(None, 'dp', 'group')
- v_state: float32 [2, 256, 16384], P(None, 'dp', 'group')
- v_absmax: float32 [2, 256, 8], P(None, 'dp', 'group')
- rollout: bfloat16 [2, 256, 16384], P(None, None, 'dp')
All inputs are finite; a program needn't handle non-finite values. Where the computation divides by a largest or mean magnitude, that divisor is 1e-20 or more.
Results may differ from a plain program's by a relative error of at most 0.001.
Values may be sent and summed in bfloat16 or wider, within the bound.
No kernel may reach another device: no remote copies, remote signals or barrier semaphores. Data moves between devices by JAX's collectives and lax.ppermute only.
A program may use at most 64 MiB of HBM per device.

v0:
```python
import jax
import jax.numpy as jnp
from jax import lax
from jax.sharding import PartitionSpec as P

BLOCK = 2048


beta_first = 0.9
beta_second = 0.999
first_bias = 1.0 - 0.9**10
second_bias = 1.0 - 0.999**10
learn_rate = 0.001
decay_rate = 0.1
adam_eps = 1e-08
scale_eps = 1e-06


def blocked(values):
    return values.reshape(values.shape[:-1] + (values.shape[-1] // BLOCK, BLOCK))


def adam_step(gradient, master, m_codes, m_scale, v_codes, v_scale):
    full_shape = gradient.shape
    m_old = blocked(m_codes.astype(jnp.float32)) * (m_scale[..., None] / 127.0)
    v_old = blocked(v_codes.astype(jnp.float32)) * (v_scale[..., None] / 255.0)
    grad_blocks = blocked(gradient)
    m_new = beta_first * m_old + (1.0 - beta_first) * grad_blocks
    v_new = beta_second * v_old + (1.0 - beta_second) * grad_blocks * grad_blocks
    update = m_new / first_bias / (jnp.sqrt(v_new / second_bias) + adam_eps)
    new_master = master - learn_rate * (update.reshape(full_shape) + decay_rate * master)
    m_absmax = jnp.max(jnp.abs(m_new), axis=-1)
    m_state = (m_new / (m_absmax[..., None] + scale_eps)).reshape(full_shape)
    v_absmax = jnp.max(v_new, axis=-1)
    v_state = (v_new / (v_absmax[..., None] + scale_eps)).reshape(full_shape)
    return (new_master, m_state, m_absmax, v_state, v_absmax)


def push_weights(weights):
    bf_weights = weights.astype(jnp.bfloat16)
    gathered = lax.all_gather(bf_weights, "group", axis=1, tiled=True)
    return lax.all_to_all(gathered, "dp", split_axis=1, concat_axis=0, tiled=True)


def on_device(acts, out_grads, master, m_codes, m_scale, v_codes, v_scale):
    summed = lax.psum_scatter(
        jnp.einsum("etr,etf->ref", acts, out_grads, preferred_element_type=jnp.float32),
        "dp",
        scatter_dimension=0,
        tiled=True,
    )
    gradient = jnp.swapaxes(summed, 0, 1)
    results = adam_step(gradient, master, m_codes, m_scale, v_codes, v_scale)
    pushed = [push_weights(results[0][expert]) for expert in range(2)]
    rollout = jnp.stack(pushed)
    return (results[0], results[1], results[2], results[3], results[4], rollout)


def solution(mesh):
    return jax.shard_map(
        on_device,
        mesh=mesh,
        in_specs=(
            P(None, "dp", None),
            P(None, "dp", "group"),
            P(None, "dp", "group"),
            P(None, "dp", "group"),
            P(None, "dp", "group"),
            P(None, "dp", "group"),
            P(None, "dp", "group"),
        ),
        out_specs=(
            P(None, "dp", "group"),
            P(None, "dp", "group"),
            P(None, "dp", "group"),
            P(None, "dp", "group"),
            P(None, "dp", "group"),
            P(None, None, "dp"),
        ),
        check_vma=False,
    )
```

profile of v0, /device:TPU:1, one launch (start us, length us, event | category | flops | bytes accessed | tf_op | source)
XLA Modules:
  0.0 814.0 jit_solution(10695839446405107698)
XLA Ops:
  7.2 0.0 copy-start
  7.2 0.0 all-reduce.3.cloned.1.call-start
  7.2 0.9 copy-done
  8.1 7.1 convolution_bitcast_fusion
  15.3 13.4 %copy.61 = f32[256,2,4096]{2,1,0:T(2,128)} copy(f32[256,2,4096]{0,2,1:T(8,128)} %convolution_bitcast_fusion) | data formatting | bytes 16777216 | tf_op jit(solution)/shard_map/etr,etf->ref/transpose | solution.py:47
  28.7 0.0 copy-start.6
  28.7 0.0 copy-start.3
  28.7 0.0 all-reduce.3.cloned.1.call-update
  28.8 0.6 copy-done.4
  29.4 0.1 copy.59
  29.5 0.1 mul.91
  29.6 0.2 mul.92
  29.8 0.0 copy-done.5
  29.8 0.1 copy.63
  29.9 0.1 mul.98
  30.0 0.2 mul.99
  30.1 0.0 copy-done.2
  30.2 0.1 copy_convert_fusion.1
  30.3 0.2 reshape.52
  30.4 0.0 copy-done.1
  30.4 0.1 copy_convert_fusion
  30.6 0.2 reshape.54
  30.7 0.0 copy-done.6
  30.7 0.6 dynamic-slice
  32.0 680.3 %all-reduce.3.cloned.1.call-done = f32[256,2,4096]{2,1,0:T(2,128)} async-done(((f32[256,2,4096]{2,1,0:T(2,128)}), f32[256,2,4096]{2,1,0:T(2,128)}) %all-reduce.3.cloned.1.call-update) | async-done | bytes 8388624
  712.3 1.5 fusion.5
  713.9 0.2 reshape.53
  714.0 0.1 fusion.6
  714.1 49.9 %all-gather.1 = bf16[1,4,16384]{2,0,1:T(2,128)(2,1)S(1)} all-gather(bf16[1,4,4096]{2,0,1:T(2,128)(2,1)S(1)} %get-tuple-element.38), channel_id=3, replica_groups=mesh['dp'=64,'group'=4] {'group'}, dimensions={2}, use_global_device_ids=true | all-gather | bytes 163840 | tf_op jit(solution)/shard_map/all_gather | solution.py:41
  764.0 1.5 reduce.1
  765.5 8.4 %all-to-all-start.1 = ((bf16[4,64,256]{2,0,1:T(4,128)(2,1)}), bf16[4,64,256]{2,0,1:T(4,128)(2,1)S(1)}, u32[]{:S(2)}, u32[]{:S(2)}) async-start(bf16[4,64,256]{2,0,1:T(4,128)(2,1)} %bitcast.6), calls=%async_computation.1 | async-start | bytes 262144 | tf_op jit(solution)/shard_map/all_to_all | solution.py:42
  773.9 0.4 fusion.2
  774.3 0.1 div.51
  774.4 0.2 div.52
  774.6 0.1 div.54
  774.7 0.2 div.55
  774.9 6.4 all-gather
  781.3 1.5 reduce
  782.7 2.7 all-to-all-done.1
  785.4 9.5 %all-to-all-start = ((bf16[4,64,256]{2,0,1:T(4,128)(2,1)}), bf16[4,64,256]{2,0,1:T(4,128)(2,1)S(1)}, u32[]{:S(2)}, u32[]{:S(2)}) async-start(bf16[4,64,256]{2,0,1:T(4,128)(2,1)} %bitcast.5), calls=%async_computation | async-start | bytes 262144 | tf_op jit(solution)/shard_map/all_to_all | solution.py:42
  794.9 0.4 fusion.4
  795.4 0.7 copy.70
  796.0 0.7 copy.72
  796.7 0.7 copy.69
  797.5 0.7 copy.71
  798.2 0.7 copy.68
  799.0 7.4 all-to-all-done
  806.4 0.7 pad_maximum_fusion
  (10 shorter events, 0.1 us)
Async XLA Ops:
  7.2 1.0 copy-start
  7.2 705.1 %all-reduce.3.cloned.1.call-start = ((), (), s32[]{:S(2)}) async-start(), calls=%async_computation.2 | async-start | bytes 16777216
  28.7 0.7 copy-start.4
  28.7 1.1 copy-start.5
  28.7 1.5 copy-start.2
  28.7 1.7 copy-start.1
  28.7 2.0 copy-start.6
  28.7 683.6 %copy-start.3 = (f32[2,4,4096]{2,1,0:T(4,128)S(1)}, f32[2,4,4096]{2,1,0:T(4,128)}, u32[]{:S(2)}) copy-start(f32[2,4,4096]{2,1,0:T(4,128)} %param.9) | copy-start | bytes 393220
  765.5 19.9 %all-to-all-start.1 = ((bf16[4,64,256]{2,0,1:T(4,128)(2,1)}), bf16[4,64,256]{2,0,1:T(4,128)(2,1)S(1)}, u32[]{:S(2)}, u32[]{:S(2)}) async-start(bf16[4,64,256]{2,0,1:T(4,128)(2,1)} %bitcast.6), calls=%async_computation.1 | async-start | bytes 262144 | tf_op jit(solution)/shard_map/all_to_all | solution.py:42
  785.4 21.0 %all-to-all-start = ((bf16[4,64,256]{2,0,1:T(4,128)(2,1)}), bf16[4,64,256]{2,0,1:T(4,128)(2,1)S(1)}, u32[]{:S(2)}, u32[]{:S(2)}) async-start(bf16[4,64,256]{2,0,1:T(4,128)(2,1)} %bitcast.5), calls=%async_computation | async-start | bytes 262144 | tf_op jit(solution)/shard_map/all_to_all | solution.py:42
Sparse Core Ops, SparseCore 0:
  28.9 683.3 all-reduce.2
where the time goes:
time: 815 us; the launch traced here: 814 us
  waiting for transfers between devices  690 us (85%)
  blocking collectives  56.3 us (7%)
  local copies, waits for them, and re-layouts  21 us (3%)
  starting transfers between devices  18 us (2%)
  between operations  14.9 us (2%)
    unnamed x2, waiting for transfers between devices  680 us
    all_gather x2, blocking collectives, push_weights(): gathered = lax.all_gather(bf_weights, 'group', axis=1, tiled=True)  56.3 us
    all_to_all x2, starting transfers between devices, push_weights(): lax.all_to_all(gathered, 'dp', split_axis=1, concat_axis=0, tiled=True)  18 us
  transfers between devices with their start and end apart: 3, of which 3 were waited for; matrix products, arithmetic and copies ran while one was open for 1% of the time, Pallas kernels for 0%

commit v1 on v0

v1 whole, which is shorter than its diff:
```python
import functools

import jax
import jax.numpy as jnp
from jax import lax
from jax.experimental import pallas as pl
from jax.experimental.pallas import tpu as pltpu
from jax.sharding import PartitionSpec as P

BLOCK = 2048
LANES = 128
TOP = 32700.0
STEPS = 16.0

beta_first = 0.9
beta_second = 0.999
first_bias = 1.0 - 0.9**10
second_bias = 1.0 - 0.999**10
learn_rate = 0.001
decay_rate = 0.1
adam_eps = 1e-08
scale_eps = 1e-06

FIRST = 2560

PARAMS = pltpu.CompilerParams(vmem_limit_bytes=48 * 1024 * 1024)

Z_GROUPS = [[y * 32 + z * 4 + x for z in range(8)] for y in range(2) for x in range(4)]
YX_GROUPS = [[y * 32 + z * 4 + x for y in range(2) for x in range(4)] for z in range(8)]


def z_shift(k):
    return [
        (y * 32 + z * 4 + x, y * 32 + ((z + k) % 8) * 4 + x)
        for y in range(2)
        for z in range(8)
        for x in range(4)
    ]


def level_of(top):
    return jnp.ceil(STEPS * jnp.log2(jnp.maximum(top, 1e-30)))


def step_of(level):
    return jnp.exp2(level * (1.0 / STEPS)) * (1.0 / TOP)


def unit_of(level):
    return jnp.exp2(level * (-1.0 / STEPS)) * TOP


def coded(values, unit):
    return jnp.round(values * unit).astype(jnp.int32).astype(jnp.int16)


def decoded(codes):
    return codes.astype(jnp.int32).astype(jnp.float32)


def lane_max(top, values):
    for j in range(values.shape[1] // LANES):
        top = jnp.maximum(top, jnp.abs(values[:, j * LANES : (j + 1) * LANES]))
    return top


def pieces(width, size):
    return [(at, min(size, width - at)) for at in range(0, width, size)]


def partial_kernel(z_first, zs_ref, acts_ref, grads_ref, *rest):
    outs, sums = rest[:-1], rest[-1]
    width = grads_ref.shape[2]
    new = lax.broadcasted_iota(jnp.int32, (256, 256), 0)
    row = lax.broadcasted_iota(jnp.int32, (256, 256), 1)
    i = new & 3
    if z_first:
        x, y = (new >> 2) & 3, (new >> 4) & 1
        z = ((new >> 5) + zs_ref[0]) & 7
    else:
        z, x, y = (new >> 2) & 7, (new >> 5) & 3, new >> 7
    pick = jnp.where(row == y * 128 + z * 16 + x * 4 + i, 1.0, 0.0).astype(jnp.bfloat16)
    lhs = lax.dot_general(
        pick, acts_ref[0], (((1,), (1,)), ((), ())), preferred_element_type=jnp.float32
    ).astype(jnp.bfloat16)
    top = jnp.zeros((256, LANES), jnp.float32)
    for at, size in pieces(width, 512):
        part = jnp.dot(lhs, grads_ref[0, :, at : at + size], preferred_element_type=jnp.float32)
        sums[:, at : at + size] = part
        top = lane_max(top, part)
    level = level_of(jnp.max(top, axis=1, keepdims=True))
    unit = unit_of(level)
    note = jnp.broadcast_to(level, (256, LANES)).astype(jnp.int32).astype(jnp.int16)
    for b in range(8):
        rows = slice(b * 32, (b + 1) * 32)
        out = outs[b].at[0] if z_first else outs[0].at[b, 0]
        for at, size in pieces(width, 512):
            out[:, at : at + size] = coded(sums[rows, at : at + size], unit[rows])
        out[:, width:] = note[rows]


def partial_codes(acts, out_grads, zs, start, width, z_first):
    block = (2, 32, width + LANES)
    if z_first:
        out_shape = [jax.ShapeDtypeStruct(block, jnp.int16)] * 8
        out_specs = [pl.BlockSpec((1, 32, width + LANES), lambda e: (e, 0, 0))] * 8
    else:
        out_shape = [jax.ShapeDtypeStruct((8,) + block, jnp.int16)]
        out_specs = [pl.BlockSpec((8, 1, 32, width + LANES), lambda e: (0, e, 0, 0))]
    return pl.pallas_call(
        functools.partial(partial_kernel, z_first),
        grid=(2,),
        in_specs=[
            pl.BlockSpec(memory_space=pltpu.SMEM),
            pl.BlockSpec((1, 256, 256), lambda e: (e, 0, 0)),
            pl.BlockSpec((pl.Element(1), pl.Element(256), pl.Element(width)), lambda e: (e, 0, start)),
        ],
        out_shape=out_shape,
        out_specs=out_specs,
        scratch_shapes=[pltpu.VMEM((256, width), jnp.float32)],
        compiler_params=PARAMS,
        cost_estimate=pl.CostEstimate(
            flops=2 * 2 * 256 * 256 * width, bytes_accessed=2 * 256 * width * 4, transcendentals=0
        ),
    )(zs, acts, out_grads)


def regroup_kernel(*refs):
    *ins, out, sums = refs
    width = sums.shape[2]
    half = width // 2
    sources = [ins[0].at[s] for s in range(8)] if len(ins) == 1 else list(ins)
    for e in range(2):
        steps = [step_of(decoded(s[e, :, width:])[:, :1]) for s in sources]
        for at, size in pieces(width, 256):
            total = decoded(sources[0][e, :, at : at + size]) * steps[0]
            for s in range(1, 8):
                total = total + decoded(sources[s][e, :, at : at + size]) * steps[s]
            sums[e, :, at : at + size] = total
    upper = lax.broadcasted_iota(jnp.int32, (8, 1), 0) < 4
    for h in range(2):
        for b in range(0, 8, 2):
            tile = slice(b * 4, b * 4 + 8)
            first = sums[0, tile, h * half : (h + 1) * half]
            second = sums[1, tile, h * half : (h + 1) * half]
            even = jnp.where(upper, first, pltpu.roll(second, 4, 0))
            odd = jnp.where(upper, pltpu.roll(first, 4, 0), second)
            for k, values in ((b, even), (b + 1, odd)):
                top = lane_max(jnp.zeros((8, LANES), jnp.float32), values)
                level = level_of(jnp.max(top, axis=1, keepdims=True))
                note = jnp.broadcast_to(level, (8, LANES)).astype(jnp.int32).astype(jnp.int16)
                out[k, h * 8 : (h + 1) * 8, :half] = coded(values, unit_of(level))
                out[k, h * 8 : (h + 1) * 8, half:] = note


def regroup(received, width):
    return pl.pallas_call(
        regroup_kernel,
        out_shape=jax.ShapeDtypeStruct((8, 16, width // 2 + LANES), jnp.int16),
        scratch_shapes=[pltpu.VMEM((2, 32, width), jnp.float32)],
        compiler_params=PARAMS,
        cost_estimate=pl.CostEstimate(flops=8 * 64 * width * 4, bytes_accessed=8 * 64 * width * 2, transcendentals=0),
    )(*received)


def adam_kernel(a_ref, b_ref, master, m_codes, m_scale, v_codes, v_scale,
                new_master, m_state, m_absmax, v_state, v_absmax, rollout, grad):
    start = 0
    for ref in (a_ref, b_ref):
        half = ref.shape[2] - LANES
        total = None
        for s in range(8):
            term = decoded(ref[s, :, :half]) * step_of(decoded(ref[s, :, half:])[:, :1])
            total = term if total is None else total + term
        for h in range(2):
            grad[:, start : start + half] = total[h * 8 : (h + 1) * 8]
            start += half
    for e in range(2):
        for b in range(2):
            cols = slice(b * BLOCK, (b + 1) * BLOCK)
            g = grad[e * 4 : (e + 1) * 4, cols]
            m_old = m_codes[e, :, cols].astype(jnp.float32) * (m_scale[e, :, b : b + 1] / 127.0)
            v_old = v_codes[e, :, cols].astype(jnp.float32) * (v_scale[e, :, b : b + 1] / 255.0)
            m_new = beta_first * m_old + (1.0 - beta_first) * g
            v_new = beta_second * v_old + (1.0 - beta_second) * g * g
            update = m_new / first_bias / (jnp.sqrt(v_new / second_bias) + adam_eps)
            old = master[e, :, cols]
            new = old - learn_rate * (update + decay_rate * old)
            new_master[e, :, cols] = new
            m_top = jnp.max(jnp.abs(m_new), axis=1, keepdims=True)
            v_top = jnp.max(v_new, axis=1, keepdims=True)
            m_absmax[e, :, b : b + 1] = m_top
            v_absmax[e, :, b : b + 1] = v_top
            m_state[e, :, cols] = m_new / (m_top + scale_eps)
            v_state[e, :, cols] = v_new / (v_top + scale_eps)
            grad[e * 4 : (e + 1) * 4, cols] = new
    for k in range(16):
        for h in range(2):
            at = k * 256 + h * LANES
            rollout[k, h * 8 : (h + 1) * 8, :] = grad[:, at : at + LANES].astype(jnp.bfloat16)


def adam(a, b, master, m_codes, m_scale, v_codes, v_scale):
    big = jax.ShapeDtypeStruct((2, 4, 4096), jnp.float32)
    small = jax.ShapeDtypeStruct((2, 4, 2), jnp.float32)
    return pl.pallas_call(
        adam_kernel,
        out_shape=[big, big, small, big, small, jax.ShapeDtypeStruct((16, 16, LANES), jnp.bfloat16)],
        scratch_shapes=[pltpu.VMEM((8, 4096), jnp.float32)],
        compiler_params=PARAMS,
        cost_estimate=pl.CostEstimate(flops=2 * 4 * 4096 * 40, bytes_accessed=2 << 20, transcendentals=0),
    )(a, b, master, m_codes, m_scale, v_codes, v_scale)


def push_weights(weights):
    gathered = lax.all_gather(weights, "group", axis=0, tiled=True)
    swapped = lax.all_to_all(gathered, "dp", split_axis=0, concat_axis=0, tiled=True)
    spread = swapped.reshape(64, 2, 2, 4, LANES)
    return jnp.transpose(spread, (2, 0, 3, 1, 4)).reshape(2, 256, 256)


def on_device(acts, out_grads, master, m_codes, m_scale, v_codes, v_scale):
    width = out_grads.shape[2]
    me = lax.axis_index("dp")
    zs = ((me >> 2) & 7).reshape(1).astype(jnp.int32)
    [first] = partial_codes(acts, out_grads, zs, 0, FIRST, False)
    second = partial_codes(acts, out_grads, zs, FIRST, width - FIRST, True)
    second = [second[0]] + [lax.ppermute(second[k], "dp", z_shift(k)) for k in range(1, 8)]
    first = lax.all_to_all(first, "dp", 0, 0, axis_index_groups=YX_GROUPS, tiled=True)
    first = regroup([first], FIRST)
    second = regroup(second, width - FIRST)
    first = lax.all_to_all(first, "dp", 0, 0, axis_index_groups=Z_GROUPS, tiled=True)
    second = lax.all_to_all(second, "dp", 0, 0, axis_index_groups=YX_GROUPS, tiled=True)
    *state, weights = adam(first, second, master, m_codes, m_scale, v_codes, v_scale)
    return (*state, push_weights(weights))


def solution(mesh):
    split = P(None, "dp", "group")
    return jax.shard_map(
        on_device,
        mesh=mesh,
        in_specs=(P(None, "dp", None),) + (split,) * 6,
        out_specs=(split,) * 5 + (P(None, None, "dp"),),
        check_vma=False,
    )
```

time: 815 us -> 128 us (0.16)
  waiting for transfers between devices: 690 us -> 55.1 us
  blocking collectives: 56.3 us -> 9.54 us
  starting transfers between devices: 18 us -> 45.8 us
  local copies, waits for them, and re-layouts: 21 us -> 5.76 us
  between operations: 14.9 us -> 0.71 us
  Pallas kernels: 0 us -> 10.1 us
    unnamed x2 -> x0, waiting for transfers between devices: 680 us -> none
    all_gather x2 -> x1, blocking collectives: 56.3 us -> 9.54 us  [push_weights(): gathered = lax.all_gather(weights, 'group', axis=0, tiled=True)]
    ppermute x0 -> x7, waiting for transfers between devices: none -> 26.3 us  [on_device(): lax.ppermute(second[k], 'dp', z_shift(k))]
    ppermute x0 -> x7, starting transfers between devices: none -> 20.8 us  [on_device(): lax.ppermute(second[k], 'dp', z_shift(k))]
    all_to_all x2 -> x4, waiting for transfers between devices: 10.1 us -> 28.8 us  [the longest x1 11.7 us: push_weights(): lax.all_to_all(gathered, 'dp', split_axis=0, concat_axis=0, tiled=True)]
    transpose x1, local copies, waits for them, and re-layouts: 13.4 us -> 0.21 us  [push_weights(): return jnp.transpose(spread, (2, 0, 3, 1, 4)).reshape(2, 256, 256)]
    pallas_call x0 -> x5, Pallas kernels: none -> 10.1 us  [the longest x2 6.07 us: partial_codes(): pl.pallas_call(functools.partial(partial_kernel, z_first), grid=(2,), in_...]
    all_to_all x2 -> x4, starting transfers between devices: 18 us -> 25.1 us  [the longest x1 7.61 us: on_device(): lax.all_to_all(first, 'dp', 0, 0, axis_index_groups=YX_GROUPS, tiled=True)]
  transfers between devices with their start and end apart: 3 -> 11, of which waited for: 3 -> 8; matrix products, arithmetic and copies ran while one was open for 1% -> 1% of each run, Pallas kernels for 0% -> 4%
where the time goes in v1:
time: 128 us; the launch traced here: 127 us
  waiting for transfers between devices  55.1 us (43%)
  starting transfers between devices  45.8 us (36%)
  Pallas kernels  10.1 us (8%)
  blocking collectives  9.54 us (7%)
  local copies, waits for them, and re-layouts  5.76 us (4%)
    ppermute x7, waiting for transfers between devices, on_device(): lax.ppermute(second[k], 'dp', z_shift(k))  26.3 us
    ppermute x7, starting transfers between devices, on_device(): lax.ppermute(second[k], 'dp', z_shift(k))  20.8 us
    all_to_all x1, waiting for transfers between devices, push_weights(): lax.all_to_all(gathered, 'dp', split_axis=0, concat_axis=0, tiled=True)  11.7 us
    all_to_all x1, waiting for transfers between devices, on_device(): lax.all_to_all(first, 'dp', 0, 0, axis_index_groups=Z_GROUPS, tiled=True)  11.2 us
    all_gather x1, blocking collectives, push_weights(): gathered = lax.all_gather(weights, 'group', axis=0, tiled=True)  9.54 us
    all_to_all x1, starting transfers between devices, on_device(): lax.all_to_all(first, 'dp', 0, 0, axis_index_groups=YX_GROUPS, tiled=True)  7.61 us
    all_to_all x1, starting transfers between devices, on_device(): lax.all_to_all(second, 'dp', 0, 0, axis_index_groups=YX_GROUPS, tiled=True)  6.86 us
    pallas_call x2, Pallas kernels, partial_codes(): pl.pallas_call(functools.partial(partial_kernel, z_first), grid=(2,), in_...  6.07 us
  transfers between devices with their start and end apart: 11, of which 8 were waited for; matrix products, arithmetic and copies ran while one was open for 1% of the time, Pallas kernels for 4%

profile of v1, /device:TPU:1, one launch (start us, length us, event | category | flops | bytes accessed | tf_op | source)
XLA Modules:
  0.0 127.0 jit_solution(5691202189039427666)
XLA Ops:
  0.6 0.0 copy-start.1
  0.6 0.9 copy-done.1
  1.6 4.4 %shard_map.118 = s16[8,2,32,2688]{3,2,1,0:T(8,128)(2,1)} custom-call(s32[1]{0:T(128)} %bitcast.zs_ref, bf16[2,256,256]{2,1,0:T(8,128)(2,1)S(1)} %copy-done.1, bf16[2,256,4096]{2,1,0:T(8,128)(2,1)} %grads_ref.3), custom_call_target="tpu_custom_call" | custom-call | flops 671088640 | bytes 5242880 | tf_op jit(solution)/shard_map/pallas_call | solution.py:110
  6.0 0.0 copy-start.2
  6.0 7.6 %all-to-all-start = ((s16[8,2,32,2688]{3,2,1,0:T(8,128)(2,1)}), s16[8,2,32,2688]{3,2,1,0:T(8,128)(2,1)S(1)}, u32[]{:S(2)}, u32[]{:S(2)}) async-start(s16[8,2,32,2688]{3,2,1,0:T(8,128)(2,1)} %shard_map.118), calls=%async_computation | async-start | bytes 5505024 | tf_op jit(solution)/shard_map/all_to_all | solution.py:229
  13.6 0.0 copy-done.2
  13.6 0.0 copy-start
  13.6 2.2 %copy-done = bf16[2,256,4096]{2,1,0:T(8,128)(2,1)S(1)} copy-done((bf16[2,256,4096]{2,1,0:T(8,128)(2,1)S(1)}, bf16[2,256,4096]{2,1,0:T(8,128)(2,1)}, u32[]{:S(2)}) %copy-start) | copy-done | bytes 4194328
  15.8 1.7 %shard_map.120 = (s16[2,32,1664]{2,1,0:T(8,128)(2,1)S(1)}, s16[2,32,1664]{2,1,0:T(8,128)(2,1)S(1)}, s16[2,32,1664]{2,1,0:T(8,128)(2,1)S(1)}, s16[2,32,1664]{2,1,...) custom-call(s32[1]{0:T(128)} %bitcast.zs_ref, ...), custom_call_target="tpu_custom_call" | custom-call | flops 402653184 | bytes 3145728 | tf_op jit(solution)/shard_map/pallas_call | solution.py:110
  17.5 1.7 %collective-permute-start = (s16[2,32,1664]{2,1,0:T(8,128)(2,1)S(1)}, s16[2,32,1664]{2,1,0:T(8,128)(2,1)S(1)}, u32[]{:S(2)}, u32[]{:S(2)}) collective-permute-start(s16[2,32,1664]{2,1,0:T(8,128)(2,1)S(1)} %get-tuple-element.21), channel_id=1, source_target_pairs={{0,16},{4,20},{8,24},{12,28},{16,32},{20,36},{24,40},{28,44},{32,4... | collective-permute-start | bytes 638984 | tf_op jit(solution)/shard_map/ppermute | solution.py:228
  19.2 3.0 %collective-permute-start.1 = (s16[2,32,1664]{2,1,0:T(8,128)(2,1)S(1)}, s16[2,32,1664]{2,1,0:T(8,128)(2,1)S(1)}, u32[]{:S(2)}, u32[]{:S(2)}) collective-permute-start(s16[2,32,1664]{2,1,0:T(8,128)(2,1)S(1)} %get-tuple-element.22), channel_id=1, source_target_pairs={{0,32},{4,36},{8,40},{12,44},{16,48},{20,52},{24,56},{28,60},{32,6... | collective-permute-start | bytes 638984 | tf_op jit(solution)/shard_map/ppermute | solution.py:228
  22.2 3.8 %collective-permute-start.2 = (s16[2,32,1664]{2,1,0:T(8,128)(2,1)S(1)}, s16[2,32,1664]{2,1,0:T(8,128)(2,1)S(1)}, u32[]{:S(2)}, u32[]{:S(2)}) collective-permute-start(s16[2,32,1664]{2,1,0:T(8,128)(2,1)S(1)} %get-tuple-element.23), channel_id=1, source_target_pairs={{0,48},{4,52},{8,56},{12,60},{16,64},{20,68},{24,72},{28,76},{32,8... | collective-permute-start | bytes 638984 | tf_op jit(solution)/shard_map/ppermute | solution.py:228
  26.0 0.4 collective-permute-start.3
  26.4 4.5 %collective-permute-start.4 = (s16[2,32,1664]{2,1,0:T(8,128)(2,1)S(1)}, s16[2,32,1664]{2,1,0:T(8,128)(2,1)S(1)}, u32[]{:S(2)}, u32[]{:S(2)}) collective-permute-start(s16[2,32,1664]{2,1,0:T(8,128)(2,1)S(1)} %get-tuple-element.25), channel_id=1, source_target_pairs={{0,80},{4,84},{8,88},{12,92},{16,96},{20,100},{24,104},{28,108},{3... | collective-permute-start | bytes 638984 | tf_op jit(solution)/shard_map/ppermute | solution.py:228
  30.9 0.0 collective-permute-done.refs_1_
  30.9 2.4 %collective-permute-start.5 = (s16[2,32,1664]{2,1,0:T(8,128)(2,1)S(1)}, s16[2,32,1664]{2,1,0:T(8,128)(2,1)S(1)}, u32[]{:S(2)}, u32[]{:S(2)}) collective-permute-start(s16[2,32,1664]{2,1,0:T(8,128)(2,1)S(1)} %get-tuple-element.26), channel_id=1, source_target_pairs={{0,96},{4,100},{8,104},{12,108},{16,112},{20,116},{24,120},{28,124... | collective-permute-start | bytes 638984 | tf_op jit(solution)/shard_map/ppermute | solution.py:228
  33.3 1.1 collective-permute-done.1.refs_2_
  34.3 5.0 %collective-permute-start.6 = (s16[2,32,1664]{2,1,0:T(8,128)(2,1)S(1)}, s16[2,32,1664]{2,1,0:T(8,128)(2,1)S(1)}, u32[]{:S(2)}, u32[]{:S(2)}) collective-permute-start(s16[2,32,1664]{2,1,0:T(8,128)(2,1)S(1)} %get-tuple-element.27), channel_id=1, source_target_pairs={{0,112},{4,116},{8,120},{12,124},{16,0},{20,4},{24,8},{28,12},{32,... | collective-permute-start | bytes 638984 | tf_op jit(solution)/shard_map/ppermute | solution.py:228
  39.3 9.7 %collective-permute-done.2.refs_3_ = s16[2,32,1664]{2,1,0:T(8,128)(2,1)S(1)} collective-permute-done((s16[2,32,1664]{2,1,0:T(8,128)(2,1)S(1)}, s16[2,32,1664]{2,1,0:T(8,128)(2,1)S(1)}, u32[]{:S(2)}, u32[]{:S(2)}) %collective-permute-start.2) | collective-permute-done | bytes 213024 | tf_op jit(solution)/shard_map/ppermute | solution.py:228
  49.0 5.8 %collective-permute-done.3.refs_4_ = s16[2,32,1664]{2,1,0:T(8,128)(2,1)S(1)} collective-permute-done((s16[2,32,1664]{2,1,0:T(8,128)(2,1)S(1)}, s16[2,32,1664]{2,1,0:T(8,128)(2,1)S(1)}, u32[]{:S(2)}, u32[]{:S(2)}) %collective-permute-start.3) | collective-permute-done | bytes 213024 | tf_op jit(solution)/shard_map/ppermute | solution.py:228
  54.8 0.0 collective-permute-done.4.refs_5_
  54.8 8.2 %collective-permute-done.5.refs_6_ = s16[2,32,1664]{2,1,0:T(8,128)(2,1)S(1)} collective-permute-done((s16[2,32,1664]{2,1,0:T(8,128)(2,1)S(1)}, s16[2,32,1664]{2,1,0:T(8,128)(2,1)S(1)}, u32[]{:S(2)}, u32[]{:S(2)}) %collective-permute-start.5) | collective-permute-done | bytes 213024 | tf_op jit(solution)/shard_map/ppermute | solution.py:228
  63.0 1.6 %collective-permute-done.6.refs_7_ = s16[2,32,1664]{2,1,0:T(8,128)(2,1)S(1)} collective-permute-done((s16[2,32,1664]{2,1,0:T(8,128)(2,1)S(1)}, s16[2,32,1664]{2,1,0:T(8,128)(2,1)S(1)}, u32[]{:S(2)}, u32[]{:S(2)}) %collective-permute-start.6) | collective-permute-done | bytes 213024 | tf_op jit(solution)/shard_map/ppermute | solution.py:228
  64.5 0.0 copy-start.6
  64.5 0.0 copy-start.7
  64.5 0.0 copy-start.4
  64.5 1.3 %shard_map.121 = s16[8,16,896]{2,1,0:T(8,128)(2,1)} custom-call(s16[2,32,1664]{2,1,0:T(8,128)(2,1)S(1)} %get-tuple-element.20.refs_0_, s16[2,32,1664]{2,1,0:T(8,128)(2,1)S(1)} %collective-permute-done.refs_1_, s16[2,32,1664]{2,1,0:T(8,128)(2,1)S(1)} %collective-permute-done.1.refs_2_, s16[2,32,1664]{2,1,0:T(8,128)(2,1)S(1)} %collective-permute-done.2.refs_3_, ...), custom_call_target="tpu_custom_call" | custom-call | flops 3145728 | bytes 1572864 | tf_op jit(solution)/shard_map/pallas_call | solution.py:157
  65.8 0.0 all-to-all-done.refs_0_
  65.8 6.9 %all-to-all-start.2 = ((s16[8,16,896]{2,1,0:T(8,128)(2,1)}), s16[8,16,896]{2,1,0:T(8,128)(2,1)S(1)}, u32[]{:S(2)}, u32[]{:S(2)}) async-start(s16[8,16,896]{2,1,0:T(8,128)(2,1)} %shard_map.121), calls=%async_computation.2 | async-start | bytes 458752 | tf_op jit(solution)/shard_map/all_to_all | solution.py:233
  72.7 1.6 %shard_map.119 = s16[8,16,1408]{2,1,0:T(8,128)(2,1)} custom-call(s16[8,2,32,2688]{3,2,1,0:T(8,128)(2,1)S(1)} %all-to-all-done.refs_0_), custom_call_target="tpu_custom_call" | custom-call | flops 5242880 | bytes 2621440 | tf_op jit(solution)/shard_map/pallas_call | solution.py:157
  74.3 5.8 %all-to-all-done.2.b_ref = s16[8,16,896]{2,1,0:T(8,128)(2,1)S(1)} async-done(((s16[8,16,896]{2,1,0:T(8,128)(2,1)}), s16[8,16,896]{2,1,0:T(8,128)(2,1)S(1)}, u32[]{:S(2)}, u32[]{:S(2)}) %all-to-all-start.2) | async-done | bytes 229408 | tf_op jit(solution)/shard_map/all_to_all | solution.py:233
  80.1 6.0 %all-to-all-start.1 = ((s16[8,16,1408]{2,1,0:T(8,128)(2,1)}), s16[8,16,1408]{2,1,0:T(8,128)(2,1)S(1)}, u32[]{:S(2)}, u32[]{:S(2)}) async-start(s16[8,16,1408]{2,1,0:T(8,128)(2,1)} %shard_map.119), calls=%async_computation.1 | async-start | bytes 720896 | tf_op jit(solution)/shard_map/all_to_all | solution.py:232
  86.1 0.0 copy-done.6
  86.1 0.1 copy.18.m_scale
  86.2 0.0 copy-done.7
  86.2 0.1 copy.19.v_scale
  86.3 11.2 %all-to-all-done.1.a_ref = s16[8,16,1408]{2,1,0:T(8,128)(2,1)S(1)} async-done(((s16[8,16,1408]{2,1,0:T(8,128)(2,1)}), s16[8,16,1408]{2,1,0:T(8,128)(2,1)S(1)}, u32[]{:S(2)}, u32[]{:S(2)}) %all-to-all-start.1) | async-done | bytes 360480 | tf_op jit(solution)/shard_map/all_to_all | solution.py:232
  97.6 0.0 copy-done.3
  97.6 0.0 copy-done.4
  97.6 0.0 copy-done.5
  97.6 1.1 shard_map.122
  98.7 9.5 %all_gather.3 = bf16[64,16,128]{2,1,0:T(8,128)(2,1)} all-gather(bf16[16,16,128]{2,1,0:T(8,128)(2,1)S(1)} %get-tuple-element.33), channel_id=1, replica_groups=mesh['dp'=64,'group'=4] {'group'}, dimensions={0}, use_global_device_ids=true | all-gather | bytes 327680 | tf_op jit(solution)/shard_map/all_gather | solution.py:216
  108.3 4.6 %all-to-all-start.3 = ((bf16[64,16,128]{2,1,0:T(8,128)(2,1)}), bf16[64,16,128]{2,1,0:T(8,128)(2,1)S(1)}, u32[]{:S(2)}, u32[]{:S(2)}) async-start(bf16[64,16,128]{2,1,0:T(8,128)(2,1)} %all_gather.3), calls=%async_computation.3 | async-start | bytes 524288 | tf_op jit(solution)/shard_map/all_to_all | solution.py:217
  112.9 0.7 copy.21
  113.5 0.7 copy.22
  114.2 11.7 %all-to-all-done.3 = bf16[64,16,128]{2,1,0:T(8,128)(2,1)S(1)} async-done(((bf16[64,16,128]{2,1,0:T(8,128)(2,1)}), bf16[64,16,128]{2,1,0:T(8,128)(2,1)S(1)}, u32[]{:S(2)}, u32[]{:S(2)}) %all-to-all-start.3) | async-done | bytes 262176 | tf_op jit(solution)/shard_map/all_to_all | solution.py:217
  125.9 0.2 copy.20
  126.1 0.9 reshape.23
  (2 shorter events, 0.0 us)
Async XLA Ops:
  0.6 1.0 copy-start.1
  6.0 7.6 %copy-start.2 = (bf16[2,256,256]{2,1,0:T(8,128)(2,1)S(1)}, bf16[2,256,256]{2,1,0:T(8,128)(2,1)}, u32[]{:S(2)}) copy-start(bf16[2,256,256]{2,1,0:T(8,128)(2,1)} %acts_ref.3) | copy-start | bytes 786436
  6.0 59.8 %all-to-all-start = ((s16[8,2,32,2688]{3,2,1,0:T(8,128)(2,1)}), s16[8,2,32,2688]{3,2,1,0:T(8,128)(2,1)S(1)}, u32[]{:S(2)}, u32[]{:S(2)}) async-start(s16[8,2,32,2688]{3,2,1,0:T(8,128)(2,1)} %shard_map.118), calls=%async_computation | async-start | bytes 5505024 | tf_op jit(solution)/shard_map/all_to_all | solution.py:229
  13.6 2.2 %copy-start = (bf16[2,256,4096]{2,1,0:T(8,128)(2,1)S(1)}, bf16[2,256,4096]{2,1,0:T(8,128)(2,1)}, u32[]{:S(2)}) copy-start(bf16[2,256,4096]{2,1,0:T(8,128)(2,1)} %grads_ref.3) | copy-start | bytes 12582916
  17.5 13.4 %collective-permute-start = (s16[2,32,1664]{2,1,0:T(8,128)(2,1)S(1)}, s16[2,32,1664]{2,1,0:T(8,128)(2,1)S(1)}, u32[]{:S(2)}, u32[]{:S(2)}) collective-permute-start(s16[2,32,1664]{2,1,0:T(8,128)(2,1)S(1)} %get-tuple-element.21), channel_id=1, source_target_pairs={{0,16},{4,20},{8,24},{12,28},{16,32},{20,36},{24,40},{28,44},{32,4... | collective-permute-start | bytes 638984 | tf_op jit(solution)/shard_map/ppermute | solution.py:228
  19.2 15.2 %collective-permute-start.1 = (s16[2,32,1664]{2,1,0:T(8,128)(2,1)S(1)}, s16[2,32,1664]{2,1,0:T(8,128)(2,1)S(1)}, u32[]{:S(2)}, u32[]{:S(2)}) collective-permute-start(s16[2,32,1664]{2,1,0:T(8,128)(2,1)S(1)} %get-tuple-element.22), channel_id=1, source_target_pairs={{0,32},{4,36},{8,40},{12,44},{16,48},{20,52},{24,56},{28,60},{32,6... | collective-permute-start | bytes 638984 | tf_op jit(solution)/shard_map/ppermute | solution.py:228
  22.2 26.8 %collective-permute-start.2 = (s16[2,32,1664]{2,1,0:T(8,128)(2,1)S(1)}, s16[2,32,1664]{2,1,0:T(8,128)(2,1)S(1)}, u32[]{:S(2)}, u32[]{:S(2)}) collective-permute-start(s16[2,32,1664]{2,1,0:T(8,128)(2,1)S(1)} %get-tuple-element.23), channel_id=1, source_target_pairs={{0,48},{4,52},{8,56},{12,60},{16,64},{20,68},{24,72},{28,76},{32,8... | collective-permute-start | bytes 638984 | tf_op jit(solution)/shard_map/ppermute | solution.py:228
  26.0 28.9 %collective-permute-start.3 = (s16[2,32,1664]{2,1,0:T(8,128)(2,1)S(1)}, s16[2,32,1664]{2,1,0:T(8,128)(2,1)S(1)}, u32[]{:S(2)}, u32[]{:S(2)}) collective-permute-start(s16[2,32,1664]{2,1,0:T(8,128)(2,1)S(1)} %get-tuple-element.24), channel_id=1, source_target_pairs={{0,64},{4,68},{8,72},{12,76},{16,80},{20,84},{24,88},{28,92},{32,9... | collective-permute-start | bytes 638984 | tf_op jit(solution)/shard_map/ppermute | solution.py:228
  26.4 28.4 %collective-permute-start.4 = (s16[2,32,1664]{2,1,0:T(8,128)(2,1)S(1)}, s16[2,32,1664]{2,1,0:T(8,128)(2,1)S(1)}, u32[]{:S(2)}, u32[]{:S(2)}) collective-permute-start(s16[2,32,1664]{2,1,0:T(8,128)(2,1)S(1)} %get-tuple-element.25), channel_id=1, source_target_pairs={{0,80},{4,84},{8,88},{12,92},{16,96},{20,100},{24,104},{28,108},{3... | collective-permute-start | bytes 638984 | tf_op jit(solution)/shard_map/ppermute | solution.py:228
  30.9 32.1 %collective-permute-start.5 = (s16[2,32,1664]{2,1,0:T(8,128)(2,1)S(1)}, s16[2,32,1664]{2,1,0:T(8,128)(2,1)S(1)}, u32[]{:S(2)}, u32[]{:S(2)}) collective-permute-start(s16[2,32,1664]{2,1,0:T(8,128)(2,1)S(1)} %get-tuple-element.26), channel_id=1, source_target_pairs={{0,96},{4,100},{8,104},{12,108},{16,112},{20,116},{24,120},{28,124... | collective-permute-start | bytes 638984 | tf_op jit(solution)/shard_map/ppermute | solution.py:228
  34.3 30.2 %collective-permute-start.6 = (s16[2,32,1664]{2,1,0:T(8,128)(2,1)S(1)}, s16[2,32,1664]{2,1,0:T(8,128)(2,1)S(1)}, u32[]{:S(2)}, u32[]{:S(2)}) collective-permute-start(s16[2,32,1664]{2,1,0:T(8,128)(2,1)S(1)} %get-tuple-element.27), channel_id=1, source_target_pairs={{0,112},{4,116},{8,120},{12,124},{16,0},{20,4},{24,8},{28,12},{32,... | collective-permute-start | bytes 638984 | tf_op jit(solution)/shard_map/ppermute | solution.py:228
  64.5 21.6 %copy-start.6 = (f32[2,4,2]{1,2,0:T(2,128)S(1)}, f32[2,4,2]{1,2,0:T(2,128)}, u32[]{:S(2)}) copy-start(f32[2,4,2]{1,2,0:T(2,128)} %param.11) | copy-start | bytes 196
  64.5 21.7 %copy-start.7 = (f32[2,4,2]{1,2,0:T(2,128)S(1)}, f32[2,4,2]{1,2,0:T(2,128)}, u32[]{:S(2)}) copy-start(f32[2,4,2]{1,2,0:T(2,128)} %param.13) | copy-start | bytes 196
  64.5 33.1 %copy-start.3 = (f32[2,4,4096]{2,1,0:T(4,128)S(1)}, f32[2,4,4096]{2,1,0:T(4,128)}, u32[]{:S(2)}) copy-start(f32[2,4,4096]{2,1,0:T(4,128)} %master.1) | copy-start | bytes 393220
  64.5 33.1 %copy-start.4 = (s32[2,4,4096]{2,1,0:T(4,128)S(1)}, s32[2,4,4096]{2,1,0:T(4,128)}, u32[]{:S(2)}) copy-start(s32[2,4,4096]{2,1,0:T(4,128)} %m_codes.1) | copy-start | bytes 393220
  64.5 33.1 %copy-start.5 = (s32[2,4,4096]{2,1,0:T(4,128)S(1)}, s32[2,4,4096]{2,1,0:T(4,128)}, u32[]{:S(2)}) copy-start(s32[2,4,4096]{2,1,0:T(4,128)} %v_codes.1) | copy-start | bytes 393220
  65.8 14.3 %all-to-all-start.2 = ((s16[8,16,896]{2,1,0:T(8,128)(2,1)}), s16[8,16,896]{2,1,0:T(8,128)(2,1)S(1)}, u32[]{:S(2)}, u32[]{:S(2)}) async-start(s16[8,16,896]{2,1,0:T(8,128)(2,1)} %shard_map.121), calls=%async_computation.2 | async-start | bytes 458752 | tf_op jit(solution)/shard_map/all_to_all | solution.py:233
  80.1 17.4 %all-to-all-start.1 = ((s16[8,16,1408]{2,1,0:T(8,128)(2,1)}), s16[8,16,1408]{2,1,0:T(8,128)(2,1)S(1)}, u32[]{:S(2)}, u32[]{:S(2)}) async-start(s16[8,16,1408]{2,1,0:T(8,128)(2,1)} %shard_map.119), calls=%async_computation.1 | async-start | bytes 720896 | tf_op jit(solution)/shard_map/all_to_all | solution.py:232
  108.3 17.7 %all-to-all-start.3 = ((bf16[64,16,128]{2,1,0:T(8,128)(2,1)}), bf16[64,16,128]{2,1,0:T(8,128)(2,1)S(1)}, u32[]{:S(2)}, u32[]{:S(2)}) async-start(bf16[64,16,128]{2,1,0:T(8,128)(2,1)} %all_gather.3), calls=%async_computation.3 | async-start | bytes 524288 | tf_op jit(solution)/shard_map/all_to_all | solution.py:217

commit v2 on v1

v2 whole, which is shorter than its diff:
```python
import functools

import jax
import jax.numpy as jnp
from jax import lax
from jax.experimental import pallas as pl
from jax.experimental.pallas import tpu as pltpu
from jax.sharding import PartitionSpec as P

BLOCK = 2048
LANES = 128
TOP = 32700.0
STEPS = 16.0

beta_first = 0.9
beta_second = 0.999
first_bias = 1.0 - 0.9**10
second_bias = 1.0 - 0.999**10
learn_rate = 0.001
decay_rate = 0.1
adam_eps = 1e-08
scale_eps = 1e-06

PARAMS = pltpu.CompilerParams(vmem_limit_bytes=56 * 1024 * 1024)

CHUNK = 2048
TILES = CHUNK // LANES

NEAR = [
    [y * 32 + (2 * zz + zl) * 4 + x for y in range(2) for zl in range(2) for x in range(4)]
    for zz in range(4)
]


def far_shift(k):
    return [
        (y * 32 + z * 4 + x, y * 32 + (z + 2 * k) % 8 * 4 + x)
        for y in range(2)
        for z in range(8)
        for x in range(4)
    ]


def swap_groups():
    pairs = [((a, g), (g, a)) for a in range(4) for g in range(a)]
    pairs += [((0, 0), (1, 1)), ((2, 2), (3, 3))]
    return [[(a * 16 + k) * 4 + g for a, g in pair for k in range(16)] for pair in pairs]


def level_of(top):
    return jnp.ceil(STEPS * jnp.log2(jnp.maximum(top, 1e-30)))


def step_of(level):
    return jnp.exp2(level * (1.0 / STEPS)) * (1.0 / TOP)


def unit_of(level):
    return jnp.exp2(level * (-1.0 / STEPS)) * TOP


def to_short(values):
    return values.astype(jnp.int32).astype(jnp.int16)


def coded(values, unit):
    return to_short(jnp.round(values * unit))


def decoded(codes):
    return codes.astype(jnp.int32).astype(jnp.float32)


def lane_max(top, values):
    for j in range(values.shape[1] // LANES):
        top = jnp.maximum(top, jnp.abs(values[:, j * LANES : (j + 1) * LANES]))
    return top


def lane_index(rows):
    return lax.broadcasted_iota(jnp.int32, (rows, LANES), 1)


def partial_kernel(zz_ref, acts_ref, grads_ref, out, grads, sums, codes, notes, sems_in, sems_out):
    chunks = grads.shape[0] // 2
    steps = 2 * chunks

    def load(s):
        source = grads_ref.at[s // chunks, :, pl.ds(s % chunks * CHUNK, CHUNK)]
        return pltpu.make_async_copy(source, grads.at[s], sems_in.at[s])

    def store(s):
        return pltpu.make_async_copy(codes.at[s], out.at[:, pl.ds(s * TILES, TILES)], sems_out.at[s])

    for s in range(steps):
        load(s).start()
    new = lax.broadcasted_iota(jnp.int32, (256, 256), 0)
    row = lax.broadcasted_iota(jnp.int32, (256, 256), 1)
    i, k, x, zl, y = new & 3, (new >> 2) & 3, (new >> 4) & 3, (new >> 6) & 1, new >> 7
    zz = (zz_ref[0] + k) & 3
    pick = jnp.where(row == y * 128 + zz * 32 + zl * 16 + x * 4 + i, 1.0, 0.0).astype(jnp.bfloat16)
    lane = lane_index(256)
    note = jnp.zeros((256, LANES), jnp.int32)
    for s in range(steps):
        if s % chunks == 0:
            lhs = lax.dot_general(
                pick, acts_ref[s // chunks], (((1,), (1,)), ((), ())), preferred_element_type=jnp.float32
            ).astype(jnp.bfloat16)
        load(s).wait()
        top = jnp.zeros((256, LANES), jnp.float32)
        for at in range(0, CHUNK, 512):
            part = jnp.dot(lhs, grads[s, :, at : at + 512], preferred_element_type=jnp.float32)
            sums[s % 2, :, at : at + 512] = part
            top = lane_max(top, part)
        level = level_of(jnp.max(top, axis=1, keepdims=True))
        unit = unit_of(level)
        note = jnp.where(lane == s, level.astype(jnp.int32), note)
        for b in range(16):
            rows = slice(b * 16, (b + 1) * 16)
            for t in range(TILES):
                codes[s, b, t] = coded(sums[s % 2, rows, t * LANES : (t + 1) * LANES], unit[rows])
        store(s).start()
    for b in range(16):
        notes[b, 0] = note[b * 16 : (b + 1) * 16].astype(jnp.int16)
    final = pltpu.make_async_copy(notes, out.at[:, pl.ds(steps * TILES, 1)], sems_out.at[steps])
    final.start()
    for s in range(steps):
        store(s).wait()
    final.wait()


def partial_codes(zz, acts, out_grads):
    steps = 2 * out_grads.shape[2] // CHUNK
    return pl.pallas_call(
        partial_kernel,
        in_specs=[
            pl.BlockSpec(memory_space=pltpu.SMEM),
            pl.BlockSpec(memory_space=pltpu.VMEM),
            pl.BlockSpec(memory_space=pl.ANY),
        ],
        out_shape=jax.ShapeDtypeStruct((16, steps * TILES + 1, 16, LANES), jnp.int16),
        out_specs=pl.BlockSpec(memory_space=pl.ANY),
        scratch_shapes=[
            pltpu.VMEM((steps, 256, CHUNK), jnp.bfloat16),
            pltpu.VMEM((2, 256, CHUNK), jnp.float32),
            pltpu.VMEM((steps, 16, TILES, 16, LANES), jnp.int16),
            pltpu.VMEM((16, 1, 16, LANES), jnp.int16),
            pltpu.SemaphoreType.DMA((steps,)),
            pltpu.SemaphoreType.DMA((steps + 1,)),
        ],
        compiler_params=PARAMS,
        cost_estimate=pl.CostEstimate(
            flops=4 * 256 * 256 * 4096, bytes_accessed=8 << 20, transcendentals=0
        ),
    )(zz, acts, out_grads)


def regroup_kernel(received, *rest):
    *outs, codes, notes, sums, sems = rest
    steps = codes.shape[0]
    chunks = steps // 2
    final = pltpu.make_async_copy(received.at[:, pl.ds(steps * TILES, 1)], notes, sems.at[steps])
    final.start()

    def load(s):
        return pltpu.make_async_copy(received.at[:, pl.ds(s * TILES, TILES)], codes.at[s], sems.at[s])

    for s in range(steps):
        load(s).start()
    final.wait()
    levels = [decoded(notes[n, 0]) for n in range(16)]
    for s in range(steps):
        scales = [step_of(level[:, s : s + 1]) for level in levels]
        load(s).wait()
        for t in range(TILES):
            total = decoded(codes[s, 0, t]) * scales[0]
            for n in range(1, 16):
                total = total + decoded(codes[s, n, t]) * scales[n]
            at = s % chunks * CHUNK + t * LANES
            sums[s // chunks, :, at : at + LANES] = total
    upper = lax.broadcasted_iota(jnp.int32, (8, 1), 0) < 4
    for pair in range(2):
        tile = slice(pair * 8, pair * 8 + 8)
        z = [[sums[e, tile, h * BLOCK : (h + 1) * BLOCK] for h in range(2)] for e in range(2)]
        even = [jnp.where(upper, z[0][h], pltpu.roll(z[1][h], 4, 0)) for h in range(2)]
        odd = [jnp.where(upper, pltpu.roll(z[0][h], 4, 0), z[1][h]) for h in range(2)]
        for out, halves in ((outs[pair * 2], even), (outs[pair * 2 + 1], odd)):
            values = jnp.concatenate(halves, axis=0)
            top = lane_max(jnp.zeros((16, LANES), jnp.float32), values)
            level = level_of(jnp.max(top, axis=1, keepdims=True))
            unit = unit_of(level)
            for t in range(16):
                out[t] = coded(values[:, t * LANES : (t + 1) * LANES], unit)
            out[16] = to_short(jnp.broadcast_to(level, (16, LANES)))


def regroup(received):
    steps = received.shape[1] // TILES
    return pl.pallas_call(
        regroup_kernel,
        in_specs=[pl.BlockSpec(memory_space=pl.ANY)],
        out_shape=[jax.ShapeDtypeStruct((17, 16, LANES), jnp.int16)] * 4,
        scratch_shapes=[
            pltpu.VMEM((steps, 16, TILES, 16, LANES), jnp.int16),
            pltpu.VMEM((16, 1, 16, LANES), jnp.int16),
            pltpu.VMEM((2, 16, 2 * BLOCK), jnp.float32),
            pltpu.SemaphoreType.DMA((steps + 1,)),
        ],
        compiler_params=PARAMS,
        cost_estimate=pl.CostEstimate(flops=4 << 20, bytes_accessed=4 << 20, transcendentals=0),
    )(received)


def adam_kernel(c0, c1, c2, c3, master, m_codes, m_scale, v_codes, v_scale,
                new_master, m_state, m_absmax, v_state, v_absmax, rollout, grad):
    codes = (c0, c1, c2, c3)
    steps = [step_of(decoded(c[16])[:, :1]) for c in codes]
    for t in range(16):
        total = decoded(c0[t]) * steps[0]
        for s in range(1, 4):
            total = total + decoded(codes[s][t]) * steps[s]
        for h in range(2):
            grad[:, h * BLOCK + t * LANES : h * BLOCK + (t + 1) * LANES] = total[h * 8 : (h + 1) * 8]
    for e in range(2):
        for b in range(2):
            cols = slice(b * BLOCK, (b + 1) * BLOCK)
            g = grad[e * 4 : (e + 1) * 4, cols]
            m_old = m_codes[e, :, cols].astype(jnp.float32) * (m_scale[e, :, b : b + 1] / 127.0)
            v_old = v_codes[e, :, cols].astype(jnp.float32) * (v_scale[e, :, b : b + 1] / 255.0)
            m_new = beta_first * m_old + (1.0 - beta_first) * g
            v_new = beta_second * v_old + (1.0 - beta_second) * g * g
            update = m_new / first_bias / (jnp.sqrt(v_new / second_bias) + adam_eps)
            old = master[e, :, cols]
            new = old - learn_rate * (update + decay_rate * old)
            new_master[e, :, cols] = new
            m_top = jnp.max(jnp.abs(m_new), axis=1, keepdims=True)
            v_top = jnp.max(v_new, axis=1, keepdims=True)
            m_absmax[e, :, b : b + 1] = m_top
            v_absmax[e, :, b : b + 1] = v_top
            m_state[e, :, cols] = m_new / (m_top + scale_eps)
            v_state[e, :, cols] = v_new / (v_top + scale_eps)
            grad[e * 4 : (e + 1) * 4, cols] = new
    for k in range(16):
        for h in range(2):
            at = k * 256 + h * LANES
            tile = grad[:, at : at + LANES].astype(jnp.bfloat16)
            for copy in range(2):
                rollout[copy * 16 + k, h * 8 : (h + 1) * 8, :] = tile


def adam(codes, master, m_codes, m_scale, v_codes, v_scale):
    big = jax.ShapeDtypeStruct((2, 4, 4096), jnp.float32)
    small = jax.ShapeDtypeStruct((2, 4, 2), jnp.float32)
    return pl.pallas_call(
        adam_kernel,
        out_shape=[big, big, small, big, small, jax.ShapeDtypeStruct((32, 16, LANES), jnp.bfloat16)],
        scratch_shapes=[pltpu.VMEM((8, 4096), jnp.float32)],
        compiler_params=PARAMS,
        cost_estimate=pl.CostEstimate(flops=2 * 4 * 4096 * 40, bytes_accessed=2 << 20, transcendentals=0),
    )(*codes, master, m_codes, m_scale, v_codes, v_scale)


def push_weights(weights):
    plane, group = lax.axis_index("dp") // 16, lax.axis_index("group")
    swapped = lax.all_to_all(
        weights, ("dp", "group"), 0, 0, axis_index_groups=swap_groups(), tiled=True
    )
    upper = jnp.where(plane == group, plane % 2 == 1, plane > group)
    slab = jnp.where(upper, swapped[16:], swapped[:16])
    gathered = lax.all_gather(slab, "group", axis=0, tiled=True)
    spread = gathered.reshape(64, 2, 2, 4, LANES)
    return jnp.transpose(spread, (2, 0, 3, 1, 4)).reshape(2, 256, 256)


def on_device(acts, out_grads, master, m_codes, m_scale, v_codes, v_scale):
    zz = ((lax.axis_index("dp") >> 3) & 3).reshape(1).astype(jnp.int32)
    codes = partial_codes(zz, acts, out_grads)
    codes = lax.all_to_all(codes, "dp", 0, 0, axis_index_groups=NEAR, tiled=True)
    codes = regroup(codes)
    codes = [codes[0]] + [lax.ppermute(codes[k], "dp", far_shift(k)) for k in range(1, 4)]
    *state, weights = adam(codes, master, m_codes, m_scale, v_codes, v_scale)
    return (*state, push_weights(weights))


def solution(mesh):
    split = P(None, "dp", "group")
    return jax.shard_map(
        on_device,
        mesh=mesh,
        in_specs=(P(None, "dp", None),) + (split,) * 6,
        out_specs=(split,) * 5 + (P(None, None, "dp"),),
        check_vma=False,
    )
```

time: 128 us -> 112 us (0.88)
  blocking collectives: 9.54 us -> 66.6 us
  waiting for transfers between devices: 55.1 us -> 6.05 us
  starting transfers between devices: 45.8 us -> 20.2 us
  Pallas kernels: 10.1 us -> 12 us
    all_to_all x0 -> x1, blocking collectives: none -> 60.6 us  [on_device(): lax.all_to_all(codes, 'dp', 0, 0, axis_index_groups=NEAR, tiled=True)]
    all_to_all x4 -> x1, waiting for transfers between devices: 28.8 us -> 3.65 us  [push_weights(): lax.all_to_all(weights, ('dp', 'group'), 0, 0, axis_index_groups=swap_gro...]
    ppermute x7 -> x3, waiting for transfers between devices: 26.3 us -> 2.4 us  [on_device(): lax.ppermute(codes[k], 'dp', far_shift(k))]
    all_to_all x4 -> x1, starting transfers between devices: 25.1 us -> 10.5 us  [push_weights(): lax.all_to_all(weights, ('dp', 'group'), 0, 0, axis_index_groups=swap_gro...]
    ppermute x7 -> x3, starting transfers between devices: 20.8 us -> 9.66 us  [on_device(): lax.ppermute(codes[k], 'dp', far_shift(k))]
    all_gather x1, blocking collectives: 9.54 us -> 6.04 us  [push_weights(): gathered = lax.all_gather(slab, 'group', axis=0, tiled=True)]
    pallas_call x4 -> x2, Pallas kernels: 8.98 us -> 9.66 us  [the longest x1 6.28 us: partial_codes(): pl.pallas_call(partial_kernel, in_specs=[pl.BlockSpec(memory_space=pltpu....]
    unnamed x20 -> x14, local copies, waits for them, and re-layouts: 4.69 us -> 4.68 us
  transfers between devices with their start and end apart: 11 -> 4, of which waited for: 8 -> 3; matrix products, arithmetic and copies ran while one was open for 1% -> 4% of each run, Pallas kernels for 4% -> 0%
where the time goes in v2:
time: 112 us; the launch traced here: 111 us
  blocking collectives  66.6 us (59%)
  starting transfers between devices  20.2 us (18%)
  Pallas kernels  12 us (11%)
  waiting for transfers between devices  6.05 us (5%)
  local copies, waits for them, and re-layouts  5.76 us (5%)
    all_to_all x1, blocking collectives, on_device(): lax.all_to_all(codes, 'dp', 0, 0, axis_index_groups=NEAR, tiled=True)  60.6 us
    all_to_all x1, starting transfers between devices, push_weights(): lax.all_to_all(weights, ('dp', 'group'), 0, 0, axis_index_groups=swap_gro...  10.5 us
    ppermute x3, starting transfers between devices, on_device(): lax.ppermute(codes[k], 'dp', far_shift(k))  9.66 us
    pallas_call x1, Pallas kernels, partial_codes(): pl.pallas_call(partial_kernel, in_specs=[pl.BlockSpec(memory_space=pltpu....  6.28 us
    all_gather x1, blocking collectives, push_weights(): gathered = lax.all_gather(slab, 'group', axis=0, tiled=True)  6.04 us
    unnamed x14, local copies, waits for them, and re-layouts  4.68 us
    all_to_all x1, waiting for transfers between devices, push_weights(): lax.all_to_all(weights, ('dp', 'group'), 0, 0, axis_index_groups=swap_gro...  3.65 us
    pallas_call x1, Pallas kernels, regroup(): pl.pallas_call(regroup_kernel, in_specs=[pl.BlockSpec(memory_space=pl.ANY...  3.39 us
  transfers between devices with their start and end apart: 4, of which 3 were waited for; matrix products, arithmetic and copies ran while one was open for 4% of the time, Pallas kernels for 0%

profile of v2, /device:TPU:1, one launch (start us, length us, event | category | flops | bytes accessed | tf_op | source)
XLA Modules:
  0.0 111.3 jit_solution(4936904004489854637)
XLA Ops:
  0.6 6.3 %shard_map.118 = s16[16,65,16,128]{3,2,1,0:T(8,128)(2,1)} custom-call(s32[1]{0:T(128)} %bitcast.zz_ref, bf16[2,256,256]{2,1,0:T(8,128)(2,1)} %acts_ref.1, bf16[2,256,4096]{2,1,0:T(8,128)(2,1)} %grads_ref.1), custom_call_target="tpu_custom_call" | custom-call | flops 1073741824 | bytes 8388608 | tf_op jit(solution)/shard_map/pallas_call | solution.py:134
  6.9 60.6 %all_to_all.10.received = s16[16,65,16,128]{3,2,1,0:T(8,128)(2,1)} all-to-all(s16[16,65,16,128]{3,2,1,0:T(8,128)(2,1)} %shard_map.118), channel_id=1, replica_groups={{0,4,8,12,16,20,24,28,128,132,136,140,144,148,152,156},{32,36,40,44,48,..., dimensions={0} | all-to-all | bytes 8519680 | tf_op jit(solution)/shard_map/all_to_all | solution.py:278
  67.5 0.0 copy-start.3
  67.5 0.0 copy-start.4
  67.5 3.4 %shard_map.119 = (s16[17,16,128]{2,1,0:T(8,128)(2,1)}, s16[17,16,128]{2,1,0:T(8,128)(2,1)}, s16[17,16,128]{2,1,0:T(8,128)(2,1)}, s16[17,16,128]{2,1,0:T(8,128)(2,1)}) custom-call(s16[16,65,16,128]{3,2,1,0:T(8,128)(2,1)} %all_to_all.10.received), custom_call_target="tpu_custom_call" | custom-call | flops 4194304 | bytes 4194304 | tf_op jit(solution)/shard_map/pallas_call | solution.py:199
  70.9 3.1 %collective-permute-start = (s16[17,16,128]{2,1,0:T(8,128)(2,1)}, s16[17,16,128]{2,1,0:T(8,128)(2,1)S(1)}, u32[]{:S(2)}, u32[]{:S(2)}) collective-permute-start(s16[17,16,128]{2,1,0:T(8,128)(2,1)} %get-tuple-element.17), channel_id=1, source_target_pairs={{0,32},{4,36},{8,40},{12,44},{16,48},{20,52},{24,56},{28,60},{32,6... | collective-permute-start | bytes 208904 | tf_op jit(solution)/shard_map/ppermute | solution.py:280
  74.0 4.2 %collective-permute-start.1 = (s16[17,16,128]{2,1,0:T(8,128)(2,1)}, s16[17,16,128]{2,1,0:T(8,128)(2,1)S(1)}, u32[]{:S(2)}, u32[]{:S(2)}) collective-permute-start(s16[17,16,128]{2,1,0:T(8,128)(2,1)} %get-tuple-element.18), channel_id=1, source_target_pairs={{0,64},{4,68},{8,72},{12,76},{16,80},{20,84},{24,88},{28,92},{32,9... | collective-permute-start | bytes 208904 | tf_op jit(solution)/shard_map/ppermute | solution.py:280
  78.2 2.4 %collective-permute-start.2 = (s16[17,16,128]{2,1,0:T(8,128)(2,1)}, s16[17,16,128]{2,1,0:T(8,128)(2,1)S(1)}, u32[]{:S(2)}, u32[]{:S(2)}) collective-permute-start(s16[17,16,128]{2,1,0:T(8,128)(2,1)} %get-tuple-element.19), channel_id=1, source_target_pairs={{0,96},{4,100},{8,104},{12,108},{16,112},{20,116},{24,120},{28,124... | collective-permute-start | bytes 208904 | tf_op jit(solution)/shard_map/ppermute | solution.py:280
  80.6 0.0 copy-done.3
  80.6 0.7 copy.18.m_scale
  81.3 0.0 copy-done.4
  81.3 0.7 copy.19.v_scale
  81.9 0.0 collective-permute-done.c1
  81.9 0.0 copy-start
  82.0 0.1 collective-permute-done.1.c2
  82.1 0.0 copy-start.1
  82.1 2.3 %collective-permute-done.2.c3 = s16[17,16,128]{2,1,0:T(8,128)(2,1)S(1)} collective-permute-done((s16[17,16,128]{2,1,0:T(8,128)(2,1)}, s16[17,16,128]{2,1,0:T(8,128)(2,1)S(1)}, u32[]{:S(2)}, u32[]{:S(2)}) %collective-permute-start.2) | collective-permute-done | bytes 69664 | tf_op jit(solution)/shard_map/ppermute | solution.py:280
  84.4 0.0 copy-start.2
  84.4 0.0 copy-done
  84.4 0.0 copy-done.1
  84.4 0.6 copy-done.2
  85.0 2.3 %shard_map.120 = (f32[2,4,4096]{2,1,0:T(4,128)}, f32[2,4,4096]{2,1,0:T(4,128)}, f32[2,4,2]{2,1,0:T(4,128)}, f32[2,4,4096]{2,1,0:T(4,128)}, f32[2,4,2]{2,1,0:T(4,128)}, /*index=5*/bf16[32,16,128]{2,1,0:T(8,128)(2,1)}) custom-call(s16[17,16,128]{2,1,0:T(8,128)(2,1)} %get-tuple-element.16.c0, s16[17,16,128]{2,1,0:T(8,128)(2,1)} %copy-done, ...), custom_call_target="tpu_custom_call" | custom-call | flops 1310720 | bytes 2097152 | tf_op jit(solution)/shard_map/pallas_call | solution.py:254
  87.3 10.5 %all-to-all-start.1 = ((bf16[32,16,128]{2,1,0:T(8,128)(2,1)}), bf16[32,16,128]{2,1,0:T(8,128)(2,1)S(1)}, u32[]{:S(2)}, u32[]{:S(2)}) async-start(bf16[32,16,128]{2,1,0:T(8,128)(2,1)} %get-tuple-element.25), calls=%async_computation.1 | async-start | bytes 262144 | tf_op jit(solution)/shard_map/all_to_all | solution.py:265
  97.8 1.3 %copy.21 = f32[2,4,2]{1,2,0:T(2,128)} copy(f32[2,4,2]{2,1,0:T(4,128)} %get-tuple-element.34) | data formatting | bytes 128
  99.2 1.3 %copy.22 = f32[2,4,2]{1,2,0:T(2,128)} copy(f32[2,4,2]{2,1,0:T(4,128)} %get-tuple-element.36) | data formatting | bytes 128
  100.5 3.6 %all-to-all-done.1 = bf16[32,16,128]{2,1,0:T(8,128)(2,1)S(1)} async-done(((bf16[32,16,128]{2,1,0:T(8,128)(2,1)}), bf16[32,16,128]{2,1,0:T(8,128)(2,1)S(1)}, u32[]{:S(2)}, u32[]{:S(2)}) %all-to-all-start.1) | async-done | bytes 131104 | tf_op jit(solution)/shard_map/all_to_all | solution.py:265
  104.2 6.0 %all_gather.3 = bf16[64,16,128]{2,1,0:T(8,128)(2,1)S(1)} all-gather(bf16[16,16,128]{2,1,0:T(8,128)(2,1)S(1)} %slice_select_fusion), channel_id=1, replica_groups=mesh['dp'=64,'group'=4] {'group'}, dimensions={0}, use_global_device_ids=true | all-gather | bytes 327680 | tf_op jit(solution)/shard_map/all_gather | solution.py:270
  110.2 0.2 copy.20
  110.4 0.9 reshape.23
  (1 shorter events, 0.0 us)
Async XLA Ops:
  67.5 13.1 %copy-start.3 = (f32[2,4,2]{1,2,0:T(2,128)S(1)}, f32[2,4,2]{1,2,0:T(2,128)}, u32[]{:S(2)}) copy-start(f32[2,4,2]{1,2,0:T(2,128)} %param.11) | copy-start | bytes 196
  67.5 13.7 %copy-start.4 = (f32[2,4,2]{1,2,0:T(2,128)S(1)}, f32[2,4,2]{1,2,0:T(2,128)}, u32[]{:S(2)}) copy-start(f32[2,4,2]{1,2,0:T(2,128)} %param.13) | copy-start | bytes 196
  70.9 11.0 %collective-permute-start = (s16[17,16,128]{2,1,0:T(8,128)(2,1)}, s16[17,16,128]{2,1,0:T(8,128)(2,1)S(1)}, u32[]{:S(2)}, u32[]{:S(2)}) collective-permute-start(s16[17,16,128]{2,1,0:T(8,128)(2,1)} %get-tuple-element.17), channel_id=1, source_target_pairs={{0,32},{4,36},{8,40},{12,44},{16,48},{20,52},{24,56},{28,60},{32,6... | collective-permute-start | bytes 208904 | tf_op jit(solution)/shard_map/ppermute | solution.py:280
  74.0 8.1 %collective-permute-start.1 = (s16[17,16,128]{2,1,0:T(8,128)(2,1)}, s16[17,16,128]{2,1,0:T(8,128)(2,1)S(1)}, u32[]{:S(2)}, u32[]{:S(2)}) collective-permute-start(s16[17,16,128]{2,1,0:T(8,128)(2,1)} %get-tuple-element.18), channel_id=1, source_target_pairs={{0,64},{4,68},{8,72},{12,76},{16,80},{20,84},{24,88},{28,92},{32,9... | collective-permute-start | bytes 208904 | tf_op jit(solution)/shard_map/ppermute | solution.py:280
  78.2 6.1 %collective-permute-start.2 = (s16[17,16,128]{2,1,0:T(8,128)(2,1)}, s16[17,16,128]{2,1,0:T(8,128)(2,1)S(1)}, u32[]{:S(2)}, u32[]{:S(2)}) collective-permute-start(s16[17,16,128]{2,1,0:T(8,128)(2,1)} %get-tuple-element.19), channel_id=1, source_target_pairs={{0,96},{4,100},{8,104},{12,108},{16,112},{20,116},{24,120},{28,124... | collective-permute-start | bytes 208904 | tf_op jit(solution)/shard_map/ppermute | solution.py:280
  81.9 2.4 %copy-start = (s16[17,16,128]{2,1,0:T(8,128)(2,1)}, s16[17,16,128]{2,1,0:T(8,128)(2,1)S(1)}, u32[]{:S(2)}) copy-start(s16[17,16,128]{2,1,0:T(8,128)(2,1)S(1)} %collective-permute-done.c1) | copy-start | bytes 208900
  82.1 2.3 %copy-start.1 = (s16[17,16,128]{2,1,0:T(8,128)(2,1)}, s16[17,16,128]{2,1,0:T(8,128)(2,1)S(1)}, u32[]{:S(2)}) copy-start(s16[17,16,128]{2,1,0:T(8,128)(2,1)S(1)} %collective-permute-done.1.c2) | copy-start | bytes 208900
  84.4 0.6 copy-start.2
  87.3 16.9 %all-to-all-start.1 = ((bf16[32,16,128]{2,1,0:T(8,128)(2,1)}), bf16[32,16,128]{2,1,0:T(8,128)(2,1)S(1)}, u32[]{:S(2)}, u32[]{:S(2)}) async-start(bf16[32,16,128]{2,1,0:T(8,128)(2,1)} %get-tuple-element.25), calls=%async_computation.1 | async-start | bytes 262144 | tf_op jit(solution)/shard_map/all_to_all | solution.py:265

commit v3 on v2

v3 whole, which is shorter than its diff:
```python
import functools

import jax
import jax.numpy as jnp
from jax import lax
from jax.experimental import pallas as pl
from jax.experimental.pallas import tpu as pltpu
from jax.sharding import PartitionSpec as P

BLOCK = 2048
LANES = 128
TOP = 32700.0
STEPS = 16.0

beta_first = 0.9
beta_second = 0.999
first_bias = 1.0 - 0.9**10
second_bias = 1.0 - 0.999**10
learn_rate = 0.001
decay_rate = 0.1
adam_eps = 1e-08
scale_eps = 1e-06

CHUNK = 1024
WIDTH = 4096
TILES = WIDTH // LANES

PARAMS = pltpu.CompilerParams(vmem_limit_bytes=20 * 1024 * 1024)
FIRST_PARAMS = pltpu.CompilerParams(vmem_limit_bytes=56 * 1024 * 1024)


def moved(step):
    def index(y, z, x):
        return y % 2 * 32 + z % 8 * 4 + x % 4

    return [(index(y, z, x), index(*step(y, z, x))) for y in range(2) for z in range(8) for x in range(4)]


UP = moved(lambda y, z, x: (y, z, x + 1))
DOWN = moved(lambda y, z, x: (y, z, x - 1))
PAIR = [moved(lambda y, z, x, e=e: (y, z + 1 if z % 2 == e else z - 1, x)) for e in range(2)]
ACROSS = moved(lambda y, z, x: (y + 1, z, x))


def z_shift(k):
    return moved(lambda y, z, x: (y, z + 2 * k, x))


def swap_groups():
    pairs = [((a, g), (g, a)) for a in range(4) for g in range(a)]
    pairs += [((0, 0), (1, 1)), ((2, 2), (3, 3))]
    return [[(a * 16 + k) * 4 + g for a, g in pair for k in range(16)] for pair in pairs]


def level_of(top):
    return jnp.ceil(STEPS * jnp.log2(jnp.maximum(top, 1e-30)))


def step_of(level):
    return jnp.exp2(level * (1.0 / STEPS)) * (1.0 / TOP)


def unit_of(level):
    return jnp.exp2(level * (-1.0 / STEPS)) * TOP


def to_short(values):
    return values.astype(jnp.int32).astype(jnp.int16)


def coded(values, unit):
    return to_short(jnp.round(values * unit))


def decoded(codes):
    return codes.astype(jnp.int32).astype(jnp.float32)


def lane_max(top, values):
    for j in range(values.shape[1] // LANES):
        top = jnp.maximum(top, jnp.abs(values[:, j * LANES : (j + 1) * LANES]))
    return top


def lane_index(rows):
    return lax.broadcasted_iota(jnp.int32, (rows, LANES), 1)


def picked(acts, expert, place, steps):
    y, z, x = place
    new = lax.broadcasted_iota(jnp.int32, (64, 256), 0)
    old = lax.broadcasted_iota(jnp.int32, (64, 256), 1)
    i, k, here_y, here_z = new & 3, (new >> 2) & 3, (new >> 4) & 1, new >> 5
    neighbour = jnp.where((z & 1) == expert, z + 1, z + 7)
    row_y = jnp.where(here_y == 1, y, 1 - y)
    row_z = (jnp.where(here_z == 1, z, neighbour) + 2 * k) & 7
    row = row_y * 128 + row_z * 16 + ((x + steps) & 3) * 4 + i
    pick = jnp.where(old == row, 1.0, 0.0).astype(jnp.bfloat16)
    return lax.dot_general(
        pick, acts, (((1,), (1,)), ((), ())), preferred_element_type=jnp.float32
    ).astype(jnp.bfloat16)


def add_up(steps, me, acts_ref, grads_ref, received, acts, grads, sums, sems):
    pieces = [(e, at) for e in range(2) for at in range(0, WIDTH, CHUNK)]

    def load(n):
        e, at = pieces[n]
        source = grads_ref.at[e, :, pl.ds(at, CHUNK)]
        return pltpu.make_async_copy(source, grads.at[e, :, pl.ds(at, CHUNK)], sems.at[n])

    load_acts = pltpu.make_async_copy(acts_ref, acts, sems.at[len(pieces)])
    load_acts.start()
    for n in range(len(pieces)):
        load(n).start()
    load_acts.wait()
    place = me >> 5, (me >> 2) & 7, me & 3
    lhs = [picked(acts[e], e, place, steps[e]) for e in range(2)]
    scales = []
    for e in range(2):
        notes = [decoded(r[4 * TILES]) for r in received[e]]
        scales.append([[step_of(note[:, g : g + 1]) for note in notes] for g in range(4)])
    tops = [[jnp.zeros((16, LANES), jnp.float32)] * 4 for _ in range(2)]
    for n, (e, first) in enumerate(pieces):
        load(n).wait()
        for at in range(first, first + CHUNK, 512):
            part = jnp.dot(lhs[e], grads[e, :, at : at + 512], preferred_element_type=jnp.float32)
            for g in range(4):
                for j in range(0, 512, LANES):
                    total = part[g * 16 : (g + 1) * 16, j : j + LANES]
                    for r, scale in zip(received[e], scales[e][g]):
                        total = total + decoded(r[g * TILES + (at + j) // LANES]) * scale
                    sums[e, g * 16 : (g + 1) * 16, at + j : at + j + LANES] = total
                    tops[e][g] = jnp.maximum(tops[e][g], jnp.abs(total))
    return tops


def codes_kernel(steps, me_ref, acts_ref, grads_ref, *rest):
    received, (out0, out1, acts, grads, sums, sems) = rest[:-6], rest[-6:]
    tops = add_up(steps, me_ref[0], acts_ref, grads_ref, [received[:1], received[1:]], acts, grads, sums, sems)
    for e, out in enumerate((out0, out1)):
        write_groups(out, [(sums.at[e], g, tops[e][g]) for g in range(4)])


def write_groups(out, groups):
    lane = lane_index(16)
    note = jnp.zeros((16, LANES), jnp.int32)
    for n, (sums, g, top) in enumerate(groups):
        level = level_of(jnp.max(top, axis=1, keepdims=True))
        unit = unit_of(level)
        note = jnp.where(lane == n, level.astype(jnp.int32), note)
        for t in range(TILES):
            out[n * TILES + t] = coded(sums[g * 16 : (g + 1) * 16, t * LANES : (t + 1) * LANES], unit)
    out[len(groups) * TILES] = note.astype(jnp.int16)


SPECS = [
    pl.BlockSpec(memory_space=pltpu.SMEM),
    pl.BlockSpec(memory_space=pl.ANY),
    pl.BlockSpec(memory_space=pl.ANY),
]


SCRATCH = [
    pltpu.VMEM((2, 256, 256), jnp.bfloat16),
    pltpu.VMEM((2, 256, WIDTH), jnp.bfloat16),
    pltpu.VMEM((2, 64, WIDTH), jnp.float32),
    pltpu.SemaphoreType.DMA((2 * WIDTH // CHUNK + 1,)),
]


COST = pl.CostEstimate(flops=4 * 64 * 256 * WIDTH, bytes_accessed=3 << 20, transcendentals=0)


def codes_for(steps, me, acts, out_grads, *received):
    return pl.pallas_call(
        functools.partial(codes_kernel, steps),
        in_specs=SPECS + [pl.BlockSpec(memory_space=pltpu.VMEM)] * len(received),
        out_shape=[jax.ShapeDtypeStruct((4 * TILES + 1, 16, LANES), jnp.int16)] * 2,
        scratch_shapes=SCRATCH,
        compiler_params=PARAMS if received else FIRST_PARAMS,
        cost_estimate=COST,
    )(me, acts, out_grads, *received)


def own_kernel(me_ref, acts_ref, grads_ref, a0, b0, a1, b1, out0, out1, kept, acts, grads, sums, sems):
    tops = add_up((0, 0), me_ref[0], acts_ref, grads_ref, [(a0, b0), (a1, b1)], acts, grads, sums, sems)
    for e, out in enumerate((out0, out1)):
        write_groups(out, [(sums.at[e], g, tops[e][g]) for g in range(2)])
        kept[e] = sums[e, 32:]


def own_codes(me, acts, out_grads, *received):
    codes = jax.ShapeDtypeStruct((2 * TILES + 1, 16, LANES), jnp.int16)
    return pl.pallas_call(
        own_kernel,
        in_specs=SPECS + [pl.BlockSpec(memory_space=pltpu.VMEM)] * 4,
        out_shape=[codes, codes, jax.ShapeDtypeStruct((2, 32, WIDTH), jnp.float32)],
        scratch_shapes=SCRATCH,
        compiler_params=PARAMS,
        cost_estimate=COST,
    )(me, acts, out_grads, *received)


def pair_kernel(kept, got0, got1, out, rest, sums):
    tops = []
    for e, got in enumerate((got0, got1)):
        note = decoded(got[2 * TILES])
        for g in range(2):
            scale = step_of(note[:, g : g + 1])
            top = jnp.zeros((16, LANES), jnp.float32)
            for t in range(TILES):
                cols = slice(t * LANES, (t + 1) * LANES)
                total = kept[e, g * 16 : (g + 1) * 16, cols] + decoded(got[g * TILES + t]) * scale
                if g == 0:
                    sums[e, :, cols] = total
                    top = jnp.maximum(top, jnp.abs(total))
                else:
                    rest[e, :, cols] = total
            if g == 0:
                tops.append(top)
    write_groups(out, [(sums.at[e], 0, tops[e]) for e in range(2)])


def pair_codes(kept, got0, got1):
    return pl.pallas_call(
        pair_kernel,
        out_shape=[
            jax.ShapeDtypeStruct((2 * TILES + 1, 16, LANES), jnp.int16),
            jax.ShapeDtypeStruct((2, 16, WIDTH), jnp.float32),
        ],
        scratch_shapes=[pltpu.VMEM((2, 16, WIDTH), jnp.float32)],
        compiler_params=PARAMS,
        cost_estimate=COST,
    )(kept, got0, got1)


def across_kernel(rest, got, *refs):
    *outs, sums = refs
    note = decoded(got[2 * TILES])
    for e in range(2):
        scale = step_of(note[:, e : e + 1])
        for t in range(TILES):
            cols = slice(t * LANES, (t + 1) * LANES)
            sums[e, :, cols] = rest[e, :, cols] + decoded(got[e * TILES + t]) * scale
    upper = lax.broadcasted_iota(jnp.int32, (8, 1), 0) < 4
    half = WIDTH // 2
    for pair in range(2):
        tile = slice(pair * 8, pair * 8 + 8)
        z = [[sums[e, tile, h * half : (h + 1) * half] for h in range(2)] for e in range(2)]
        even = [jnp.where(upper, z[0][h], pltpu.roll(z[1][h], 4, 0)) for h in range(2)]
        odd = [jnp.where(upper, pltpu.roll(z[0][h], 4, 0), z[1][h]) for h in range(2)]
        for out, halves in ((outs[pair * 2], even), (outs[pair * 2 + 1], odd)):
            values = jnp.concatenate(halves, axis=0)
            top = lane_max(jnp.zeros((16, LANES), jnp.float32), values)
            level = level_of(jnp.max(top, axis=1, keepdims=True))
            unit = unit_of(level)
            for t in range(TILES // 2):
                out[t] = coded(values[:, t * LANES : (t + 1) * LANES], unit)
            out[TILES // 2] = to_short(jnp.broadcast_to(level, (16, LANES)))


def across_codes(rest, got):
    return pl.pallas_call(
        across_kernel,
        out_shape=[jax.ShapeDtypeStruct((TILES // 2 + 1, 16, LANES), jnp.int16)] * 4,
        scratch_shapes=[pltpu.VMEM((2, 16, WIDTH), jnp.float32)],
        compiler_params=PARAMS,
        cost_estimate=COST,
    )(rest, got)


def adam_kernel(c0, c1, c2, c3, master, m_codes, m_scale, v_codes, v_scale,
                new_master, m_state, m_absmax, v_state, v_absmax, rollout, grad):
    codes = (c0, c1, c2, c3)
    tiles = TILES // 2
    steps = [step_of(decoded(c[tiles])[:, :1]) for c in codes]
    for t in range(tiles):
        total = decoded(c0[t]) * steps[0]
        for s in range(1, 4):
            total = total + decoded(codes[s][t]) * steps[s]
        for h in range(2):
            grad[:, (h * tiles + t) * LANES : (h * tiles + t + 1) * LANES] = total[h * 8 : (h + 1) * 8]
    diagonal = lax.broadcasted_iota(jnp.int32, (4, 4), 0) == lax.broadcasted_iota(jnp.int32, (4, 4), 1)

    def upright(row):
        return jnp.sum(jnp.where(diagonal, row, 0.0), axis=1, keepdims=True)

    def level_row(column):
        return jnp.sum(jnp.where(diagonal, column, 0.0), axis=0, keepdims=True)

    for e in range(2):
        for b in range(2):
            cols = slice(b * BLOCK, (b + 1) * BLOCK)
            g = grad[e * 4 : (e + 1) * 4, cols]
            m_old = m_codes[e, :, cols].astype(jnp.float32) * (upright(m_scale[e, b : b + 1, :]) / 127.0)
            v_old = v_codes[e, :, cols].astype(jnp.float32) * (upright(v_scale[e, b : b + 1, :]) / 255.0)
            m_new = beta_first * m_old + (1.0 - beta_first) * g
            v_new = beta_second * v_old + (1.0 - beta_second) * g * g
            update = m_new / first_bias / (jnp.sqrt(v_new / second_bias) + adam_eps)
            old = master[e, :, cols]
            new = old - learn_rate * (update + decay_rate * old)
            new_master[e, :, cols] = new
            m_top = jnp.max(jnp.abs(m_new), axis=1, keepdims=True)
            v_top = jnp.max(v_new, axis=1, keepdims=True)
            m_absmax[e, b : b + 1, :] = level_row(m_top)
            v_absmax[e, b : b + 1, :] = level_row(v_top)
            m_state[e, :, cols] = m_new / (m_top + scale_eps)
            v_state[e, :, cols] = v_new / (v_top + scale_eps)
            grad[e * 4 : (e + 1) * 4, cols] = new
    for k in range(16):
        for h in range(2):
            at = k * 256 + h * LANES
            tile = grad[:, at : at + LANES].astype(jnp.bfloat16)
            for copy in range(2):
                rollout[copy * 16 + k, h * 8 : (h + 1) * 8, :] = tile


def adam(codes, master, m_codes, m_scale, v_codes, v_scale):
    big = jax.ShapeDtypeStruct((2, 4, 4096), jnp.float32)
    small = jax.ShapeDtypeStruct((2, 2, 4), jnp.float32)
    new_master, m_state, m_absmax, v_state, v_absmax, weights = pl.pallas_call(
        adam_kernel,
        out_shape=[big, big, small, big, small, jax.ShapeDtypeStruct((32, 16, LANES), jnp.bfloat16)],
        scratch_shapes=[pltpu.VMEM((8, 4096), jnp.float32)],
        compiler_params=PARAMS,
        cost_estimate=pl.CostEstimate(flops=2 * 4 * 4096 * 40, bytes_accessed=2 << 20, transcendentals=0),
    )(*codes, master, m_codes, jnp.swapaxes(m_scale, 1, 2), v_codes, jnp.swapaxes(v_scale, 1, 2))
    return new_master, m_state, jnp.swapaxes(m_absmax, 1, 2), v_state, jnp.swapaxes(v_absmax, 1, 2), weights


def push_weights(weights):
    plane, group = lax.axis_index("dp") // 16, lax.axis_index("group")
    swapped = lax.all_to_all(
        weights, ("dp", "group"), 0, 0, axis_index_groups=swap_groups(), tiled=True
    )
    upper = jnp.where(plane == group, plane % 2 == 1, plane > group)
    slab = jnp.where(upper, swapped[16:], swapped[:16])
    slab = jnp.transpose(slab.reshape(16, 2, 2, 4, LANES), (2, 0, 3, 1, 4)).reshape(2, 64, 256)
    return lax.all_gather(slab, "group", axis=1, tiled=True)


def on_device(acts, out_grads, master, m_codes, m_scale, v_codes, v_scale):
    me = lax.axis_index("dp").reshape(1).astype(jnp.int32)

    far0, far1 = codes_for((2, 2), me, acts, out_grads)
    far0, far1 = lax.ppermute(far0, "dp", UP), lax.ppermute(far1, "dp", DOWN)
    down0, up1 = codes_for((3, 1), me, acts, out_grads)
    down0, up1 = lax.ppermute(down0, "dp", DOWN), lax.ppermute(up1, "dp", UP)
    up0, down1 = codes_for((1, 3), me, acts, out_grads, far0, far1)
    up0, down1 = lax.ppermute(up0, "dp", UP), lax.ppermute(down1, "dp", DOWN)
    near0, near1, kept = own_codes(me, acts, out_grads, down0, up0, up1, down1)
    near0, near1 = lax.ppermute(near0, "dp", PAIR[0]), lax.ppermute(near1, "dp", PAIR[1])
    across, rest = pair_codes(kept, near0, near1)
    codes = across_codes(rest, lax.ppermute(across, "dp", ACROSS))
    codes = [codes[0]] + [lax.ppermute(codes[k], "dp", z_shift(k)) for k in range(1, 4)]
    *state, weights = adam(codes, master, m_codes, m_scale, v_codes, v_scale)
    return (*state, push_weights(weights))


def solution(mesh):
    split = P(None, "dp", "group")
    return jax.shard_map(
        on_device,
        mesh=mesh,
        in_specs=(P(None, "dp", None),) + (split,) * 6,
        out_specs=(split,) * 5 + (P(None, None, "dp"),),
        check_vma=False,
    )
```

time: 112 us -> 104 us (0.929)
  blocking collectives: 66.6 us -> 6.49 us
  waiting for transfers between devices: 6.05 us -> 39.5 us
  starting transfers between devices: 20.2 us -> 40.6 us
  local copies, waits for them, and re-layouts: 5.76 us -> 0.84 us
  Pallas kernels: 12 us -> 15.6 us
    all_to_all x1 -> x0, blocking collectives: 60.6 us -> none  [on_device(): lax.all_to_all(codes, 'dp', 0, 0, axis_index_groups=NEAR, tiled=True)]
    ppermute x3 -> x12, waiting for transfers between devices: 2.4 us -> 33.3 us  [the longest x2 11.3 us: on_device(): up0, down1 = (lax.ppermute(up0, 'dp', UP), lax.ppermute(down1, 'dp', DOWN))]
    ppermute x3 -> x12, starting transfers between devices: 9.66 us -> 25.5 us  [the longest x3 7.38 us: on_device(): lax.ppermute(codes[k], 'dp', z_shift(k))]
    pallas_call x2 -> x6, Pallas kernels: 9.66 us -> 14.4 us  [the longest x3 11.1 us: codes_for(): pl.pallas_call(functools.partial(codes_kernel, steps), in_specs=SPECS + [...]
    all_to_all x1, starting transfers between devices: 10.5 us -> 15.1 us  [push_weights(): lax.all_to_all(weights, ('dp', 'group'), 0, 0, axis_index_groups=swap_gro...]
    unnamed x14 -> x15, local copies, waits for them, and re-layouts: 4.68 us -> 0.74 us
    all_to_all x1, waiting for transfers between devices: 3.65 us -> 6.26 us  [push_weights(): lax.all_to_all(weights, ('dp', 'group'), 0, 0, axis_index_groups=swap_gro...]
    pallas_call x1, Pallas kernels: 2.31 us -> 1.14 us  [adam(): pl.pallas_call(adam_kernel, out_shape=[big, big, small, big, small, jax.S...]
  transfers between devices with their start and end apart: 4 -> 13, of which waited for: 3 -> 11; matrix products, arithmetic and copies ran while one was open for 4% -> 0% of each run, Pallas kernels for 0% -> 7%
where the time goes in v3:
time: 104 us
  starting transfers between devices  40.6 us (39%)
  waiting for transfers between devices  39.5 us (38%)
  Pallas kernels  15.6 us (15%)
  blocking collectives  6.49 us (6%)
    all_to_all x1, starting transfers between devices, push_weights(): lax.all_to_all(weights, ('dp', 'group'), 0, 0, axis_index_groups=swap_gro...  15.1 us
    ppermute x2, waiting for transfers between devices, on_device(): up0, down1 = (lax.ppermute(up0, 'dp', UP), lax.ppermute(down1, 'dp', DOWN))  11.3 us
    pallas_call x3, Pallas kernels, codes_for(): pl.pallas_call(functools.partial(codes_kernel, steps), in_specs=SPECS + [...  11.1 us
    ppermute x3, starting transfers between devices, on_device(): lax.ppermute(codes[k], 'dp', z_shift(k))  7.38 us
    all_gather x1, blocking collectives, push_weights(): return lax.all_gather(slab, 'group', axis=1, tiled=True)  6.49 us
    all_to_all x1, waiting for transfers between devices, push_weights(): lax.all_to_all(weights, ('dp', 'group'), 0, 0, axis_index_groups=swap_gro...  6.26 us
    ppermute x2, waiting for transfers between devices, on_device(): down0, up1 = (lax.ppermute(down0, 'dp', DOWN), lax.ppermute(up1, 'dp', UP))  5.74 us
    ppermute x2, waiting for transfers between devices, on_device(): far0, far1 = (lax.ppermute(far0, 'dp', UP), lax.ppermute(far1, 'dp', DOWN))  5.38 us
  transfers between devices with their start and end apart: 13, of which 11 were waited for; matrix products, arithmetic and copies ran while one was open for 0% of the time, Pallas kernels for 7%

profile of v3, /device:TPU:1, one launch (start us, length us, event | category | flops | bytes accessed | tf_op | source)
XLA Modules:
  0.0 103.8 jit_solution(9967525695933981333)
XLA Ops:
  0.6 0.0 copy-start
  0.6 0.0 copy-start.1
  0.7 4.2 %shard_map.119 = (s16[129,16,128]{2,1,0:T(8,128)(2,1)}, s16[129,16,128]{2,1,0:T(8,128)(2,1)}) custom-call(s32[1]{0:T(128)} %bitcast.me_ref, bf16[2,256,256]{2,1,0:T(8,128)(2,1)} %acts_ref.7, bf16[2,256,4096]{2,1,0:T(8,128)(2,1)} %grads_ref.7), custom_call_target="tpu_custom_call" | custom-call | flops 268435456 | bytes 3145728 | tf_op jit(solution)/shard_map/pallas_call | solution.py:176
  4.9 2.1 %collective-permute-start.1 = (s16[129,16,128]{2,1,0:T(8,128)(2,1)}, s16[129,16,128]{2,1,0:T(8,128)(2,1)S(1)}, u32[]{:S(2)}, u32[]{:S(2)}) collective-permute-start(s16[129,16,128]{2,1,0:T(8,128)(2,1)} %get-tuple-element.28), channel_id=1, source_target_pairs={{0,4},{4,8},{8,12},{12,0},{16,20},{20,24},{24,28},{28,16},{32,36},... | collective-permute-start | bytes 1585160 | tf_op jit(solution)/shard_map/ppermute | solution.py:347
  7.0 1.4 %collective-permute-start.2 = (s16[129,16,128]{2,1,0:T(8,128)(2,1)}, s16[129,16,128]{2,1,0:T(8,128)(2,1)S(1)}, u32[]{:S(2)}, u32[]{:S(2)}) collective-permute-start(s16[129,16,128]{2,1,0:T(8,128)(2,1)} %get-tuple-element.29), channel_id=1, source_target_pairs={{0,12},{4,0},{8,4},{12,8},{16,28},{20,16},{24,20},{28,24},{32,44},... | collective-permute-start | bytes 1585160 | tf_op jit(solution)/shard_map/ppermute | solution.py:347
  8.4 4.1 %shard_map.118 = (s16[129,16,128]{2,1,0:T(8,128)(2,1)}, s16[129,16,128]{2,1,0:T(8,128)(2,1)}) custom-call(s32[1]{0:T(128)} %bitcast.me_ref, bf16[2,256,256]{2,1,0:T(8,128)(2,1)} %acts_ref.7, bf16[2,256,4096]{2,1,0:T(8,128)(2,1)} %grads_ref.7), custom_call_target="tpu_custom_call" | custom-call | flops 268435456 | bytes 3145728 | tf_op jit(solution)/shard_map/pallas_call | solution.py:176
  12.5 1.5 %collective-permute-start = (s16[129,16,128]{2,1,0:T(8,128)(2,1)}, s16[129,16,128]{2,1,0:T(8,128)(2,1)S(1)}, u32[]{:S(2)}, u32[]{:S(2)}) collective-permute-start(s16[129,16,128]{2,1,0:T(8,128)(2,1)} %get-tuple-element.27), channel_id=1, source_target_pairs={{0,12},{4,0},{8,4},{12,8},{16,28},{20,16},{24,20},{28,24},{32,44},... | collective-permute-start | bytes 1585160 | tf_op jit(solution)/shard_map/ppermute | solution.py:349
  14.0 0.1 collective-permute-start.4
  14.1 3.9 %collective-permute-done.1.rest_0_ = s16[129,16,128]{2,1,0:T(8,128)(2,1)S(1)} collective-permute-done((s16[129,16,128]{2,1,0:T(8,128)(2,1)}, s16[129,16,128]{2,1,0:T(8,128)(2,1)S(1)}, u32[]{:S(2)}, u32[]{:S(2)}) %collective-permute-start.1) | collective-permute-done | bytes 528416 | tf_op jit(solution)/shard_map/ppermute | solution.py:347
  17.9 1.5 %collective-permute-done.2.rest_1_ = s16[129,16,128]{2,1,0:T(8,128)(2,1)S(1)} collective-permute-done((s16[129,16,128]{2,1,0:T(8,128)(2,1)}, s16[129,16,128]{2,1,0:T(8,128)(2,1)S(1)}, u32[]{:S(2)}, u32[]{:S(2)}) %collective-permute-start.2) | collective-permute-done | bytes 528416 | tf_op jit(solution)/shard_map/ppermute | solution.py:347
  19.4 0.0 copy-done
  19.4 0.0 copy-done.1
  19.4 2.7 %shard_map.120 = (s16[129,16,128]{2,1,0:T(8,128)(2,1)S(1)}, s16[129,16,128]{2,1,0:T(8,128)(2,1)S(1)}) custom-call(s32[1]{0:T(128)} %bitcast.me_ref, bf16[2,256,256]{2,1,0:T(8,128)(2,1)S(1)} %copy-done.1, bf16[2,256,4096]{2,1,0:T(8,128)(2,1)S(1)} %copy-done, s16[129,16,128]{2,1,0:T(8,128)(2,1)S(1)} %collective-permute-done.1.rest_0_, ...), custom_call_target="tpu_custom_call" | custom-call | flops 268435456 | bytes 3145728 | tf_op jit(solution)/shard_map/pallas_call | solution.py:176
  22.2 1.6 %collective-permute-start.3 = (s16[129,16,128]{2,1,0:T(8,128)(2,1)S(1)}, s16[129,16,128]{2,1,0:T(8,128)(2,1)S(1)}, u32[]{:S(2)}, u32[]{:S(2)}) collective-permute-start(s16[129,16,128]{2,1,0:T(8,128)(2,1)S(1)} %get-tuple-element.30), channel_id=1, source_target_pairs={{0,4},{4,8},{8,12},{12,0},{16,20},{20,24},{24,28},{28,16},{32,36},... | collective-permute-start | bytes 1585160 | tf_op jit(solution)/shard_map/ppermute | solution.py:351
  23.8 0.0 copy-start.2
  23.8 0.0 copy-start.4
  23.8 0.0 copy-start.6
  23.8 1.2 %collective-permute-start.5 = (s16[129,16,128]{2,1,0:T(8,128)(2,1)S(1)}, s16[129,16,128]{2,1,0:T(8,128)(2,1)S(1)}, u32[]{:S(2)}, u32[]{:S(2)}) collective-permute-start(s16[129,16,128]{2,1,0:T(8,128)(2,1)S(1)} %get-tuple-element.32), channel_id=1, source_target_pairs={{0,12},{4,0},{8,4},{12,8},{16,28},{20,16},{24,20},{28,24},{32,44},... | collective-permute-start | bytes 1585160 | tf_op jit(solution)/shard_map/ppermute | solution.py:351
  25.0 5.7 %collective-permute-done.a0 = s16[129,16,128]{2,1,0:T(8,128)(2,1)S(1)} collective-permute-done((s16[129,16,128]{2,1,0:T(8,128)(2,1)}, s16[129,16,128]{2,1,0:T(8,128)(2,1)S(1)}, u32[]{:S(2)}, u32[]{:S(2)}) %collective-permute-start) | collective-permute-done | bytes 528416 | tf_op jit(solution)/shard_map/ppermute | solution.py:349
  30.8 0.0 collective-permute-done.4.a1
  30.8 10.0 %collective-permute-done.3.b0 = s16[129,16,128]{2,1,0:T(8,128)(2,1)S(1)} collective-permute-done((s16[129,16,128]{2,1,0:T(8,128)(2,1)S(1)}, s16[129,16,128]{2,1,0:T(8,128)(2,1)S(1)}, u32[]{:S(2)}, u32[]{:S(2)}) %collective-permute-start.3) | collective-permute-done | bytes 528416 | tf_op jit(solution)/shard_map/ppermute | solution.py:351
  40.8 1.3 %collective-permute-done.5.b1 = s16[129,16,128]{2,1,0:T(8,128)(2,1)S(1)} collective-permute-done((s16[129,16,128]{2,1,0:T(8,128)(2,1)S(1)}, s16[129,16,128]{2,1,0:T(8,128)(2,1)S(1)}, u32[]{:S(2)}, u32[]{:S(2)}) %collective-permute-start.5) | collective-permute-done | bytes 528416 | tf_op jit(solution)/shard_map/ppermute | solution.py:351
  42.1 2.7 %shard_map.121 = (s16[65,16,128]{2,1,0:T(8,128)(2,1)S(1)}, s16[65,16,128]{2,1,0:T(8,128)(2,1)S(1)}, f32[2,32,4096]{2,1,0:T(8,128)S(1)}) custom-call(s32[1]{0:T(128)} %bitcast.me_ref, bf16[2,256,256]{2,1,0:T(8,128)(2,1)S(1)} %copy-done.1, bf16[2,256,4096]{2,1,0:T(8,128)(2,1)S(1)} %copy-done, s16[129,16,128]{2,1,0:T(8,128)(2,1)S(1)} %collective-permute-done.a0, ...), custom_call_target="tpu_custom_call" | custom-call | flops 268435456 | bytes 3145728 | tf_op jit(solution)/shard_map/pallas_call | solution.py:195
  44.8 2.4 %collective-permute-start.6 = (s16[65,16,128]{2,1,0:T(8,128)(2,1)S(1)}, s16[65,16,128]{2,1,0:T(8,128)(2,1)S(1)}, u32[]{:S(2)}, u32[]{:S(2)}) collective-permute-start(s16[65,16,128]{2,1,0:T(8,128)(2,1)S(1)} %get-tuple-element.34), channel_id=1, source_target_pairs={{0,16},{4,20},{8,24},{12,28},{16,0},{20,4},{24,8},{28,12},{32,48},... | collective-permute-start | bytes 798728 | tf_op jit(solution)/shard_map/ppermute | solution.py:353
  47.2 4.7 %collective-permute-start.7 = (s16[65,16,128]{2,1,0:T(8,128)(2,1)S(1)}, s16[65,16,128]{2,1,0:T(8,128)(2,1)S(1)}, u32[]{:S(2)}, u32[]{:S(2)}) collective-permute-start(s16[65,16,128]{2,1,0:T(8,128)(2,1)S(1)} %get-tuple-element.35), channel_id=1, source_target_pairs={{0,112},{4,116},{8,120},{12,124},{16,32},{20,36},{24,40},{28,44},{... | collective-permute-start | bytes 798728 | tf_op jit(solution)/shard_map/ppermute | solution.py:353
  51.8 0.4 collective-permute-done.6.got0
  52.2 4.5 %collective-permute-done.7.got1 = s16[65,16,128]{2,1,0:T(8,128)(2,1)S(1)} collective-permute-done((s16[65,16,128]{2,1,0:T(8,128)(2,1)S(1)}, s16[65,16,128]{2,1,0:T(8,128)(2,1)S(1)}, u32[]{:S(2)}, u32[]{:S(2)}) %collective-permute-start.7) | collective-permute-done | bytes 266272 | tf_op jit(solution)/shard_map/ppermute | solution.py:353
  56.7 0.4 shard_map.122
  57.1 3.2 %collective-permute-start.8 = (s16[65,16,128]{2,1,0:T(8,128)(2,1)S(1)}, s16[65,16,128]{2,1,0:T(8,128)(2,1)S(1)}, u32[]{:S(2)}, u32[]{:S(2)}) collective-permute-start(s16[65,16,128]{2,1,0:T(8,128)(2,1)S(1)} %get-tuple-element.37), channel_id=1, source_target_pairs={{0,128},{4,132},{8,136},{12,140},{16,144},{20,148},{24,152},{28,15... | collective-permute-start | bytes 798728 | tf_op jit(solution)/shard_map/ppermute | solution.py:355
  60.2 3.9 %collective-permute-done.8.got = s16[65,16,128]{2,1,0:T(8,128)(2,1)S(1)} collective-permute-done((s16[65,16,128]{2,1,0:T(8,128)(2,1)S(1)}, s16[65,16,128]{2,1,0:T(8,128)(2,1)S(1)}, u32[]{:S(2)}, u32[]{:S(2)}) %collective-permute-start.8) | collective-permute-done | bytes 266272 | tf_op jit(solution)/shard_map/ppermute | solution.py:355
  64.1 0.3 shard_map.123
  64.4 0.1 collective-permute-start.9
  64.5 3.8 %collective-permute-start.10 = (s16[17,16,128]{2,1,0:T(8,128)(2,1)S(1)}, s16[17,16,128]{2,1,0:T(8,128)(2,1)S(1)}, u32[]{:S(2)}, u32[]{:S(2)}) collective-permute-start(s16[17,16,128]{2,1,0:T(8,128)(2,1)S(1)} %get-tuple-element.40), channel_id=1, source_target_pairs={{0,64},{4,68},{8,72},{12,76},{16,80},{20,84},{24,88},{28,92},{32,9... | collective-permute-start | bytes 208904 | tf_op jit(solution)/shard_map/ppermute | solution.py:356
  68.3 3.5 %collective-permute-start.11 = (s16[17,16,128]{2,1,0:T(8,128)(2,1)S(1)}, s16[17,16,128]{2,1,0:T(8,128)(2,1)S(1)}, u32[]{:S(2)}, u32[]{:S(2)}) collective-permute-start(s16[17,16,128]{2,1,0:T(8,128)(2,1)S(1)} %get-tuple-element.41), channel_id=1, source_target_pairs={{0,96},{4,100},{8,104},{12,108},{16,112},{20,116},{24,120},{28,124... | collective-permute-start | bytes 208904 | tf_op jit(solution)/shard_map/ppermute | solution.py:356
  71.8 0.0 collective-permute-done.9.c1
  71.8 0.5 collective-permute-done.10.c2
  72.3 1.6 %collective-permute-done.11.c3 = s16[17,16,128]{2,1,0:T(8,128)(2,1)S(1)} collective-permute-done((s16[17,16,128]{2,1,0:T(8,128)(2,1)S(1)}, s16[17,16,128]{2,1,0:T(8,128)(2,1)S(1)}, u32[]{:S(2)}, u32[]{:S(2)}) %collective-permute-start.11) | collective-permute-done | bytes 69664 | tf_op jit(solution)/shard_map/ppermute | solution.py:356
  73.9 0.0 copy-done.2
  73.9 0.0 copy-done.3
  73.9 0.0 copy-done.4
  73.9 0.0 copy-done.5
  73.9 0.0 copy-done.6
  74.0 1.1 %shard_map.124 = (f32[2,4,4096]{2,1,0:T(4,128)}, f32[2,4,4096]{2,1,0:T(4,128)}, f32[2,2,4]{2,1,0:T(2,128)}, f32[2,4,4096]{2,1,0:T(4,128)}, f32[2,2,4]{2,1,0:T(2,128)}, /*index=5*/bf16[32,16,128]{2,1,0:T(8,128)(2,1)}) custom-call(s16[17,16,128]{2,1,0:T(8,128)(2,1)S(1)} %get-tuple-element.38.c0, s16[17,16,128]{2,1,0:T(8,128)(2,1)S(1)} %collective-permute-done.9.c1, ...), custom_call_target="tpu_custom_call" | custom-call | flops 1310720 | bytes 2097152 | tf_op jit(solution)/shard_map/pallas_call | solution.py:322
  75.1 15.1 %all-to-all-start = ((bf16[32,16,128]{2,1,0:T(8,128)(2,1)}), bf16[32,16,128]{2,1,0:T(8,128)(2,1)S(1)}, u32[]{:S(2)}, u32[]{:S(2)}) async-start(bf16[32,16,128]{2,1,0:T(8,128)(2,1)} %get-tuple-element.47), calls=%async_computation | async-start | bytes 262144 | tf_op jit(solution)/shard_map/all_to_all | solution.py:334
  90.3 6.3 %all-to-all-done = bf16[32,16,128]{2,1,0:T(8,128)(2,1)S(1)} async-done(((bf16[32,16,128]{2,1,0:T(8,128)(2,1)}), bf16[32,16,128]{2,1,0:T(8,128)(2,1)S(1)}, u32[]{:S(2)}, u32[]{:S(2)}) %all-to-all-start) | async-done | bytes 131104 | tf_op jit(solution)/shard_map/all_to_all | solution.py:334
  96.5 0.1 copy.13
  96.7 6.5 %all_gather.3 = bf16[2,256,256]{2,1,0:T(8,128)(2,1)S(1)} all-gather(bf16[2,64,256]{2,1,0:T(8,128)(2,1)S(1)} %reshape.23), channel_id=1, replica_groups=mesh['dp'=64,'group'=4] {'group'}, dimensions={1}, use_global_device_ids=true | all-gather | bytes 327680 | tf_op jit(solution)/shard_map/all_gather | solution.py:340
  103.1 0.7 copy.15
  (4 shorter events, 0.1 us)
Async XLA Ops:
  0.6 18.8 %copy-start = (bf16[2,256,4096]{2,1,0:T(8,128)(2,1)S(1)}, bf16[2,256,4096]{2,1,0:T(8,128)(2,1)}, u32[]{:S(2)}) copy-start(bf16[2,256,4096]{2,1,0:T(8,128)(2,1)} %grads_ref.7) | copy-start | bytes 12582916
  0.6 18.8 %copy-start.1 = (bf16[2,256,256]{2,1,0:T(8,128)(2,1)S(1)}, bf16[2,256,256]{2,1,0:T(8,128)(2,1)}, u32[]{:S(2)}) copy-start(bf16[2,256,256]{2,1,0:T(8,128)(2,1)} %acts_ref.7) | copy-start | bytes 786436
  4.9 13.0 %collective-permute-start.1 = (s16[129,16,128]{2,1,0:T(8,128)(2,1)}, s16[129,16,128]{2,1,0:T(8,128)(2,1)S(1)}, u32[]{:S(2)}, u32[]{:S(2)}) collective-permute-start(s16[129,16,128]{2,1,0:T(8,128)(2,1)} %get-tuple-element.28), channel_id=1, source_target_pairs={{0,4},{4,8},{8,12},{12,0},{16,20},{20,24},{24,28},{28,16},{32,36},... | collective-permute-start | bytes 1585160 | tf_op jit(solution)/shard_map/ppermute | solution.py:347
  7.0 12.4 %collective-permute-start.2 = (s16[129,16,128]{2,1,0:T(8,128)(2,1)}, s16[129,16,128]{2,1,0:T(8,128)(2,1)S(1)}, u32[]{:S(2)}, u32[]{:S(2)}) collective-permute-start(s16[129,16,128]{2,1,0:T(8,128)(2,1)} %get-tuple-element.29), channel_id=1, source_target_pairs={{0,12},{4,0},{8,4},{12,8},{16,28},{20,16},{24,20},{28,24},{32,44},... | collective-permute-start | bytes 1585160 | tf_op jit(solution)/shard_map/ppermute | solution.py:347
  12.5 18.2 %collective-permute-start = (s16[129,16,128]{2,1,0:T(8,128)(2,1)}, s16[129,16,128]{2,1,0:T(8,128)(2,1)S(1)}, u32[]{:S(2)}, u32[]{:S(2)}) collective-permute-start(s16[129,16,128]{2,1,0:T(8,128)(2,1)} %get-tuple-element.27), channel_id=1, source_target_pairs={{0,12},{4,0},{8,4},{12,8},{16,28},{20,16},{24,20},{28,24},{32,44},... | collective-permute-start | bytes 1585160 | tf_op jit(solution)/shard_map/ppermute | solution.py:349
  14.0 16.8 %collective-permute-start.4 = (s16[129,16,128]{2,1,0:T(8,128)(2,1)}, s16[129,16,128]{2,1,0:T(8,128)(2,1)S(1)}, u32[]{:S(2)}, u32[]{:S(2)}) collective-permute-start(s16[129,16,128]{2,1,0:T(8,128)(2,1)} %get-tuple-element.31), channel_id=1, source_target_pairs={{0,4},{4,8},{8,12},{12,0},{16,20},{20,24},{24,28},{28,16},{32,36},... | collective-permute-start | bytes 1585160 | tf_op jit(solution)/shard_map/ppermute | solution.py:349
  22.2 18.6 %collective-permute-start.3 = (s16[129,16,128]{2,1,0:T(8,128)(2,1)S(1)}, s16[129,16,128]{2,1,0:T(8,128)(2,1)S(1)}, u32[]{:S(2)}, u32[]{:S(2)}) collective-permute-start(s16[129,16,128]{2,1,0:T(8,128)(2,1)S(1)} %get-tuple-element.30), channel_id=1, source_target_pairs={{0,4},{4,8},{8,12},{12,0},{16,20},{20,24},{24,28},{28,16},{32,36},... | collective-permute-start | bytes 1585160 | tf_op jit(solution)/shard_map/ppermute | solution.py:351
  23.8 50.1 %copy-start.2 = (f32[2,4,4096]{2,1,0:T(4,128)S(1)}, f32[2,4,4096]{2,1,0:T(4,128)}, u32[]{:S(2)}) copy-start(f32[2,4,4096]{2,1,0:T(4,128)} %master.1) | copy-start | bytes 393220
  23.8 50.1 %copy-start.3 = (s32[2,4,4096]{2,1,0:T(4,128)S(1)}, s32[2,4,4096]{2,1,0:T(4,128)}, u32[]{:S(2)}) copy-start(s32[2,4,4096]{2,1,0:T(4,128)} %m_codes.1) | copy-start | bytes 393220
  23.8 50.1 %copy-start.4 = (s32[2,4,4096]{2,1,0:T(4,128)S(1)}, s32[2,4,4096]{2,1,0:T(4,128)}, u32[]{:S(2)}) copy-start(s32[2,4,4096]{2,1,0:T(4,128)} %v_codes.1) | copy-start | bytes 393220
  23.8 50.1 %copy-start.5 = (f32[2,4,2]{1,2,0:T(2,128)S(1)}, f32[2,4,2]{1,2,0:T(2,128)}, u32[]{:S(2)}) copy-start(f32[2,4,2]{1,2,0:T(2,128)} %param.11) | copy-start | bytes 196
  23.8 50.1 %copy-start.6 = (f32[2,4,2]{1,2,0:T(2,128)S(1)}, f32[2,4,2]{1,2,0:T(2,128)}, u32[]{:S(2)}) copy-start(f32[2,4,2]{1,2,0:T(2,128)} %param.13) | copy-start | bytes 196
  23.8 18.2 %collective-permute-start.5 = (s16[129,16,128]{2,1,0:T(8,128)(2,1)S(1)}, s16[129,16,128]{2,1,0:T(8,128)(2,1)S(1)}, u32[]{:S(2)}, u32[]{:S(2)}) collective-permute-start(s16[129,16,128]{2,1,0:T(8,128)(2,1)S(1)} %get-tuple-element.32), channel_id=1, source_target_pairs={{0,12},{4,0},{8,4},{12,8},{16,28},{20,16},{24,20},{28,24},{32,44},... | collective-permute-start | bytes 1585160 | tf_op jit(solution)/shard_map/ppermute | solution.py:351
  44.8 7.4 %collective-permute-start.6 = (s16[65,16,128]{2,1,0:T(8,128)(2,1)S(1)}, s16[65,16,128]{2,1,0:T(8,128)(2,1)S(1)}, u32[]{:S(2)}, u32[]{:S(2)}) collective-permute-start(s16[65,16,128]{2,1,0:T(8,128)(2,1)S(1)} %get-tuple-element.34), channel_id=1, source_target_pairs={{0,16},{4,20},{8,24},{12,28},{16,0},{20,4},{24,8},{28,12},{32,48},... | collective-permute-start | bytes 798728 | tf_op jit(solution)/shard_map/ppermute | solution.py:353
  47.2 9.6 %collective-permute-start.7 = (s16[65,16,128]{2,1,0:T(8,128)(2,1)S(1)}, s16[65,16,128]{2,1,0:T(8,128)(2,1)S(1)}, u32[]{:S(2)}, u32[]{:S(2)}) collective-permute-start(s16[65,16,128]{2,1,0:T(8,128)(2,1)S(1)} %get-tuple-element.35), channel_id=1, source_target_pairs={{0,112},{4,116},{8,120},{12,124},{16,32},{20,36},{24,40},{28,44},{... | collective-permute-start | bytes 798728 | tf_op jit(solution)/shard_map/ppermute | solution.py:353
  57.1 7.0 %collective-permute-start.8 = (s16[65,16,128]{2,1,0:T(8,128)(2,1)S(1)}, s16[65,16,128]{2,1,0:T(8,128)(2,1)S(1)}, u32[]{:S(2)}, u32[]{:S(2)}) collective-permute-start(s16[65,16,128]{2,1,0:T(8,128)(2,1)S(1)} %get-tuple-element.37), channel_id=1, source_target_pairs={{0,128},{4,132},{8,136},{12,140},{16,144},{20,148},{24,152},{28,15... | collective-permute-start | bytes 798728 | tf_op jit(solution)/shard_map/ppermute | solution.py:355
  64.4 7.4 %collective-permute-start.9 = (s16[17,16,128]{2,1,0:T(8,128)(2,1)S(1)}, s16[17,16,128]{2,1,0:T(8,128)(2,1)S(1)}, u32[]{:S(2)}, u32[]{:S(2)}) collective-permute-start(s16[17,16,128]{2,1,0:T(8,128)(2,1)S(1)} %get-tuple-element.39), channel_id=1, source_target_pairs={{0,32},{4,36},{8,40},{12,44},{16,48},{20,52},{24,56},{28,60},{32,6... | collective-permute-start | bytes 208904 | tf_op jit(solution)/shard_map/ppermute | solution.py:356
  64.5 7.8 %collective-permute-start.10 = (s16[17,16,128]{2,1,0:T(8,128)(2,1)S(1)}, s16[17,16,128]{2,1,0:T(8,128)(2,1)S(1)}, u32[]{:S(2)}, u32[]{:S(2)}) collective-permute-start(s16[17,16,128]{2,1,0:T(8,128)(2,1)S(1)} %get-tuple-element.40), channel_id=1, source_target_pairs={{0,64},{4,68},{8,72},{12,76},{16,80},{20,84},{24,88},{28,92},{32,9... | collective-permute-start | bytes 208904 | tf_op jit(solution)/shard_map/ppermute | solution.py:356
  68.3 5.6 %collective-permute-start.11 = (s16[17,16,128]{2,1,0:T(8,128)(2,1)S(1)}, s16[17,16,128]{2,1,0:T(8,128)(2,1)S(1)}, u32[]{:S(2)}, u32[]{:S(2)}) collective-permute-start(s16[17,16,128]{2,1,0:T(8,128)(2,1)S(1)} %get-tuple-element.41), channel_id=1, source_target_pairs={{0,96},{4,100},{8,104},{12,108},{16,112},{20,116},{24,120},{28,124... | collective-permute-start | bytes 208904 | tf_op jit(solution)/shard_map/ppermute | solution.py:356
  75.1 21.4 %all-to-all-start = ((bf16[32,16,128]{2,1,0:T(8,128)(2,1)}), bf16[32,16,128]{2,1,0:T(8,128)(2,1)S(1)}, u32[]{:S(2)}, u32[]{:S(2)}) async-start(bf16[32,16,128]{2,1,0:T(8,128)(2,1)} %get-tuple-element.47), calls=%async_computation | async-start | bytes 262144 | tf_op jit(solution)/shard_map/all_to_all | solution.py:334

commit v4 on v3

v4 whole, which is shorter than its diff:
```python
import functools

import jax
import jax.numpy as jnp
from jax import lax
from jax.experimental import pallas as pl
from jax.experimental.pallas import tpu as pltpu
from jax.sharding import PartitionSpec as P

BLOCK = 2048
LANES = 128
TOP = 32700.0
STEPS = 16.0

beta_first = 0.9
beta_second = 0.999
first_bias = 1.0 - 0.9**10
second_bias = 1.0 - 0.999**10
learn_rate = 0.001
decay_rate = 0.1
adam_eps = 1e-08
scale_eps = 1e-06

PART_A = (0, 2560)
PART_B = (2560, 1536)
PIECE = 256

PARAMS = pltpu.CompilerParams(vmem_limit_bytes=20 * 1024 * 1024)
FIRST_PARAMS = pltpu.CompilerParams(vmem_limit_bytes=56 * 1024 * 1024)


def moved(step):
    def index(y, z, x):
        return y % 2 * 32 + z % 8 * 4 + x % 4

    return [(index(y, z, x), index(*step(y, z, x))) for y in range(2) for z in range(8) for x in range(4)]


UP = moved(lambda y, z, x: (y, z, x + 1))
DOWN = moved(lambda y, z, x: (y, z, x - 1))
TWO = moved(lambda y, z, x: (y, z, x + 2))
PAIR = [moved(lambda y, z, x, e=e: (y, z + 1 if z % 2 == e else z - 1, x)) for e in range(2)]
ACROSS = moved(lambda y, z, x: (y + 1, z, x))


def z_shift(k):
    return moved(lambda y, z, x: (y, z + 2 * k, x))


def swap_groups():
    pairs = [((a, g), (g, a)) for a in range(4) for g in range(a)]
    pairs += [((0, 0), (1, 1)), ((2, 2), (3, 3))]
    return [[(a * 16 + k) * 4 + g for a, g in pair for k in range(16)] for pair in pairs]


def level_of(top):
    return jnp.ceil(STEPS * jnp.log2(jnp.maximum(top, 1e-30)))


def step_of(level):
    return jnp.exp2(level * (1.0 / STEPS)) * (1.0 / TOP)


def unit_of(level):
    return jnp.exp2(level * (-1.0 / STEPS)) * TOP


def to_short(values):
    return values.astype(jnp.int32).astype(jnp.int16)


def coded(values, unit):
    return to_short(jnp.round(values * unit))


def decoded(codes):
    return codes.astype(jnp.int32).astype(jnp.float32)


def lane_max(top, values):
    for j in range(values.shape[1] // LANES):
        top = jnp.maximum(top, jnp.abs(values[:, j * LANES : (j + 1) * LANES]))
    return top


def lane_index(rows):
    return lax.broadcasted_iota(jnp.int32, (rows, LANES), 1)


def rows_a(steps):
    def rows(expert, place, new):
        y, z, x = place
        i, k, here_y, here_z = new & 3, (new >> 2) & 3, (new >> 4) & 1, new >> 5
        return old_row(expert, place, here_y, here_z, k, x + steps[expert], i)

    return rows


def rows_b(first_step, here_y):
    def rows(expert, place, new):
        i, k, here_z, step = new & 3, (new >> 2) & 3, (new >> 4) & 1, new >> 5
        return old_row(expert, place, here_y, here_z, k, place[2] + first_step + step, i)

    return rows


def old_row(expert, place, here_y, here_z, k, x, i):
    y, z, _ = place
    neighbour = jnp.where((z & 1) == expert, z + 1, z + 7)
    row_y = jnp.where(here_y == 1, y, 1 - y)
    row_z = (jnp.where(here_z == 1, z, neighbour) + 2 * k) & 7
    return row_y * 128 + row_z * 16 + (x & 3) * 4 + i


def picked(acts, expert, place, rows, count):
    new = lax.broadcasted_iota(jnp.int32, (count, 256), 0)
    old = lax.broadcasted_iota(jnp.int32, (count, 256), 1)
    pick = jnp.where(old == rows(expert, place, new), 1.0, 0.0).astype(jnp.bfloat16)
    return lax.dot_general(
        pick, acts, (((1,), (1,)), ((), ())), preferred_element_type=jnp.float32
    ).astype(jnp.bfloat16)


def add_up(part, rows, me_ref, acts_ref, grads_ref, received, acts, grads, sums, sems):
    start, width = part
    tiles, count = width // LANES, sums.shape[1] // 16
    pieces = [(e, at) for e in range(2) for at in range(0, width, width // 2)]

    def load(n):
        e, at = pieces[n]
        source = grads_ref.at[e, :, pl.ds(start + at, width // 2)]
        return pltpu.make_async_copy(source, grads.at[e, :, pl.ds(at, width // 2)], sems.at[n])

    load_acts = pltpu.make_async_copy(acts_ref, acts, sems.at[len(pieces)])
    load_acts.start()
    for n in range(len(pieces)):
        load(n).start()
    load_acts.wait()
    me = me_ref[0]
    place = me >> 5, (me >> 2) & 7, me & 3
    lhs = [picked(acts[e], e, place, rows, 16 * count) for e in range(2)]
    scales = []
    for e in range(2):
        notes = [decoded(r[r.shape[0] - 1]) for r, _ in received[e]]
        scales.append(
            [[step_of(note[:, at + g : at + g + 1]) for note, (_, at) in zip(notes, received[e])] for g in range(count)]
        )
    tops = [[jnp.zeros((16, LANES), jnp.float32)] * count for _ in range(2)]
    for n, (e, first) in enumerate(pieces):
        load(n).wait()
        for at in range(first, first + width // 2, PIECE):
            part_sums = jnp.dot(lhs[e], grads[e, :, at : at + PIECE], preferred_element_type=jnp.float32)
            for g in range(count):
                for j in range(0, PIECE, LANES):
                    total = part_sums[g * 16 : (g + 1) * 16, j : j + LANES]
                    for (r, group), scale in zip(received[e], scales[e][g]):
                        total = total + decoded(r[(group + g) * tiles + (at + j) // LANES]) * scale
                    sums[e, g * 16 : (g + 1) * 16, at + j : at + j + LANES] = total
                    tops[e][g] = jnp.maximum(tops[e][g], jnp.abs(total))
    return tops


def codes_kernel(steps, me_ref, acts_ref, grads_ref, *rest):
    got, (out0, out1, *work) = rest[:-6], rest[-6:]
    received = [[(r, 0) for r in got[e : e + 1]] for e in range(2)]
    tops = add_up(PART_A, rows_a(steps), me_ref, acts_ref, grads_ref, received, *work)
    sums = work[2]
    for e, out in enumerate((out0, out1)):
        write_groups(out, [(sums.at[e], g, tops[e][g]) for g in range(4)])


def write_groups(out, groups):
    tiles = (out.shape[0] - 1) // len(groups)
    lane = lane_index(16)
    note = jnp.zeros((16, LANES), jnp.int32)
    for n, (sums, g, top) in enumerate(groups):
        level = level_of(jnp.max(top, axis=1, keepdims=True))
        unit = unit_of(level)
        note = jnp.where(lane == n, level.astype(jnp.int32), note)
        for t in range(tiles):
            out[n * tiles + t] = coded(sums[g * 16 : (g + 1) * 16, t * LANES : (t + 1) * LANES], unit)
    out[len(groups) * tiles] = note.astype(jnp.int16)


SPECS = [
    pl.BlockSpec(memory_space=pltpu.SMEM),
    pl.BlockSpec(memory_space=pl.ANY),
    pl.BlockSpec(memory_space=pl.ANY),
]


VMEM = pl.BlockSpec(memory_space=pltpu.VMEM)


def scratch(part, rows):
    width = part[1]
    return [
        pltpu.VMEM((2, 256, 256), jnp.bfloat16),
        pltpu.VMEM((2, 256, width), jnp.bfloat16),
        pltpu.VMEM((2, rows, width), jnp.float32),
        pltpu.SemaphoreType.DMA((5,)),
    ]


def codes_of(groups, part):
    return jax.ShapeDtypeStruct((groups * part[1] // LANES + 1, 16, LANES), jnp.int16)


def sums_of(rows, part):
    return jax.ShapeDtypeStruct((2, rows, part[1]), jnp.float32)


COST = pl.CostEstimate(flops=4 * 64 * 256 * 4096, bytes_accessed=6 << 20, transcendentals=0)


def call(kernel, outs, work, ins, params=PARAMS, inputs=3):
    return pl.pallas_call(
        kernel,
        in_specs=SPECS[:inputs] + [VMEM] * (len(ins) - inputs),
        out_shape=outs,
        scratch_shapes=work,
        compiler_params=params,
        cost_estimate=COST,
    )(*ins)


def codes_for(steps, *ins):
    return call(functools.partial(codes_kernel, steps), [codes_of(4, PART_A)] * 2, scratch(PART_A, 64), ins)


def own_kernel(me_ref, acts_ref, grads_ref, a0, b0, a1, b1, out0, out1, kept, *work):
    received = [[(a0, 0), (b0, 0)], [(a1, 0), (b1, 0)]]
    tops = add_up(PART_A, rows_a((0, 0)), me_ref, acts_ref, grads_ref, received, *work)
    sums = work[2]
    for e, out in enumerate((out0, out1)):
        write_groups(out, [(sums.at[e], g, tops[e][g]) for g in range(2)])
        kept[e] = sums[e, 32:]


def own_codes(*ins):
    return call(own_kernel, [codes_of(2, PART_A)] * 2 + [sums_of(32, PART_A)], scratch(PART_A, 64), ins)


def pair_kernel(kept, got0, got1, out, rest, sums):
    tiles = PART_A[1] // LANES
    tops = []
    for e, got in enumerate((got0, got1)):
        note = decoded(got[2 * tiles])
        for g in range(2):
            scale = step_of(note[:, g : g + 1])
            top = jnp.zeros((16, LANES), jnp.float32)
            for t in range(tiles):
                cols = slice(t * LANES, (t + 1) * LANES)
                total = kept[e, g * 16 : (g + 1) * 16, cols] + decoded(got[g * tiles + t]) * scale
                if g == 0:
                    sums[e, :, cols] = total
                    top = jnp.maximum(top, jnp.abs(total))
                else:
                    rest[e, :, cols] = total
            if g == 0:
                tops.append(top)
    write_groups(out, [(sums.at[e], 0, tops[e]) for e in range(2)])


def pair_codes(*ins):
    outs = [codes_of(2, PART_A), sums_of(16, PART_A)]
    return call(pair_kernel, outs, [pltpu.VMEM((2, 16, PART_A[1]), jnp.float32)], ins, inputs=0)


def across_first_kernel(me_ref, acts_ref, grads_ref, out, *work):
    tops = add_up(PART_B, rows_b(0, 0), me_ref, acts_ref, grads_ref, [[], []], *work)
    write_groups(out, [(work[2].at[e], g, tops[e][g]) for e in range(2) for g in range(8)])


def across_first(*ins):
    return call(across_first_kernel, codes_of(16, PART_B), scratch(PART_B, 128), ins, FIRST_PARAMS)


def along_x_kernel(me_ref, acts_ref, grads_ref, got, out1, out2, out3, *work):
    received = [[(got, e * 8 + 2)] for e in range(2)]
    tops = add_up(PART_B, rows_b(1, 1), me_ref, acts_ref, grads_ref, received, *work)
    for k, out in enumerate((out1, out2, out3)):
        write_groups(out, [(work[2].at[e], g, tops[e][g]) for e in range(2) for g in (2 * k, 2 * k + 1)])


def along_x(*ins):
    return call(along_x_kernel, [codes_of(4, PART_B)] * 3, scratch(PART_B, 96), ins)


def own_b_kernel(me_ref, acts_ref, grads_ref, got, r1, r2, r3, out0, out1, kept, *work):
    received = [[(got, e * 8)] + [(r, e * 2) for r in (r1, r2, r3)] for e in range(2)]
    tops = add_up(PART_B, rows_b(0, 1), me_ref, acts_ref, grads_ref, received, *work)
    sums = work[2]
    for e, out in enumerate((out0, out1)):
        write_groups(out, [(sums.at[e], 0, tops[e][0])])
        kept[e] = sums[e, 16:]


def own_b_codes(*ins):
    return call(own_b_kernel, [codes_of(1, PART_B)] * 2 + [sums_of(16, PART_B)], scratch(PART_B, 32), ins)


def join_kernel(rest, got, kept, near0, near1, *refs):
    *outs, sums = refs
    tiles = PART_A[1] // LANES
    note = decoded(got[2 * tiles])
    for e in range(2):
        scale = step_of(note[:, e : e + 1])
        for t in range(tiles):
            cols = slice(t * LANES, (t + 1) * LANES)
            sums[e, :, cols] = rest[e, :, cols] + decoded(got[e * tiles + t]) * scale
        near = (near0, near1)[e]
        scale = step_of(decoded(near[near.shape[0] - 1])[:, :1])
        for t in range(PART_B[1] // LANES):
            at = PART_B[0] + t * LANES
            sums[e, :, at : at + LANES] = kept[e, :, t * LANES : (t + 1) * LANES] + decoded(near[t]) * scale
    upper = lax.broadcasted_iota(jnp.int32, (8, 1), 0) < 4
    for pair in range(2):
        tile = slice(pair * 8, pair * 8 + 8)
        z = [[sums[e, tile, h * BLOCK : (h + 1) * BLOCK] for h in range(2)] for e in range(2)]
        even = [jnp.where(upper, z[0][h], pltpu.roll(z[1][h], 4, 0)) for h in range(2)]
        odd = [jnp.where(upper, pltpu.roll(z[0][h], 4, 0), z[1][h]) for h in range(2)]
        for out, halves in ((outs[pair * 2], even), (outs[pair * 2 + 1], odd)):
            values = jnp.concatenate(halves, axis=0)
            top = lane_max(jnp.zeros((16, LANES), jnp.float32), values)
            level = level_of(jnp.max(top, axis=1, keepdims=True))
            unit = unit_of(level)
            for t in range(16):
                out[t] = coded(values[:, t * LANES : (t + 1) * LANES], unit)
            out[16] = to_short(jnp.broadcast_to(level, (16, LANES)))


def join(*ins):
    outs = [jax.ShapeDtypeStruct((17, 16, LANES), jnp.int16)] * 4
    return call(join_kernel, outs, [pltpu.VMEM((2, 16, 2 * BLOCK), jnp.float32)], ins, inputs=0)


def adam_kernel(c0, c1, c2, c3, master, m_codes, m_scale, v_codes, v_scale,
                new_master, m_state, m_absmax, v_state, v_absmax, rollout, grad):
    codes = (c0, c1, c2, c3)
    tiles = BLOCK // LANES
    steps = [step_of(decoded(c[tiles])[:, :1]) for c in codes]
    for t in range(tiles):
        total = decoded(c0[t]) * steps[0]
        for s in range(1, 4):
            total = total + decoded(codes[s][t]) * steps[s]
        for h in range(2):
            grad[:, (h * tiles + t) * LANES : (h * tiles + t + 1) * LANES] = total[h * 8 : (h + 1) * 8]
    diagonal = lax.broadcasted_iota(jnp.int32, (4, 4), 0) == lax.broadcasted_iota(jnp.int32, (4, 4), 1)

    def upright(row):
        return jnp.sum(jnp.where(diagonal, row, 0.0), axis=1, keepdims=True)

    def level_row(column):
        return jnp.sum(jnp.where(diagonal, column, 0.0), axis=0, keepdims=True)

    for e in range(2):
        for b in range(2):
            cols = slice(b * BLOCK, (b + 1) * BLOCK)
            g = grad[e * 4 : (e + 1) * 4, cols]
            m_old = m_codes[e, :, cols].astype(jnp.float32) * (upright(m_scale[e, b : b + 1, :]) / 127.0)
            v_old = v_codes[e, :, cols].astype(jnp.float32) * (upright(v_scale[e, b : b + 1, :]) / 255.0)
            m_new = beta_first * m_old + (1.0 - beta_first) * g
            v_new = beta_second * v_old + (1.0 - beta_second) * g * g
            update = m_new / first_bias / (jnp.sqrt(v_new / second_bias) + adam_eps)
            old = master[e, :, cols]
            new = old - learn_rate * (update + decay_rate * old)
            new_master[e, :, cols] = new
            m_top = jnp.max(jnp.abs(m_new), axis=1, keepdims=True)
            v_top = jnp.max(v_new, axis=1, keepdims=True)
            m_absmax[e, b : b + 1, :] = level_row(m_top)
            v_absmax[e, b : b + 1, :] = level_row(v_top)
            m_state[e, :, cols] = m_new / (m_top + scale_eps)
            v_state[e, :, cols] = v_new / (v_top + scale_eps)
            grad[e * 4 : (e + 1) * 4, cols] = new
    for k in range(16):
        for h in range(2):
            at = k * 256 + h * LANES
            tile = grad[:, at : at + LANES].astype(jnp.bfloat16)
            for copy in range(2):
                rollout[copy * 16 + k, h * 8 : (h + 1) * 8, :] = tile


def adam(codes, master, m_codes, m_scale, v_codes, v_scale):
    big = jax.ShapeDtypeStruct((2, 4, 4096), jnp.float32)
    small = jax.ShapeDtypeStruct((2, 2, 4), jnp.float32)
    new_master, m_state, m_absmax, v_state, v_absmax, weights = pl.pallas_call(
        adam_kernel,
        out_shape=[big, big, small, big, small, jax.ShapeDtypeStruct((32, 16, LANES), jnp.bfloat16)],
        scratch_shapes=[pltpu.VMEM((8, 4096), jnp.float32)],
        compiler_params=PARAMS,
        cost_estimate=pl.CostEstimate(flops=2 * 4 * 4096 * 40, bytes_accessed=2 << 20, transcendentals=0),
    )(*codes, master, m_codes, jnp.swapaxes(m_scale, 1, 2), v_codes, jnp.swapaxes(v_scale, 1, 2))
    return new_master, m_state, jnp.swapaxes(m_absmax, 1, 2), v_state, jnp.swapaxes(v_absmax, 1, 2), weights


def push_weights(weights):
    plane, group = lax.axis_index("dp") // 16, lax.axis_index("group")
    swapped = lax.all_to_all(
        weights, ("dp", "group"), 0, 0, axis_index_groups=swap_groups(), tiled=True
    )
    upper = jnp.where(plane == group, plane % 2 == 1, plane > group)
    slab = jnp.where(upper, swapped[16:], swapped[:16])
    slab = jnp.transpose(slab.reshape(16, 2, 2, 4, LANES), (2, 0, 3, 1, 4)).reshape(2, 64, 256)
    return lax.all_gather(slab, "group", axis=1, tiled=True)


def on_device(acts, out_grads, master, m_codes, m_scale, v_codes, v_scale):
    me = lax.axis_index("dp").reshape(1).astype(jnp.int32)

    inputs = (me, acts, out_grads)

    def send(codes, pairs):
        return lax.ppermute(codes, "dp", pairs)

    far0, far1 = codes_for((2, 2), *inputs)
    far0, far1 = send(far0, UP), send(far1, DOWN)
    crossed = send(across_first(*inputs), ACROSS)
    down0, up1 = codes_for((3, 1), *inputs)
    down0, up1 = send(down0, DOWN), send(up1, UP)
    up0, down1 = codes_for((1, 3), *inputs, far0, far1)
    up0, down1 = send(up0, UP), send(down1, DOWN)
    steps = along_x(*inputs, crossed)
    acts, _ = lax.optimization_barrier((acts, steps[0]))
    inputs = (me, acts, out_grads)
    steps = [send(steps[0], UP), send(steps[1], TWO), send(steps[2], DOWN)]
    near0, near1, kept = own_codes(*inputs, down0, up0, up1, down1)
    near0, near1 = send(near0, PAIR[0]), send(near1, PAIR[1])
    across, rest = pair_codes(kept, near0, near1)
    across = send(across, ACROSS)
    near0, near1, kept = own_b_codes(*inputs, crossed, *steps)
    near0, near1 = send(near0, PAIR[0]), send(near1, PAIR[1])
    codes = join(rest, across, kept, near0, near1)
    codes = [codes[0]] + [send(codes[k], z_shift(k)) for k in range(1, 4)]
    *state, weights = adam(codes, master, m_codes, m_scale, v_codes, v_scale)
    return (*state, push_weights(weights))


def solution(mesh):
    split = P(None, "dp", "group")
    return jax.shard_map(
        on_device,
        mesh=mesh,
        in_specs=(P(None, "dp", None),) + (split,) * 6,
        out_specs=(split,) * 5 + (P(None, None, "dp"),),
        check_vma=False,
    )
```

time: 104 us -> 97.3 us (0.936)
  waiting for transfers between devices: 39.5 us -> 32.7 us
    ppermute x12 -> x18, waiting for transfers between devices: 33.3 us -> 26.3 us  [send(): return lax.ppermute(codes, 'dp', pairs)]
    ppermute x12 -> x18, starting transfers between devices: 25.5 us -> 28.8 us  [send(): return lax.ppermute(codes, 'dp', pairs)]
    all_to_all x1, starting transfers between devices: 15.1 us -> 12.8 us  [push_weights(): lax.all_to_all(weights, ('dp', 'group'), 0, 0, axis_index_groups=swap_gro...]
    pallas_call x6 -> x9, Pallas kernels: 14.4 us -> 13.5 us  [call(): pl.pallas_call(kernel, in_specs=SPECS[:inputs] + [VMEM] * (len(ins) - inp...]
  transfers between devices with their start and end apart: 13 -> 19, of which waited for: 11 -> 13; matrix products, arithmetic and copies ran while one was open for 0% -> 0% of each run, Pallas kernels for 7% -> 8%
where the time goes in v4:
time: 97.3 us; the launch traced here: 97.1 us
  starting transfers between devices  41.6 us (43%)
  waiting for transfers between devices  32.7 us (34%)
  Pallas kernels  14.6 us (15%)
  blocking collectives  6.49 us (7%)
    ppermute x18, starting transfers between devices, send(): return lax.ppermute(codes, 'dp', pairs)  28.8 us
    ppermute x18, waiting for transfers between devices, send(): return lax.ppermute(codes, 'dp', pairs)  26.3 us
    pallas_call x9, Pallas kernels, call(): pl.pallas_call(kernel, in_specs=SPECS[:inputs] + [VMEM] * (len(ins) - inp...  13.5 us
    all_to_all x1, starting transfers between devices, push_weights(): lax.all_to_all(weights, ('dp', 'group'), 0, 0, axis_index_groups=swap_gro...  12.8 us
    all_gather x1, blocking collectives, push_weights(): return lax.all_gather(slab, 'group', axis=1, tiled=True)  6.49 us
    all_to_all x1, waiting for transfers between devices, push_weights(): lax.all_to_all(weights, ('dp', 'group'), 0, 0, axis_index_groups=swap_gro...  6.45 us
  transfers between devices with their start and end apart: 19, of which 13 were waited for; matrix products, arithmetic and copies ran while one was open for 0% of the time, Pallas kernels for 8%

profile of v4, /device:TPU:1, one launch (start us, length us, event | category | flops | bytes accessed | tf_op | source)
XLA Modules:
  0.0 97.1 jit_solution(6900036325330324577)
XLA Ops:
  0.7 3.4 %shard_map.118 = s16[193,16,128]{2,1,0:T(8,128)(2,1)} custom-call(s32[1]{0:T(128)} %bitcast.me_ref, bf16[2,256,256]{2,1,0:T(8,128)(2,1)} %acts_ref.11, bf16[2,256,4096]{2,1,0:T(8,128)(2,1)} %grads_ref.13), custom_call_target="tpu_custom_call" | custom-call | flops 268435456 | bytes 6291456 | tf_op jit(solution)/shard_map/pallas_call | solution.py:217
  4.0 3.8 %collective-permute-start = (s16[193,16,128]{2,1,0:T(8,128)(2,1)}, s16[193,16,128]{2,1,0:T(8,128)(2,1)S(1)}, u32[]{:S(2)}, u32[]{:S(2)}) collective-permute-start(s16[193,16,128]{2,1,0:T(8,128)(2,1)} %shard_map.118), channel_id=1, source_target_pairs={{0,128},{4,132},{8,136},{12,140},{16,144},{20,148},{24,152},{28,15... | collective-permute-start | bytes 2371592 | tf_op jit(solution)/shard_map/ppermute | solution.py:414
  7.9 1.7 %shard_map.121 = (s16[81,16,128]{2,1,0:T(8,128)(2,1)S(1)}, s16[81,16,128]{2,1,0:T(8,128)(2,1)S(1)}) custom-call(s32[1]{0:T(128)} %bitcast.me_ref, bf16[2,256,256]{2,1,0:T(8,128)(2,1)S(1)} %copy-done.1, bf16[2,256,4096]{2,1,0:T(8,128)(2,1)S(1)} %copy-done), custom_call_target="tpu_custom_call" | custom-call | flops 268435456 | bytes 6291456 | tf_op jit(solution)/shard_map/pallas_call | solution.py:217
  9.6 1.3 %collective-permute-start.2 = (s16[81,16,128]{2,1,0:T(8,128)(2,1)S(1)}, s16[81,16,128]{2,1,0:T(8,128)(2,1)S(1)}, u32[]{:S(2)}, u32[]{:S(2)}) collective-permute-start(s16[81,16,128]{2,1,0:T(8,128)(2,1)S(1)} %get-tuple-element.37), channel_id=1, source_target_pairs={{0,4},{4,8},{8,12},{12,0},{16,20},{20,24},{24,28},{28,16},{32,36},... | collective-permute-start | bytes 995336 | tf_op jit(solution)/shard_map/ppermute | solution.py:414
  10.8 1.5 %collective-permute-start.3 = (s16[81,16,128]{2,1,0:T(8,128)(2,1)S(1)}, s16[81,16,128]{2,1,0:T(8,128)(2,1)S(1)}, u32[]{:S(2)}, u32[]{:S(2)}) collective-permute-start(s16[81,16,128]{2,1,0:T(8,128)(2,1)S(1)} %get-tuple-element.38), channel_id=1, source_target_pairs={{0,12},{4,0},{8,4},{12,8},{16,28},{20,16},{24,20},{28,24},{32,44},... | collective-permute-start | bytes 995336 | tf_op jit(solution)/shard_map/ppermute | solution.py:414
  12.3 1.7 %shard_map.120 = (s16[81,16,128]{2,1,0:T(8,128)(2,1)S(1)}, s16[81,16,128]{2,1,0:T(8,128)(2,1)S(1)}) custom-call(s32[1]{0:T(128)} %bitcast.me_ref, bf16[2,256,256]{2,1,0:T(8,128)(2,1)S(1)} %copy-done.1, bf16[2,256,4096]{2,1,0:T(8,128)(2,1)S(1)} %copy-done), custom_call_target="tpu_custom_call" | custom-call | flops 268435456 | bytes 6291456 | tf_op jit(solution)/shard_map/pallas_call | solution.py:217
  14.0 1.4 %collective-permute-start.1 = (s16[81,16,128]{2,1,0:T(8,128)(2,1)S(1)}, s16[81,16,128]{2,1,0:T(8,128)(2,1)S(1)}, u32[]{:S(2)}, u32[]{:S(2)}) collective-permute-start(s16[81,16,128]{2,1,0:T(8,128)(2,1)S(1)} %get-tuple-element.36), channel_id=1, source_target_pairs={{0,12},{4,0},{8,4},{12,8},{16,28},{20,16},{24,20},{28,24},{32,44},... | collective-permute-start | bytes 995336 | tf_op jit(solution)/shard_map/ppermute | solution.py:414
  15.3 0.2 collective-permute-start.5
  15.5 3.6 %collective-permute-done.2.rest_0_ = s16[81,16,128]{2,1,0:T(8,128)(2,1)S(1)} collective-permute-done((s16[81,16,128]{2,1,0:T(8,128)(2,1)S(1)}, s16[81,16,128]{2,1,0:T(8,128)(2,1)S(1)}, u32[]{:S(2)}, u32[]{:S(2)}) %collective-permute-start.2) | collective-permute-done | bytes 331808 | tf_op jit(solution)/shard_map/ppermute | solution.py:414
  19.2 1.7 %shard_map.122 = (s16[81,16,128]{2,1,0:T(8,128)(2,1)S(1)}, s16[81,16,128]{2,1,0:T(8,128)(2,1)S(1)}) custom-call(s32[1]{0:T(128)} %bitcast.me_ref, bf16[2,256,256]{2,1,0:T(8,128)(2,1)S(1)} %copy-done.1, bf16[2,256,4096]{2,1,0:T(8,128)(2,1)S(1)} %copy-done, s16[81,16,128]{2,1,0:T(8,128)(2,1)S(1)} %collective-permute-done.2.rest_0_, ...), custom_call_target="tpu_custom_call" | custom-call | flops 268435456 | bytes 6291456 | tf_op jit(solution)/shard_map/pallas_call | solution.py:217
  20.9 1.0 %collective-permute-start.4 = (s16[81,16,128]{2,1,0:T(8,128)(2,1)S(1)}, s16[81,16,128]{2,1,0:T(8,128)(2,1)S(1)}, u32[]{:S(2)}, u32[]{:S(2)}) collective-permute-start(s16[81,16,128]{2,1,0:T(8,128)(2,1)S(1)} %get-tuple-element.39), channel_id=1, source_target_pairs={{0,4},{4,8},{8,12},{12,0},{16,20},{20,24},{24,28},{28,16},{32,36},... | collective-permute-start | bytes 995336 | tf_op jit(solution)/shard_map/ppermute | solution.py:414
  21.9 1.8 %collective-permute-start.6 = (s16[81,16,128]{2,1,0:T(8,128)(2,1)S(1)}, s16[81,16,128]{2,1,0:T(8,128)(2,1)S(1)}, u32[]{:S(2)}, u32[]{:S(2)}) collective-permute-start(s16[81,16,128]{2,1,0:T(8,128)(2,1)S(1)} %get-tuple-element.41), channel_id=1, source_target_pairs={{0,12},{4,0},{8,4},{12,8},{16,28},{20,16},{24,20},{28,24},{32,44},... | collective-permute-start | bytes 995336 | tf_op jit(solution)/shard_map/ppermute | solution.py:414
  23.6 0.8 collective-permute-done.got
  24.5 1.5 %shard_map.119 = (s16[49,16,128]{2,1,0:T(8,128)(2,1)S(1)}, s16[49,16,128]{2,1,0:T(8,128)(2,1)S(1)}, s16[49,16,128]{2,1,0:T(8,128)(2,1)S(1)}) custom-call(s32[1]{0:T(128)} %bitcast.me_ref, bf16[2,256,256]{2,1,0:T(8,128)(2,1)S(1)} %copy-done.1, bf16[2,256,4096]{2,1,0:T(8,128)(2,1)S(1)} %copy-done, s16[193,16,128]{2,1,0:T(8,128)(2,1)S(1)} %collective-permute-done.got), custom_call_target="tpu_custom_call" | custom-call | flops 268435456 | bytes 6291456 | tf_op jit(solution)/shard_map/pallas_call | solution.py:217
  25.9 0.1 collective-permute-done.1.a0
  26.0 0.4 collective-permute-done.5.a1
  26.4 7.1 %collective-permute-done.4.b0 = s16[81,16,128]{2,1,0:T(8,128)(2,1)S(1)} collective-permute-done((s16[81,16,128]{2,1,0:T(8,128)(2,1)S(1)}, s16[81,16,128]{2,1,0:T(8,128)(2,1)S(1)}, u32[]{:S(2)}, u32[]{:S(2)}) %collective-permute-start.4) | collective-permute-done | bytes 331808 | tf_op jit(solution)/shard_map/ppermute | solution.py:414
  33.5 1.7 %shard_map.123 = (s16[41,16,128]{2,1,0:T(8,128)(2,1)S(1)}, s16[41,16,128]{2,1,0:T(8,128)(2,1)S(1)}, f32[2,32,2560]{2,1,0:T(8,128)S(1)}) custom-call(s32[1]{0:T(128)} %bitcast.me_ref, bf16[2,256,256]{2,1,0:T(8,128)(2,1)S(1)} %copy-done.1, bf16[2,256,4096]{2,1,0:T(8,128)(2,1)S(1)} %copy-done, s16[81,16,128]{2,1,0:T(8,128)(2,1)S(1)} %collective-permute-done.1.a0, ...), custom_call_target="tpu_custom_call" | custom-call | flops 268435456 | bytes 6291456 | tf_op jit(solution)/shard_map/pallas_call | solution.py:217
  35.2 0.0 copy-start.2
  35.3 0.0 copy-start.3
  35.3 0.0 copy-start.4
  35.3 1.7 %collective-permute-start.7 = (s16[41,16,128]{2,1,0:T(8,128)(2,1)S(1)}, s16[41,16,128]{2,1,0:T(8,128)(2,1)S(1)}, u32[]{:S(2)}, u32[]{:S(2)}) collective-permute-start(s16[41,16,128]{2,1,0:T(8,128)(2,1)S(1)} %get-tuple-element.43), channel_id=1, source_target_pairs={{0,16},{4,20},{8,24},{12,28},{16,0},{20,4},{24,8},{28,12},{32,48},... | collective-permute-start | bytes 503816 | tf_op jit(solution)/shard_map/ppermute | solution.py:414
  37.0 4.7 %collective-permute-start.8 = (s16[41,16,128]{2,1,0:T(8,128)(2,1)S(1)}, s16[41,16,128]{2,1,0:T(8,128)(2,1)S(1)}, u32[]{:S(2)}, u32[]{:S(2)}) collective-permute-start(s16[41,16,128]{2,1,0:T(8,128)(2,1)S(1)} %get-tuple-element.44), channel_id=1, source_target_pairs={{0,112},{4,116},{8,120},{12,124},{16,32},{20,36},{24,40},{28,44},{... | collective-permute-start | bytes 503816 | tf_op jit(solution)/shard_map/ppermute | solution.py:414
  41.7 2.0 %collective-permute-start.11 = (s16[49,16,128]{2,1,0:T(8,128)(2,1)S(1)}, s16[49,16,128]{2,1,0:T(8,128)(2,1)S(1)}, u32[]{:S(2)}, u32[]{:S(2)}) collective-permute-start(s16[49,16,128]{2,1,0:T(8,128)(2,1)S(1)} %get-tuple-element.47), channel_id=1, source_target_pairs={{0,8},{4,12},{8,0},{12,4},{16,24},{20,28},{24,16},{28,20},{32,40},... | collective-permute-start | bytes 602120 | tf_op jit(solution)/shard_map/ppermute | solution.py:414
  43.7 1.2 %collective-permute-start.12 = (s16[49,16,128]{2,1,0:T(8,128)(2,1)S(1)}, s16[49,16,128]{2,1,0:T(8,128)(2,1)S(1)}, u32[]{:S(2)}, u32[]{:S(2)}) collective-permute-start(s16[49,16,128]{2,1,0:T(8,128)(2,1)S(1)} %get-tuple-element.48), channel_id=1, source_target_pairs={{0,12},{4,0},{8,4},{12,8},{16,28},{20,16},{24,20},{28,24},{32,44},... | collective-permute-start | bytes 602120 | tf_op jit(solution)/shard_map/ppermute | solution.py:414
  44.9 0.3 collective-permute-start.10
  45.2 0.3 shard_map.124
  45.5 0.1 collective-permute-start.9
  45.6 2.2 %collective-permute-done.11.r2 = s16[49,16,128]{2,1,0:T(8,128)(2,1)S(1)} collective-permute-done((s16[49,16,128]{2,1,0:T(8,128)(2,1)S(1)}, s16[49,16,128]{2,1,0:T(8,128)(2,1)S(1)}, u32[]{:S(2)}, u32[]{:S(2)}) %collective-permute-start.11) | collective-permute-done | bytes 200736 | tf_op jit(solution)/shard_map/ppermute | solution.py:414
  47.8 3.9 %collective-permute-done.12.r3 = s16[49,16,128]{2,1,0:T(8,128)(2,1)S(1)} collective-permute-done((s16[49,16,128]{2,1,0:T(8,128)(2,1)S(1)}, s16[49,16,128]{2,1,0:T(8,128)(2,1)S(1)}, u32[]{:S(2)}, u32[]{:S(2)}) %collective-permute-start.12) | collective-permute-done | bytes 200736 | tf_op jit(solution)/shard_map/ppermute | solution.py:414
  51.6 1.9 %collective-permute-done.10.r1 = s16[49,16,128]{2,1,0:T(8,128)(2,1)S(1)} collective-permute-done((s16[49,16,128]{2,1,0:T(8,128)(2,1)S(1)}, s16[49,16,128]{2,1,0:T(8,128)(2,1)S(1)}, u32[]{:S(2)}, u32[]{:S(2)}) %collective-permute-start.10) | collective-permute-done | bytes 200736 | tf_op jit(solution)/shard_map/ppermute | solution.py:414
  53.5 1.3 %shard_map.125 = (s16[13,16,128]{2,1,0:T(8,128)(2,1)S(1)}, s16[13,16,128]{2,1,0:T(8,128)(2,1)S(1)}, f32[2,16,1536]{2,1,0:T(8,128)S(1)}) custom-call(s32[1]{0:T(128)} %bitcast.me_ref, bf16[2,256,256]{2,1,0:T(8,128)(2,1)S(1)} %copy-done.1, bf16[2,256,4096]{2,1,0:T(8,128)(2,1)S(1)} %copy-done, s16[193,16,128]{2,1,0:T(8,128)(2,1)S(1)} %collective-permute-done.got, ...), custom_call_target="tpu_custom_call" | custom-call | flops 268435456 | bytes 6291456 | tf_op jit(solution)/shard_map/pallas_call | solution.py:217
  54.9 0.1 collective-permute-start.13
  55.0 1.4 %collective-permute-start.14 = (s16[13,16,128]{2,1,0:T(8,128)(2,1)S(1)}, s16[13,16,128]{2,1,0:T(8,128)(2,1)S(1)}, u32[]{:S(2)}, u32[]{:S(2)}) collective-permute-start(s16[13,16,128]{2,1,0:T(8,128)(2,1)S(1)} %get-tuple-element.51), channel_id=1, source_target_pairs={{0,112},{4,116},{8,120},{12,124},{16,32},{20,36},{24,40},{28,44},{... | collective-permute-start | bytes 159752 | tf_op jit(solution)/shard_map/ppermute | solution.py:414
  56.4 1.5 %collective-permute-done.13.near0 = s16[13,16,128]{2,1,0:T(8,128)(2,1)S(1)} collective-permute-done((s16[13,16,128]{2,1,0:T(8,128)(2,1)S(1)}, s16[13,16,128]{2,1,0:T(8,128)(2,1)S(1)}, u32[]{:S(2)}, u32[]{:S(2)}) %collective-permute-start.13) | collective-permute-done | bytes 53280 | tf_op jit(solution)/shard_map/ppermute | solution.py:414
  57.9 1.3 %collective-permute-done.14.near1 = s16[13,16,128]{2,1,0:T(8,128)(2,1)S(1)} collective-permute-done((s16[13,16,128]{2,1,0:T(8,128)(2,1)S(1)}, s16[13,16,128]{2,1,0:T(8,128)(2,1)S(1)}, u32[]{:S(2)}, u32[]{:S(2)}) %collective-permute-start.14) | collective-permute-done | bytes 53280 | tf_op jit(solution)/shard_map/ppermute | solution.py:414
  59.3 0.3 shard_map.126
  59.6 0.7 collective-permute-start.15
  60.2 2.2 %collective-permute-start.16 = (s16[17,16,128]{2,1,0:T(8,128)(2,1)S(1)}, s16[17,16,128]{2,1,0:T(8,128)(2,1)S(1)}, u32[]{:S(2)}, u32[]{:S(2)}) collective-permute-start(s16[17,16,128]{2,1,0:T(8,128)(2,1)S(1)} %get-tuple-element.54), channel_id=1, source_target_pairs={{0,64},{4,68},{8,72},{12,76},{16,80},{20,84},{24,88},{28,92},{32,9... | collective-permute-start | bytes 208904 | tf_op jit(solution)/shard_map/ppermute | solution.py:414
  62.5 3.5 %collective-permute-start.17 = (s16[17,16,128]{2,1,0:T(8,128)(2,1)S(1)}, s16[17,16,128]{2,1,0:T(8,128)(2,1)S(1)}, u32[]{:S(2)}, u32[]{:S(2)}) collective-permute-start(s16[17,16,128]{2,1,0:T(8,128)(2,1)S(1)} %get-tuple-element.55), channel_id=1, source_target_pairs={{0,96},{4,100},{8,104},{12,108},{16,112},{20,116},{24,120},{28,124... | collective-permute-start | bytes 208904 | tf_op jit(solution)/shard_map/ppermute | solution.py:414
  66.0 1.4 %collective-permute-done.16.c2 = s16[17,16,128]{2,1,0:T(8,128)(2,1)S(1)} collective-permute-done((s16[17,16,128]{2,1,0:T(8,128)(2,1)S(1)}, s16[17,16,128]{2,1,0:T(8,128)(2,1)S(1)}, u32[]{:S(2)}, u32[]{:S(2)}) %collective-permute-start.16) | collective-permute-done | bytes 69664 | tf_op jit(solution)/shard_map/ppermute | solution.py:414
  67.4 2.0 %collective-permute-done.17.c3 = s16[17,16,128]{2,1,0:T(8,128)(2,1)S(1)} collective-permute-done((s16[17,16,128]{2,1,0:T(8,128)(2,1)S(1)}, s16[17,16,128]{2,1,0:T(8,128)(2,1)S(1)}, u32[]{:S(2)}, u32[]{:S(2)}) %collective-permute-start.17) | collective-permute-done | bytes 69664 | tf_op jit(solution)/shard_map/ppermute | solution.py:414
  69.4 1.1 %shard_map.127 = (f32[2,4,4096]{2,1,0:T(4,128)}, f32[2,4,4096]{2,1,0:T(4,128)}, f32[2,2,4]{2,1,0:T(2,128)}, f32[2,4,4096]{2,1,0:T(4,128)}, f32[2,2,4]{2,1,0:T(2,128)}, /*index=5*/bf16[32,16,128]{2,1,0:T(8,128)(2,1)}) custom-call(s16[17,16,128]{2,1,0:T(8,128)(2,1)S(1)} %get-tuple-element.52.c0, s16[17,16,128]{2,1,0:T(8,128)(2,1)S(1)} %collective-permute-done.15.c1, ...), custom_call_target="tpu_custom_call" | custom-call | flops 1310720 | bytes 2097152 | tf_op jit(solution)/shard_map/pallas_call | solution.py:387
  70.5 12.8 %all-to-all-start = ((bf16[32,16,128]{2,1,0:T(8,128)(2,1)}), bf16[32,16,128]{2,1,0:T(8,128)(2,1)S(1)}, u32[]{:S(2)}, u32[]{:S(2)}) async-start(bf16[32,16,128]{2,1,0:T(8,128)(2,1)} %get-tuple-element.61), calls=%async_computation | async-start | bytes 262144 | tf_op jit(solution)/shard_map/all_to_all | solution.py:399
  83.4 6.5 %all-to-all-done = bf16[32,16,128]{2,1,0:T(8,128)(2,1)S(1)} async-done(((bf16[32,16,128]{2,1,0:T(8,128)(2,1)}), bf16[32,16,128]{2,1,0:T(8,128)(2,1)S(1)}, u32[]{:S(2)}, u32[]{:S(2)}) %all-to-all-start) | async-done | bytes 131104 | tf_op jit(solution)/shard_map/all_to_all | solution.py:399
  89.8 0.1 copy.13
  89.9 6.5 %all_gather.3 = bf16[2,256,256]{2,1,0:T(8,128)(2,1)S(1)} all-gather(bf16[2,64,256]{2,1,0:T(8,128)(2,1)S(1)} %reshape.23), channel_id=1, replica_groups=mesh['dp'=64,'group'=4] {'group'}, dimensions={1}, use_global_device_ids=true | all-gather | bytes 327680 | tf_op jit(solution)/shard_map/all_gather | solution.py:405
  96.4 0.7 copy.15
  (19 shorter events, 0.1 us)
Async XLA Ops:
  0.6 7.2 %copy-start.1 = (bf16[2,256,256]{2,1,0:T(8,128)(2,1)S(1)}, bf16[2,256,256]{2,1,0:T(8,128)(2,1)}, u32[]{:S(2)}) copy-start(bf16[2,256,256]{2,1,0:T(8,128)(2,1)} %acts_ref.11) | copy-start | bytes 786436
  0.6 7.2 %copy-start = (bf16[2,256,4096]{2,1,0:T(8,128)(2,1)S(1)}, bf16[2,256,4096]{2,1,0:T(8,128)(2,1)}, u32[]{:S(2)}) copy-start(bf16[2,256,4096]{2,1,0:T(8,128)(2,1)} %grads_ref.13) | copy-start | bytes 12582916
  4.0 20.4 %collective-permute-start = (s16[193,16,128]{2,1,0:T(8,128)(2,1)}, s16[193,16,128]{2,1,0:T(8,128)(2,1)S(1)}, u32[]{:S(2)}, u32[]{:S(2)}) collective-permute-start(s16[193,16,128]{2,1,0:T(8,128)(2,1)} %shard_map.118), channel_id=1, source_target_pairs={{0,128},{4,132},{8,136},{12,140},{16,144},{20,148},{24,152},{28,15... | collective-permute-start | bytes 2371592 | tf_op jit(solution)/shard_map/ppermute | solution.py:414
  9.6 9.6 %collective-permute-start.2 = (s16[81,16,128]{2,1,0:T(8,128)(2,1)S(1)}, s16[81,16,128]{2,1,0:T(8,128)(2,1)S(1)}, u32[]{:S(2)}, u32[]{:S(2)}) collective-permute-start(s16[81,16,128]{2,1,0:T(8,128)(2,1)S(1)} %get-tuple-element.37), channel_id=1, source_target_pairs={{0,4},{4,8},{8,12},{12,0},{16,20},{20,24},{24,28},{28,16},{32,36},... | collective-permute-start | bytes 995336 | tf_op jit(solution)/shard_map/ppermute | solution.py:414
  10.8 8.3 %collective-permute-start.3 = (s16[81,16,128]{2,1,0:T(8,128)(2,1)S(1)}, s16[81,16,128]{2,1,0:T(8,128)(2,1)S(1)}, u32[]{:S(2)}, u32[]{:S(2)}) collective-permute-start(s16[81,16,128]{2,1,0:T(8,128)(2,1)S(1)} %get-tuple-element.38), channel_id=1, source_target_pairs={{0,12},{4,0},{8,4},{12,8},{16,28},{20,16},{24,20},{28,24},{32,44},... | collective-permute-start | bytes 995336 | tf_op jit(solution)/shard_map/ppermute | solution.py:414
  14.0 12.0 %collective-permute-start.1 = (s16[81,16,128]{2,1,0:T(8,128)(2,1)S(1)}, s16[81,16,128]{2,1,0:T(8,128)(2,1)S(1)}, u32[]{:S(2)}, u32[]{:S(2)}) collective-permute-start(s16[81,16,128]{2,1,0:T(8,128)(2,1)S(1)} %get-tuple-element.36), channel_id=1, source_target_pairs={{0,12},{4,0},{8,4},{12,8},{16,28},{20,16},{24,20},{28,24},{32,44},... | collective-permute-start | bytes 995336 | tf_op jit(solution)/shard_map/ppermute | solution.py:414
  15.3 11.1 %collective-permute-start.5 = (s16[81,16,128]{2,1,0:T(8,128)(2,1)S(1)}, s16[81,16,128]{2,1,0:T(8,128)(2,1)S(1)}, u32[]{:S(2)}, u32[]{:S(2)}) collective-permute-start(s16[81,16,128]{2,1,0:T(8,128)(2,1)S(1)} %get-tuple-element.40), channel_id=1, source_target_pairs={{0,4},{4,8},{8,12},{12,0},{16,20},{20,24},{24,28},{28,16},{32,36},... | collective-permute-start | bytes 995336 | tf_op jit(solution)/shard_map/ppermute | solution.py:414
  20.9 12.7 %collective-permute-start.4 = (s16[81,16,128]{2,1,0:T(8,128)(2,1)S(1)}, s16[81,16,128]{2,1,0:T(8,128)(2,1)S(1)}, u32[]{:S(2)}, u32[]{:S(2)}) collective-permute-start(s16[81,16,128]{2,1,0:T(8,128)(2,1)S(1)} %get-tuple-element.39), channel_id=1, source_target_pairs={{0,4},{4,8},{8,12},{12,0},{16,20},{20,24},{24,28},{28,16},{32,36},... | collective-permute-start | bytes 995336 | tf_op jit(solution)/shard_map/ppermute | solution.py:414
  21.9 11.7 %collective-permute-start.6 = (s16[81,16,128]{2,1,0:T(8,128)(2,1)S(1)}, s16[81,16,128]{2,1,0:T(8,128)(2,1)S(1)}, u32[]{:S(2)}, u32[]{:S(2)}) collective-permute-start(s16[81,16,128]{2,1,0:T(8,128)(2,1)S(1)} %get-tuple-element.41), channel_id=1, source_target_pairs={{0,12},{4,0},{8,4},{12,8},{16,28},{20,16},{24,20},{28,24},{32,44},... | collective-permute-start | bytes 995336 | tf_op jit(solution)/shard_map/ppermute | solution.py:414
  35.2 34.1 %copy-start.2 = (f32[2,4,4096]{2,1,0:T(4,128)S(1)}, f32[2,4,4096]{2,1,0:T(4,128)}, u32[]{:S(2)}) copy-start(f32[2,4,4096]{2,1,0:T(4,128)} %master.1) | copy-start | bytes 393220
  35.3 34.1 %copy-start.3 = (s32[2,4,4096]{2,1,0:T(4,128)S(1)}, s32[2,4,4096]{2,1,0:T(4,128)}, u32[]{:S(2)}) copy-start(s32[2,4,4096]{2,1,0:T(4,128)} %m_codes.1) | copy-start | bytes 393220
  35.3 34.1 %copy-start.4 = (s32[2,4,4096]{2,1,0:T(4,128)S(1)}, s32[2,4,4096]{2,1,0:T(4,128)}, u32[]{:S(2)}) copy-start(s32[2,4,4096]{2,1,0:T(4,128)} %v_codes.1) | copy-start | bytes 393220
  35.3 34.1 %copy-start.5 = (f32[2,4,2]{1,2,0:T(2,128)S(1)}, f32[2,4,2]{1,2,0:T(2,128)}, u32[]{:S(2)}) copy-start(f32[2,4,2]{1,2,0:T(2,128)} %param.11) | copy-start | bytes 196
  35.3 34.1 %copy-start.6 = (f32[2,4,2]{1,2,0:T(2,128)S(1)}, f32[2,4,2]{1,2,0:T(2,128)}, u32[]{:S(2)}) copy-start(f32[2,4,2]{1,2,0:T(2,128)} %param.13) | copy-start | bytes 196
  35.3 9.9 %collective-permute-start.7 = (s16[41,16,128]{2,1,0:T(8,128)(2,1)S(1)}, s16[41,16,128]{2,1,0:T(8,128)(2,1)S(1)}, u32[]{:S(2)}, u32[]{:S(2)}) collective-permute-start(s16[41,16,128]{2,1,0:T(8,128)(2,1)S(1)} %get-tuple-element.43), channel_id=1, source_target_pairs={{0,16},{4,20},{8,24},{12,28},{16,0},{20,4},{24,8},{28,12},{32,48},... | collective-permute-start | bytes 503816 | tf_op jit(solution)/shard_map/ppermute | solution.py:414
  37.0 8.2 %collective-permute-start.8 = (s16[41,16,128]{2,1,0:T(8,128)(2,1)S(1)}, s16[41,16,128]{2,1,0:T(8,128)(2,1)S(1)}, u32[]{:S(2)}, u32[]{:S(2)}) collective-permute-start(s16[41,16,128]{2,1,0:T(8,128)(2,1)S(1)} %get-tuple-element.44), channel_id=1, source_target_pairs={{0,112},{4,116},{8,120},{12,124},{16,32},{20,36},{24,40},{28,44},{... | collective-permute-start | bytes 503816 | tf_op jit(solution)/shard_map/ppermute | solution.py:414
  41.7 6.1 %collective-permute-start.11 = (s16[49,16,128]{2,1,0:T(8,128)(2,1)S(1)}, s16[49,16,128]{2,1,0:T(8,128)(2,1)S(1)}, u32[]{:S(2)}, u32[]{:S(2)}) collective-permute-start(s16[49,16,128]{2,1,0:T(8,128)(2,1)S(1)} %get-tuple-element.47), channel_id=1, source_target_pairs={{0,8},{4,12},{8,0},{12,4},{16,24},{20,28},{24,16},{28,20},{32,40},... | collective-permute-start | bytes 602120 | tf_op jit(solution)/shard_map/ppermute | solution.py:414
  43.7 7.9 %collective-permute-start.12 = (s16[49,16,128]{2,1,0:T(8,128)(2,1)S(1)}, s16[49,16,128]{2,1,0:T(8,128)(2,1)S(1)}, u32[]{:S(2)}, u32[]{:S(2)}) collective-permute-start(s16[49,16,128]{2,1,0:T(8,128)(2,1)S(1)} %get-tuple-element.48), channel_id=1, source_target_pairs={{0,12},{4,0},{8,4},{12,8},{16,28},{20,16},{24,20},{28,24},{32,44},... | collective-permute-start | bytes 602120 | tf_op jit(solution)/shard_map/ppermute | solution.py:414
  44.9 8.7 %collective-permute-start.10 = (s16[49,16,128]{2,1,0:T(8,128)(2,1)S(1)}, s16[49,16,128]{2,1,0:T(8,128)(2,1)S(1)}, u32[]{:S(2)}, u32[]{:S(2)}) collective-permute-start(s16[49,16,128]{2,1,0:T(8,128)(2,1)S(1)} %get-tuple-element.34), channel_id=1, source_target_pairs={{0,4},{4,8},{8,12},{12,0},{16,20},{20,24},{24,28},{28,16},{32,36},... | collective-permute-start | bytes 602120 | tf_op jit(solution)/shard_map/ppermute | solution.py:414
  45.5 13.8 %collective-permute-start.9 = (s16[41,16,128]{2,1,0:T(8,128)(2,1)S(1)}, s16[41,16,128]{2,1,0:T(8,128)(2,1)S(1)}, u32[]{:S(2)}, u32[]{:S(2)}) collective-permute-start(s16[41,16,128]{2,1,0:T(8,128)(2,1)S(1)} %get-tuple-element.46), channel_id=1, source_target_pairs={{0,128},{4,132},{8,136},{12,140},{16,144},{20,148},{24,152},{28,15... | collective-permute-start | bytes 503816 | tf_op jit(solution)/shard_map/ppermute | solution.py:414
  54.9 3.1 %collective-permute-start.13 = (s16[13,16,128]{2,1,0:T(8,128)(2,1)S(1)}, s16[13,16,128]{2,1,0:T(8,128)(2,1)S(1)}, u32[]{:S(2)}, u32[]{:S(2)}) collective-permute-start(s16[13,16,128]{2,1,0:T(8,128)(2,1)S(1)} %get-tuple-element.50), channel_id=1, source_target_pairs={{0,16},{4,20},{8,24},{12,28},{16,0},{20,4},{24,8},{28,12},{32,48},... | collective-permute-start | bytes 159752 | tf_op jit(solution)/shard_map/ppermute | solution.py:414
  55.0 4.3 %collective-permute-start.14 = (s16[13,16,128]{2,1,0:T(8,128)(2,1)S(1)}, s16[13,16,128]{2,1,0:T(8,128)(2,1)S(1)}, u32[]{:S(2)}, u32[]{:S(2)}) collective-permute-start(s16[13,16,128]{2,1,0:T(8,128)(2,1)S(1)} %get-tuple-element.51), channel_id=1, source_target_pairs={{0,112},{4,116},{8,120},{12,124},{16,32},{20,36},{24,40},{28,44},{... | collective-permute-start | bytes 159752 | tf_op jit(solution)/shard_map/ppermute | solution.py:414
  59.6 6.4 %collective-permute-start.15 = (s16[17,16,128]{2,1,0:T(8,128)(2,1)S(1)}, s16[17,16,128]{2,1,0:T(8,128)(2,1)S(1)}, u32[]{:S(2)}, u32[]{:S(2)}) collective-permute-start(s16[17,16,128]{2,1,0:T(8,128)(2,1)S(1)} %get-tuple-element.53), channel_id=1, source_target_pairs={{0,32},{4,36},{8,40},{12,44},{16,48},{20,52},{24,56},{28,60},{32,6... | collective-permute-start | bytes 208904 | tf_op jit(solution)/shard_map/ppermute | solution.py:414
  60.2 7.1 %collective-permute-start.16 = (s16[17,16,128]{2,1,0:T(8,128)(2,1)S(1)}, s16[17,16,128]{2,1,0:T(8,128)(2,1)S(1)}, u32[]{:S(2)}, u32[]{:S(2)}) collective-permute-start(s16[17,16,128]{2,1,0:T(8,128)(2,1)S(1)} %get-tuple-element.54), channel_id=1, source_target_pairs={{0,64},{4,68},{8,72},{12,76},{16,80},{20,84},{24,88},{28,92},{32,9... | collective-permute-start | bytes 208904 | tf_op jit(solution)/shard_map/ppermute | solution.py:414
  62.5 6.9 %collective-permute-start.17 = (s16[17,16,128]{2,1,0:T(8,128)(2,1)S(1)}, s16[17,16,128]{2,1,0:T(8,128)(2,1)S(1)}, u32[]{:S(2)}, u32[]{:S(2)}) collective-permute-start(s16[17,16,128]{2,1,0:T(8,128)(2,1)S(1)} %get-tuple-element.55), channel_id=1, source_target_pairs={{0,96},{4,100},{8,104},{12,108},{16,112},{20,116},{24,120},{28,124... | collective-permute-start | bytes 208904 | tf_op jit(solution)/shard_map/ppermute | solution.py:414
  70.5 19.3 %all-to-all-start = ((bf16[32,16,128]{2,1,0:T(8,128)(2,1)}), bf16[32,16,128]{2,1,0:T(8,128)(2,1)S(1)}, u32[]{:S(2)}, u32[]{:S(2)}) async-start(bf16[32,16,128]{2,1,0:T(8,128)(2,1)} %get-tuple-element.61), calls=%async_computation | async-start | bytes 262144 | tf_op jit(solution)/shard_map/all_to_all | solution.py:399

commit v5 on v4

--- a/solution.py
+++ b/solution.py
@@ -96,9 +96,11 @@
     return rows
 
 
-def rows_b(first_step, here_y):
+def rows_b(first_step, here_y, here_z=None):
     def rows(expert, place, new):
-        i, k, here_z, step = new & 3, (new >> 2) & 3, (new >> 4) & 1, new >> 5
+        i, k, step = new & 3, (new >> 2) & 3, new >> 4
+        if here_z is None:
+            return old_row(expert, place, here_y, step >> 2, k, place[2] + (step & 3), i)
         return old_row(expert, place, here_y, here_z, k, place[2] + first_step + step, i)
 
     return rows
@@ -276,31 +278,39 @@
     return call(across_first_kernel, codes_of(16, PART_B), scratch(PART_B, 128), ins, FIRST_PARAMS)
 
 
-def along_x_kernel(me_ref, acts_ref, grads_ref, got, out1, out2, out3, *work):
-    received = [[(got, e * 8 + 2)] for e in range(2)]
-    tops = add_up(PART_B, rows_b(1, 1), me_ref, acts_ref, grads_ref, received, *work)
+def near_kernel(me_ref, acts_ref, grads_ref, got, out0, out1, *work):
+    received = [[(got, e * 8)] for e in range(2)]
+    tops = add_up(PART_B, rows_b(0, 1, 0), me_ref, acts_ref, grads_ref, received, *work)
+    for e, out in enumerate((out0, out1)):
+        write_groups(out, [(work[2].at[e], g, tops[e][g]) for g in range(4)])
+
+
+def near_codes(*ins):
+    return call(near_kernel, [codes_of(4, PART_B)] * 2, scratch(PART_B, 64), ins)
+
+
+def along_x_kernel(me_ref, acts_ref, grads_ref, got, near0, near1, out1, out2, out3, *work):
+    received = [[(got, e * 8 + 5), ((near0, near1)[e], 1)] for e in range(2)]
+    tops = add_up(PART_B, rows_b(1, 1, 1), me_ref, acts_ref, grads_ref, received, *work)
     for k, out in enumerate((out1, out2, out3)):
-        write_groups(out, [(work[2].at[e], g, tops[e][g]) for e in range(2) for g in (2 * k, 2 * k + 1)])
+        write_groups(out, [(work[2].at[e], k, tops[e][k]) for e in range(2)])
 
 
 def along_x(*ins):
-    return call(along_x_kernel, [codes_of(4, PART_B)] * 3, scratch(PART_B, 96), ins)
-
-
-def own_b_kernel(me_ref, acts_ref, grads_ref, got, r1, r2, r3, out0, out1, kept, *work):
-    received = [[(got, e * 8)] + [(r, e * 2) for r in (r1, r2, r3)] for e in range(2)]
-    tops = add_up(PART_B, rows_b(0, 1), me_ref, acts_ref, grads_ref, received, *work)
-    sums = work[2]
-    for e, out in enumerate((out0, out1)):
-        write_groups(out, [(sums.at[e], 0, tops[e][0])])
-        kept[e] = sums[e, 16:]
-
-
-def own_b_codes(*ins):
-    return call(own_b_kernel, [codes_of(1, PART_B)] * 2 + [sums_of(16, PART_B)], scratch(PART_B, 32), ins)
-
-
-def join_kernel(rest, got, kept, near0, near1, *refs):
+    return call(along_x_kernel, [codes_of(2, PART_B)] * 3, scratch(PART_B, 48), ins)
+
+
+def own_b_kernel(me_ref, acts_ref, grads_ref, got, near0, near1, r1, r2, r3, out, *work):
+    received = [[(got, e * 8 + 4), ((near0, near1)[e], 0)] + [(r, e) for r in (r1, r2, r3)] for e in range(2)]
+    add_up(PART_B, rows_b(0, 1, 1), me_ref, acts_ref, grads_ref, received, *work)
+    out[...] = work[2][...]
+
+
+def own_b(*ins):
+    return call(own_b_kernel, sums_of(16, PART_B), scratch(PART_B, 16), ins)
+
+
+def join_kernel(rest, got, own, *refs):
     *outs, sums = refs
     tiles = PART_A[1] // LANES
     note = decoded(got[2 * tiles])
@@ -309,11 +319,7 @@
         for t in range(tiles):
             cols = slice(t * LANES, (t + 1) * LANES)
             sums[e, :, cols] = rest[e, :, cols] + decoded(got[e * tiles + t]) * scale
-        near = (near0, near1)[e]
-        scale = step_of(decoded(near[near.shape[0] - 1])[:, :1])
-        for t in range(PART_B[1] // LANES):
-            at = PART_B[0] + t * LANES
-            sums[e, :, at : at + LANES] = kept[e, :, t * LANES : (t + 1) * LANES] + decoded(near[t]) * scale
+        sums[e, :, PART_B[0] :] = own[e]
     upper = lax.broadcasted_iota(jnp.int32, (8, 1), 0) < 4
     for pair in range(2):
         tile = slice(pair * 8, pair * 8 + 8)
@@ -420,17 +426,19 @@
     down0, up1 = send(down0, DOWN), send(up1, UP)
     up0, down1 = codes_for((1, 3), *inputs, far0, far1)
     up0, down1 = send(up0, UP), send(down1, DOWN)
-    steps = along_x(*inputs, crossed)
-    acts, _ = lax.optimization_barrier((acts, steps[0]))
+    there0, there1 = near_codes(*inputs, crossed)
+    acts, _ = lax.optimization_barrier((acts, there0))
+    there0, there1 = send(there0, PAIR[0]), send(there1, PAIR[1])
     inputs = (me, acts, out_grads)
-    steps = [send(steps[0], UP), send(steps[1], TWO), send(steps[2], DOWN)]
     near0, near1, kept = own_codes(*inputs, down0, up0, up1, down1)
     near0, near1 = send(near0, PAIR[0]), send(near1, PAIR[1])
+    steps = along_x(*inputs, crossed, there0, there1)
+    kept, _ = lax.optimization_barrier((kept, steps[0]))
+    steps = [send(steps[0], UP), send(steps[1], TWO), send(steps[2], DOWN)]
     across, rest = pair_codes(kept, near0, near1)
     across = send(across, ACROSS)
-    near0, near1, kept = own_b_codes(*inputs, crossed, *steps)
-    near0, near1 = send(near0, PAIR[0]), send(near1, PAIR[1])
-    codes = join(rest, across, kept, near0, near1)
+    own = own_b(*inputs, crossed, there0, there1, *steps)
+    codes = join(rest, across, own)
     codes = [codes[0]] + [send(codes[k], z_shift(k)) for k in range(1, 4)]
     *state, weights = adam(codes, master, m_codes, m_scale, v_codes, v_scale)
     return (*state, push_weights(weights))

time: 97.3 us -> 94.3 us (0.969)
  waiting for transfers between devices: 32.7 us -> 20.4 us
  starting transfers between devices: 41.6 us -> 48.9 us
  Pallas kernels: 14.6 us -> 15.8 us
    ppermute x18, waiting for transfers between devices: 26.3 us -> 14.1 us  [send(): return lax.ppermute(codes, 'dp', pairs)]
    ppermute x18, starting transfers between devices: 28.8 us -> 33.8 us  [send(): return lax.ppermute(codes, 'dp', pairs)]
    all_to_all x1, starting transfers between devices: 12.8 us -> 15.1 us  [push_weights(): lax.all_to_all(weights, ('dp', 'group'), 0, 0, axis_index_groups=swap_gro...]
    pallas_call x9 -> x10, Pallas kernels: 13.5 us -> 14.6 us  [call(): pl.pallas_call(kernel, in_specs=SPECS[:inputs] + [VMEM] * (len(ins) - inp...]
  transfers between devices with their start and end apart: 19 -> 19, of which waited for: 13 -> 12; matrix products, arithmetic and copies ran while one was open for 0% -> 0% of each run, Pallas kernels for 8% -> 11%
where the time goes in v5:
time: 94.3 us; the launch traced here: 94.1 us
  starting transfers between devices  48.9 us (52%)
  waiting for transfers between devices  20.4 us (22%)
  Pallas kernels  15.8 us (17%)
  blocking collectives  7.29 us (8%)
    ppermute x18, starting transfers between devices, send(): return lax.ppermute(codes, 'dp', pairs)  33.8 us
    all_to_all x1, starting transfers between devices, push_weights(): lax.all_to_all(weights, ('dp', 'group'), 0, 0, axis_index_groups=swap_gro...  15.1 us
    pallas_call x10, Pallas kernels, call(): pl.pallas_call(kernel, in_specs=SPECS[:inputs] + [VMEM] * (len(ins) - inp...  14.6 us
    ppermute x18, waiting for transfers between devices, send(): return lax.ppermute(codes, 'dp', pairs)  14.1 us
    all_gather x1, blocking collectives, push_weights(): return lax.all_gather(slab, 'group', axis=1, tiled=True)  7.29 us
    all_to_all x1, waiting for transfers between devices, push_weights(): lax.all_to_all(weights, ('dp', 'group'), 0, 0, axis_index_groups=swap_gro...  6.31 us
  transfers between devices with their start and end apart: 19, of which 12 were waited for; matrix products, arithmetic and copies ran while one was open for 0% of the time, Pallas kernels for 11%

profile of v5, /device:TPU:1, one launch (start us, length us, event | category | flops | bytes accessed | tf_op | source)
XLA Modules:
  0.0 94.1 jit_solution(4786895368590587063)
XLA Ops:
  0.7 3.4 %shard_map.118 = s16[193,16,128]{2,1,0:T(8,128)(2,1)} custom-call(s32[1]{0:T(128)} %bitcast.me_ref, bf16[2,256,256]{2,1,0:T(8,128)(2,1)} %acts_ref.12, bf16[2,256,4096]{2,1,0:T(8,128)(2,1)} %grads_ref.15), custom_call_target="tpu_custom_call" | custom-call | flops 268435456 | bytes 6291456 | tf_op jit(solution)/shard_map/pallas_call | solution.py:219
  4.0 3.8 %collective-permute-start = (s16[193,16,128]{2,1,0:T(8,128)(2,1)}, s16[193,16,128]{2,1,0:T(8,128)(2,1)S(1)}, u32[]{:S(2)}, u32[]{:S(2)}) collective-permute-start(s16[193,16,128]{2,1,0:T(8,128)(2,1)} %shard_map.118), channel_id=1, source_target_pairs={{0,128},{4,132},{8,136},{12,140},{16,144},{20,148},{24,152},{28,15... | collective-permute-start | bytes 2371592 | tf_op jit(solution)/shard_map/ppermute | solution.py:420
  7.9 1.7 %shard_map.121 = (s16[81,16,128]{2,1,0:T(8,128)(2,1)S(1)}, s16[81,16,128]{2,1,0:T(8,128)(2,1)S(1)}) custom-call(s32[1]{0:T(128)} %bitcast.me_ref, bf16[2,256,256]{2,1,0:T(8,128)(2,1)S(1)} %copy-done.1, bf16[2,256,4096]{2,1,0:T(8,128)(2,1)S(1)} %copy-done), custom_call_target="tpu_custom_call" | custom-call | flops 268435456 | bytes 6291456 | tf_op jit(solution)/shard_map/pallas_call | solution.py:219
  9.5 1.3 %collective-permute-start.2 = (s16[81,16,128]{2,1,0:T(8,128)(2,1)S(1)}, s16[81,16,128]{2,1,0:T(8,128)(2,1)S(1)}, u32[]{:S(2)}, u32[]{:S(2)}) collective-permute-start(s16[81,16,128]{2,1,0:T(8,128)(2,1)S(1)} %get-tuple-element.37), channel_id=1, source_target_pairs={{0,4},{4,8},{8,12},{12,0},{16,20},{20,24},{24,28},{28,16},{32,36},... | collective-permute-start | bytes 995336 | tf_op jit(solution)/shard_map/ppermute | solution.py:420
  10.8 1.5 %collective-permute-start.3 = (s16[81,16,128]{2,1,0:T(8,128)(2,1)S(1)}, s16[81,16,128]{2,1,0:T(8,128)(2,1)S(1)}, u32[]{:S(2)}, u32[]{:S(2)}) collective-permute-start(s16[81,16,128]{2,1,0:T(8,128)(2,1)S(1)} %get-tuple-element.38), channel_id=1, source_target_pairs={{0,12},{4,0},{8,4},{12,8},{16,28},{20,16},{24,20},{28,24},{32,44},... | collective-permute-start | bytes 995336 | tf_op jit(solution)/shard_map/ppermute | solution.py:420
  12.3 1.7 %shard_map.120 = (s16[81,16,128]{2,1,0:T(8,128)(2,1)S(1)}, s16[81,16,128]{2,1,0:T(8,128)(2,1)S(1)}) custom-call(s32[1]{0:T(128)} %bitcast.me_ref, bf16[2,256,256]{2,1,0:T(8,128)(2,1)S(1)} %copy-done.1, bf16[2,256,4096]{2,1,0:T(8,128)(2,1)S(1)} %copy-done), custom_call_target="tpu_custom_call" | custom-call | flops 268435456 | bytes 6291456 | tf_op jit(solution)/shard_map/pallas_call | solution.py:219
  14.0 1.4 %collective-permute-start.1 = (s16[81,16,128]{2,1,0:T(8,128)(2,1)S(1)}, s16[81,16,128]{2,1,0:T(8,128)(2,1)S(1)}, u32[]{:S(2)}, u32[]{:S(2)}) collective-permute-start(s16[81,16,128]{2,1,0:T(8,128)(2,1)S(1)} %get-tuple-element.36), channel_id=1, source_target_pairs={{0,12},{4,0},{8,4},{12,8},{16,28},{20,16},{24,20},{28,24},{32,44},... | collective-permute-start | bytes 995336 | tf_op jit(solution)/shard_map/ppermute | solution.py:420
  15.3 0.2 collective-permute-start.5
  15.5 3.6 %collective-permute-done.2.rest_0_ = s16[81,16,128]{2,1,0:T(8,128)(2,1)S(1)} collective-permute-done((s16[81,16,128]{2,1,0:T(8,128)(2,1)S(1)}, s16[81,16,128]{2,1,0:T(8,128)(2,1)S(1)}, u32[]{:S(2)}, u32[]{:S(2)}) %collective-permute-start.2) | collective-permute-done | bytes 331808 | tf_op jit(solution)/shard_map/ppermute | solution.py:420
  19.2 1.7 %shard_map.122 = (s16[81,16,128]{2,1,0:T(8,128)(2,1)S(1)}, s16[81,16,128]{2,1,0:T(8,128)(2,1)S(1)}) custom-call(s32[1]{0:T(128)} %bitcast.me_ref, bf16[2,256,256]{2,1,0:T(8,128)(2,1)S(1)} %copy-done.1, bf16[2,256,4096]{2,1,0:T(8,128)(2,1)S(1)} %copy-done, s16[81,16,128]{2,1,0:T(8,128)(2,1)S(1)} %collective-permute-done.2.rest_0_, ...), custom_call_target="tpu_custom_call" | custom-call | flops 268435456 | bytes 6291456 | tf_op jit(solution)/shard_map/pallas_call | solution.py:219
  20.9 1.0 %collective-permute-start.4 = (s16[81,16,128]{2,1,0:T(8,128)(2,1)S(1)}, s16[81,16,128]{2,1,0:T(8,128)(2,1)S(1)}, u32[]{:S(2)}, u32[]{:S(2)}) collective-permute-start(s16[81,16,128]{2,1,0:T(8,128)(2,1)S(1)} %get-tuple-element.39), channel_id=1, source_target_pairs={{0,4},{4,8},{8,12},{12,0},{16,20},{20,24},{24,28},{28,16},{32,36},... | collective-permute-start | bytes 995336 | tf_op jit(solution)/shard_map/ppermute | solution.py:420
  21.9 1.8 %collective-permute-start.6 = (s16[81,16,128]{2,1,0:T(8,128)(2,1)S(1)}, s16[81,16,128]{2,1,0:T(8,128)(2,1)S(1)}, u32[]{:S(2)}, u32[]{:S(2)}) collective-permute-start(s16[81,16,128]{2,1,0:T(8,128)(2,1)S(1)} %get-tuple-element.41), channel_id=1, source_target_pairs={{0,12},{4,0},{8,4},{12,8},{16,28},{20,16},{24,20},{28,24},{32,44},... | collective-permute-start | bytes 995336 | tf_op jit(solution)/shard_map/ppermute | solution.py:420
  23.6 0.8 collective-permute-done.got
  24.5 1.4 %shard_map.119 = (s16[49,16,128]{2,1,0:T(8,128)(2,1)S(1)}, s16[49,16,128]{2,1,0:T(8,128)(2,1)S(1)}) custom-call(s32[1]{0:T(128)} %bitcast.me_ref, bf16[2,256,256]{2,1,0:T(8,128)(2,1)S(1)} %copy-done.1, bf16[2,256,4096]{2,1,0:T(8,128)(2,1)S(1)} %copy-done, s16[193,16,128]{2,1,0:T(8,128)(2,1)S(1)} %collective-permute-done.got), custom_call_target="tpu_custom_call" | custom-call | flops 268435456 | bytes 6291456 | tf_op jit(solution)/shard_map/pallas_call | solution.py:219
  25.9 2.4 %collective-permute-start.7 = (s16[49,16,128]{2,1,0:T(8,128)(2,1)S(1)}, s16[49,16,128]{2,1,0:T(8,128)(2,1)S(1)}, u32[]{:S(2)}, u32[]{:S(2)}) collective-permute-start(s16[49,16,128]{2,1,0:T(8,128)(2,1)S(1)} %get-tuple-element.34), channel_id=1, source_target_pairs={{0,16},{4,20},{8,24},{12,28},{16,0},{20,4},{24,8},{28,12},{32,48},... | collective-permute-start | bytes 602120 | tf_op jit(solution)/shard_map/ppermute | solution.py:420
  28.3 4.7 %collective-permute-start.8 = (s16[49,16,128]{2,1,0:T(8,128)(2,1)S(1)}, s16[49,16,128]{2,1,0:T(8,128)(2,1)S(1)}, u32[]{:S(2)}, u32[]{:S(2)}) collective-permute-start(s16[49,16,128]{2,1,0:T(8,128)(2,1)S(1)} %get-tuple-element.43), channel_id=1, source_target_pairs={{0,112},{4,116},{8,120},{12,124},{16,32},{20,36},{24,40},{28,44},{... | collective-permute-start | bytes 602120 | tf_op jit(solution)/shard_map/ppermute | solution.py:420
  33.0 0.6 collective-permute-done.4.b0
  33.5 1.7 %shard_map.123 = (s16[41,16,128]{2,1,0:T(8,128)(2,1)S(1)}, s16[41,16,128]{2,1,0:T(8,128)(2,1)S(1)}, f32[2,32,2560]{2,1,0:T(8,128)S(1)}) custom-call(s32[1]{0:T(128)} %bitcast.me_ref, bf16[2,256,256]{2,1,0:T(8,128)(2,1)S(1)} %copy-done.1, bf16[2,256,4096]{2,1,0:T(8,128)(2,1)S(1)} %copy-done, s16[81,16,128]{2,1,0:T(8,128)(2,1)S(1)} %collective-permute-done.1.a0, ...), custom_call_target="tpu_custom_call" | custom-call | flops 268435456 | bytes 6291456 | tf_op jit(solution)/shard_map/pallas_call | solution.py:219
  35.2 5.7 %collective-permute-start.10 = (s16[41,16,128]{2,1,0:T(8,128)(2,1)S(1)}, s16[41,16,128]{2,1,0:T(8,128)(2,1)S(1)}, u32[]{:S(2)}, u32[]{:S(2)}) collective-permute-start(s16[41,16,128]{2,1,0:T(8,128)(2,1)S(1)} %get-tuple-element.47), channel_id=1, source_target_pairs={{0,112},{4,116},{8,120},{12,124},{16,32},{20,36},{24,40},{28,44},{... | collective-permute-start | bytes 503816 | tf_op jit(solution)/shard_map/ppermute | solution.py:420
  40.9 1.4 %shard_map.124 = (s16[25,16,128]{2,1,0:T(8,128)(2,1)S(1)}, s16[25,16,128]{2,1,0:T(8,128)(2,1)S(1)}, s16[25,16,128]{2,1,0:T(8,128)(2,1)S(1)}) custom-call(s32[1]{0:T(128)} %bitcast.me_ref, bf16[2,256,256]{2,1,0:T(8,128)(2,1)S(1)} %copy-done.1, bf16[2,256,4096]{2,1,0:T(8,128)(2,1)S(1)} %copy-done, s16[193,16,128]{2,1,0:T(8,128)(2,1)S(1)} %collective-permute-done.got, ...), custom_call_target="tpu_custom_call" | custom-call | flops 268435456 | bytes 6291456 | tf_op jit(solution)/shard_map/pallas_call | solution.py:219
  42.3 0.0 copy-start.2
  42.3 0.0 copy-start.3
  42.3 0.0 copy-start.4
  42.3 0.0 copy-start.5
  42.4 1.3 %collective-permute-done.10.got1 = s16[41,16,128]{2,1,0:T(8,128)(2,1)S(1)} collective-permute-done((s16[41,16,128]{2,1,0:T(8,128)(2,1)S(1)}, s16[41,16,128]{2,1,0:T(8,128)(2,1)S(1)}, u32[]{:S(2)}, u32[]{:S(2)}) %collective-permute-start.10) | collective-permute-done | bytes 167968 | tf_op jit(solution)/shard_map/ppermute | solution.py:420
  43.7 1.8 %collective-permute-done.9.got0 = s16[41,16,128]{2,1,0:T(8,128)(2,1)S(1)} collective-permute-done((s16[41,16,128]{2,1,0:T(8,128)(2,1)S(1)}, s16[41,16,128]{2,1,0:T(8,128)(2,1)S(1)}, u32[]{:S(2)}, u32[]{:S(2)}) %collective-permute-start.9) | collective-permute-done | bytes 167968 | tf_op jit(solution)/shard_map/ppermute | solution.py:420
  45.4 0.3 shard_map.125
  45.7 0.1 collective-permute-start.11
  45.8 0.8 collective-permute-start.12
  46.6 2.6 %collective-permute-start.13 = (s16[25,16,128]{2,1,0:T(8,128)(2,1)S(1)}, s16[25,16,128]{2,1,0:T(8,128)(2,1)S(1)}, u32[]{:S(2)}, u32[]{:S(2)}) collective-permute-start(s16[25,16,128]{2,1,0:T(8,128)(2,1)S(1)} %get-tuple-element.50), channel_id=1, source_target_pairs={{0,8},{4,12},{8,0},{12,4},{16,24},{20,28},{24,16},{28,20},{32,40},... | collective-permute-start | bytes 307208 | tf_op jit(solution)/shard_map/ppermute | solution.py:420
  49.3 0.7 collective-permute-start.14
  49.9 0.6 collective-permute-done.12.r1
  50.6 1.9 %collective-permute-done.13.r2 = s16[25,16,128]{2,1,0:T(8,128)(2,1)S(1)} collective-permute-done((s16[25,16,128]{2,1,0:T(8,128)(2,1)S(1)}, s16[25,16,128]{2,1,0:T(8,128)(2,1)S(1)}, u32[]{:S(2)}, u32[]{:S(2)}) %collective-permute-start.13) | collective-permute-done | bytes 102432 | tf_op jit(solution)/shard_map/ppermute | solution.py:420
  52.4 0.4 collective-permute-done.14.r3
  52.8 1.2 %shard_map.126.own = f32[2,16,1536]{2,1,0:T(8,128)S(1)} custom-call(s32[1]{0:T(128)} %bitcast.me_ref, bf16[2,256,256]{2,1,0:T(8,128)(2,1)S(1)} %copy-done.1, bf16[2,256,4096]{2,1,0:T(8,128)(2,1)S(1)} %copy-done, s16[193,16,128]{2,1,0:T(8,128)(2,1)S(1)} %collective-permute-done.got, s16[49,16,128]{2,1,0:T(8,128)(2,1)S(1)} %collective-permute-done.7.near0, ...), custom_call_target="tpu_custom_call" | custom-call | flops 268435456 | bytes 6291456 | tf_op jit(solution)/shard_map/pallas_call | solution.py:219
  54.0 0.3 shard_map.127
  54.3 0.2 collective-permute-start.15
  54.5 2.8 %collective-permute-start.16 = (s16[17,16,128]{2,1,0:T(8,128)(2,1)S(1)}, s16[17,16,128]{2,1,0:T(8,128)(2,1)S(1)}, u32[]{:S(2)}, u32[]{:S(2)}) collective-permute-start(s16[17,16,128]{2,1,0:T(8,128)(2,1)S(1)} %get-tuple-element.54), channel_id=1, source_target_pairs={{0,64},{4,68},{8,72},{12,76},{16,80},{20,84},{24,88},{28,92},{32,9... | collective-permute-start | bytes 208904 | tf_op jit(solution)/shard_map/ppermute | solution.py:420
  57.3 2.9 %collective-permute-start.17 = (s16[17,16,128]{2,1,0:T(8,128)(2,1)S(1)}, s16[17,16,128]{2,1,0:T(8,128)(2,1)S(1)}, u32[]{:S(2)}, u32[]{:S(2)}) collective-permute-start(s16[17,16,128]{2,1,0:T(8,128)(2,1)S(1)} %get-tuple-element.55), channel_id=1, source_target_pairs={{0,96},{4,100},{8,104},{12,108},{16,112},{20,116},{24,120},{28,124... | collective-permute-start | bytes 208904 | tf_op jit(solution)/shard_map/ppermute | solution.py:420
  60.2 0.1 collective-permute-done.15.c1
  60.3 1.3 %collective-permute-done.16.c2 = s16[17,16,128]{2,1,0:T(8,128)(2,1)S(1)} collective-permute-done((s16[17,16,128]{2,1,0:T(8,128)(2,1)S(1)}, s16[17,16,128]{2,1,0:T(8,128)(2,1)S(1)}, u32[]{:S(2)}, u32[]{:S(2)}) %collective-permute-start.16) | collective-permute-done | bytes 69664 | tf_op jit(solution)/shard_map/ppermute | solution.py:420
  61.6 1.7 %collective-permute-done.17.c3 = s16[17,16,128]{2,1,0:T(8,128)(2,1)S(1)} collective-permute-done((s16[17,16,128]{2,1,0:T(8,128)(2,1)S(1)}, s16[17,16,128]{2,1,0:T(8,128)(2,1)S(1)}, u32[]{:S(2)}, u32[]{:S(2)}) %collective-permute-start.17) | collective-permute-done | bytes 69664 | tf_op jit(solution)/shard_map/ppermute | solution.py:420
  63.4 1.1 %shard_map.128 = (f32[2,4,4096]{2,1,0:T(4,128)}, f32[2,4,4096]{2,1,0:T(4,128)}, f32[2,2,4]{2,1,0:T(2,128)}, f32[2,4,4096]{2,1,0:T(4,128)}, f32[2,2,4]{2,1,0:T(2,128)}, /*index=5*/bf16[32,16,128]{2,1,0:T(8,128)(2,1)}) custom-call(s16[17,16,128]{2,1,0:T(8,128)(2,1)S(1)} %get-tuple-element.52.c0, s16[17,16,128]{2,1,0:T(8,128)(2,1)S(1)} %collective-permute-done.15.c1, ...), custom_call_target="tpu_custom_call" | custom-call | flops 1310720 | bytes 2097152 | tf_op jit(solution)/shard_map/pallas_call | solution.py:393
  64.5 15.1 %all-to-all-start = ((bf16[32,16,128]{2,1,0:T(8,128)(2,1)}), bf16[32,16,128]{2,1,0:T(8,128)(2,1)S(1)}, u32[]{:S(2)}, u32[]{:S(2)}) async-start(bf16[32,16,128]{2,1,0:T(8,128)(2,1)} %get-tuple-element.61), calls=%async_computation | async-start | bytes 262144 | tf_op jit(solution)/shard_map/all_to_all | solution.py:405
  79.7 6.3 %all-to-all-done = bf16[32,16,128]{2,1,0:T(8,128)(2,1)S(1)} async-done(((bf16[32,16,128]{2,1,0:T(8,128)(2,1)}), bf16[32,16,128]{2,1,0:T(8,128)(2,1)S(1)}, u32[]{:S(2)}, u32[]{:S(2)}) %all-to-all-start) | async-done | bytes 131104 | tf_op jit(solution)/shard_map/all_to_all | solution.py:405
  86.0 0.1 copy.13
  86.1 7.3 %all_gather.3 = bf16[2,256,256]{2,1,0:T(8,128)(2,1)S(1)} all-gather(bf16[2,64,256]{2,1,0:T(8,128)(2,1)S(1)} %reshape.23), channel_id=1, replica_groups=mesh['dp'=64,'group'=4] {'group'}, dimensions={1}, use_global_device_ids=true | all-gather | bytes 327680 | tf_op jit(solution)/shard_map/all_gather | solution.py:411
  93.4 0.7 copy.15
  (20 shorter events, 0.1 us)
Async XLA Ops:
  0.6 7.2 %copy-start.1 = (bf16[2,256,256]{2,1,0:T(8,128)(2,1)S(1)}, bf16[2,256,256]{2,1,0:T(8,128)(2,1)}, u32[]{:S(2)}) copy-start(bf16[2,256,256]{2,1,0:T(8,128)(2,1)} %acts_ref.12) | copy-start | bytes 786436
  0.6 7.2 %copy-start = (bf16[2,256,4096]{2,1,0:T(8,128)(2,1)S(1)}, bf16[2,256,4096]{2,1,0:T(8,128)(2,1)}, u32[]{:S(2)}) copy-start(bf16[2,256,4096]{2,1,0:T(8,128)(2,1)} %grads_ref.15) | copy-start | bytes 12582916
  4.0 20.4 %collective-permute-start = (s16[193,16,128]{2,1,0:T(8,128)(2,1)}, s16[193,16,128]{2,1,0:T(8,128)(2,1)S(1)}, u32[]{:S(2)}, u32[]{:S(2)}) collective-permute-start(s16[193,16,128]{2,1,0:T(8,128)(2,1)} %shard_map.118), channel_id=1, source_target_pairs={{0,128},{4,132},{8,136},{12,140},{16,144},{20,148},{24,152},{28,15... | collective-permute-start | bytes 2371592 | tf_op jit(solution)/shard_map/ppermute | solution.py:420
  9.5 9.6 %collective-permute-start.2 = (s16[81,16,128]{2,1,0:T(8,128)(2,1)S(1)}, s16[81,16,128]{2,1,0:T(8,128)(2,1)S(1)}, u32[]{:S(2)}, u32[]{:S(2)}) collective-permute-start(s16[81,16,128]{2,1,0:T(8,128)(2,1)S(1)} %get-tuple-element.37), channel_id=1, source_target_pairs={{0,4},{4,8},{8,12},{12,0},{16,20},{20,24},{24,28},{28,16},{32,36},... | collective-permute-start | bytes 995336 | tf_op jit(solution)/shard_map/ppermute | solution.py:420
  10.8 8.3 %collective-permute-start.3 = (s16[81,16,128]{2,1,0:T(8,128)(2,1)S(1)}, s16[81,16,128]{2,1,0:T(8,128)(2,1)S(1)}, u32[]{:S(2)}, u32[]{:S(2)}) collective-permute-start(s16[81,16,128]{2,1,0:T(8,128)(2,1)S(1)} %get-tuple-element.38), channel_id=1, source_target_pairs={{0,12},{4,0},{8,4},{12,8},{16,28},{20,16},{24,20},{28,24},{32,44},... | collective-permute-start | bytes 995336 | tf_op jit(solution)/shard_map/ppermute | solution.py:420
  14.0 14.3 %collective-permute-start.1 = (s16[81,16,128]{2,1,0:T(8,128)(2,1)S(1)}, s16[81,16,128]{2,1,0:T(8,128)(2,1)S(1)}, u32[]{:S(2)}, u32[]{:S(2)}) collective-permute-start(s16[81,16,128]{2,1,0:T(8,128)(2,1)S(1)} %get-tuple-element.36), channel_id=1, source_target_pairs={{0,12},{4,0},{8,4},{12,8},{16,28},{20,16},{24,20},{28,24},{32,44},... | collective-permute-start | bytes 995336 | tf_op jit(solution)/shard_map/ppermute | solution.py:420
  15.3 17.6 %collective-permute-start.5 = (s16[81,16,128]{2,1,0:T(8,128)(2,1)S(1)}, s16[81,16,128]{2,1,0:T(8,128)(2,1)S(1)}, u32[]{:S(2)}, u32[]{:S(2)}) collective-permute-start(s16[81,16,128]{2,1,0:T(8,128)(2,1)S(1)} %get-tuple-element.40), channel_id=1, source_target_pairs={{0,4},{4,8},{8,12},{12,0},{16,20},{20,24},{24,28},{28,16},{32,36},... | collective-permute-start | bytes 995336 | tf_op jit(solution)/shard_map/ppermute | solution.py:420
  20.9 12.7 %collective-permute-start.4 = (s16[81,16,128]{2,1,0:T(8,128)(2,1)S(1)}, s16[81,16,128]{2,1,0:T(8,128)(2,1)S(1)}, u32[]{:S(2)}, u32[]{:S(2)}) collective-permute-start(s16[81,16,128]{2,1,0:T(8,128)(2,1)S(1)} %get-tuple-element.39), channel_id=1, source_target_pairs={{0,4},{4,8},{8,12},{12,0},{16,20},{20,24},{24,28},{28,16},{32,36},... | collective-permute-start | bytes 995336 | tf_op jit(solution)/shard_map/ppermute | solution.py:420
  21.9 11.7 %collective-permute-start.6 = (s16[81,16,128]{2,1,0:T(8,128)(2,1)S(1)}, s16[81,16,128]{2,1,0:T(8,128)(2,1)S(1)}, u32[]{:S(2)}, u32[]{:S(2)}) collective-permute-start(s16[81,16,128]{2,1,0:T(8,128)(2,1)S(1)} %get-tuple-element.41), channel_id=1, source_target_pairs={{0,12},{4,0},{8,4},{12,8},{16,28},{20,16},{24,20},{28,24},{32,44},... | collective-permute-start | bytes 995336 | tf_op jit(solution)/shard_map/ppermute | solution.py:420
  25.9 15.0 %collective-permute-start.7 = (s16[49,16,128]{2,1,0:T(8,128)(2,1)S(1)}, s16[49,16,128]{2,1,0:T(8,128)(2,1)S(1)}, u32[]{:S(2)}, u32[]{:S(2)}) collective-permute-start(s16[49,16,128]{2,1,0:T(8,128)(2,1)S(1)} %get-tuple-element.34), channel_id=1, source_target_pairs={{0,16},{4,20},{8,24},{12,28},{16,0},{20,4},{24,8},{28,12},{32,48},... | collective-permute-start | bytes 602120 | tf_op jit(solution)/shard_map/ppermute | solution.py:420
  28.3 12.6 %collective-permute-start.8 = (s16[49,16,128]{2,1,0:T(8,128)(2,1)S(1)}, s16[49,16,128]{2,1,0:T(8,128)(2,1)S(1)}, u32[]{:S(2)}, u32[]{:S(2)}) collective-permute-start(s16[49,16,128]{2,1,0:T(8,128)(2,1)S(1)} %get-tuple-element.43), channel_id=1, source_target_pairs={{0,112},{4,116},{8,120},{12,124},{16,32},{20,36},{24,40},{28,44},{... | collective-permute-start | bytes 602120 | tf_op jit(solution)/shard_map/ppermute | solution.py:420
  35.2 8.4 %collective-permute-start.10 = (s16[41,16,128]{2,1,0:T(8,128)(2,1)S(1)}, s16[41,16,128]{2,1,0:T(8,128)(2,1)S(1)}, u32[]{:S(2)}, u32[]{:S(2)}) collective-permute-start(s16[41,16,128]{2,1,0:T(8,128)(2,1)S(1)} %get-tuple-element.47), channel_id=1, source_target_pairs={{0,112},{4,116},{8,120},{12,124},{16,32},{20,36},{24,40},{28,44},{... | collective-permute-start | bytes 503816 | tf_op jit(solution)/shard_map/ppermute | solution.py:420
  40.9 4.5 %collective-permute-start.9 = (s16[41,16,128]{2,1,0:T(8,128)(2,1)S(1)}, s16[41,16,128]{2,1,0:T(8,128)(2,1)S(1)}, u32[]{:S(2)}, u32[]{:S(2)}) collective-permute-start(s16[41,16,128]{2,1,0:T(8,128)(2,1)S(1)} %get-tuple-element.46), channel_id=1, source_target_pairs={{0,16},{4,20},{8,24},{12,28},{16,0},{20,4},{24,8},{28,12},{32,48},... | collective-permute-start | bytes 503816 | tf_op jit(solution)/shard_map/ppermute | solution.py:420
  42.3 21.1 %copy-start.2 = (f32[2,4,4096]{2,1,0:T(4,128)S(1)}, f32[2,4,4096]{2,1,0:T(4,128)}, u32[]{:S(2)}) copy-start(f32[2,4,4096]{2,1,0:T(4,128)} %master.1) | copy-start | bytes 393220
  42.3 21.1 %copy-start.3 = (s32[2,4,4096]{2,1,0:T(4,128)S(1)}, s32[2,4,4096]{2,1,0:T(4,128)}, u32[]{:S(2)}) copy-start(s32[2,4,4096]{2,1,0:T(4,128)} %m_codes.1) | copy-start | bytes 393220
  42.3 21.0 %copy-start.4 = (s32[2,4,4096]{2,1,0:T(4,128)S(1)}, s32[2,4,4096]{2,1,0:T(4,128)}, u32[]{:S(2)}) copy-start(s32[2,4,4096]{2,1,0:T(4,128)} %v_codes.1) | copy-start | bytes 393220
  42.3 21.0 %copy-start.5 = (f32[2,4,2]{1,2,0:T(2,128)S(1)}, f32[2,4,2]{1,2,0:T(2,128)}, u32[]{:S(2)}) copy-start(f32[2,4,2]{1,2,0:T(2,128)} %param.11) | copy-start | bytes 196
  42.4 21.0 %copy-start.6 = (f32[2,4,2]{1,2,0:T(2,128)S(1)}, f32[2,4,2]{1,2,0:T(2,128)}, u32[]{:S(2)}) copy-start(f32[2,4,2]{1,2,0:T(2,128)} %param.13) | copy-start | bytes 196
  45.7 8.3 %collective-permute-start.11 = (s16[41,16,128]{2,1,0:T(8,128)(2,1)S(1)}, s16[41,16,128]{2,1,0:T(8,128)(2,1)S(1)}, u32[]{:S(2)}, u32[]{:S(2)}) collective-permute-start(s16[41,16,128]{2,1,0:T(8,128)(2,1)S(1)} %get-tuple-element.49), channel_id=1, source_target_pairs={{0,128},{4,132},{8,136},{12,140},{16,144},{20,148},{24,152},{28,15... | collective-permute-start | bytes 503816 | tf_op jit(solution)/shard_map/ppermute | solution.py:420
  45.8 4.8 %collective-permute-start.12 = (s16[25,16,128]{2,1,0:T(8,128)(2,1)S(1)}, s16[25,16,128]{2,1,0:T(8,128)(2,1)S(1)}, u32[]{:S(2)}, u32[]{:S(2)}) collective-permute-start(s16[25,16,128]{2,1,0:T(8,128)(2,1)S(1)} %get-tuple-element.44), channel_id=1, source_target_pairs={{0,4},{4,8},{8,12},{12,0},{16,20},{20,24},{24,28},{28,16},{32,36},... | collective-permute-start | bytes 307208 | tf_op jit(solution)/shard_map/ppermute | solution.py:420
  46.6 5.8 %collective-permute-start.13 = (s16[25,16,128]{2,1,0:T(8,128)(2,1)S(1)}, s16[25,16,128]{2,1,0:T(8,128)(2,1)S(1)}, u32[]{:S(2)}, u32[]{:S(2)}) collective-permute-start(s16[25,16,128]{2,1,0:T(8,128)(2,1)S(1)} %get-tuple-element.50), channel_id=1, source_target_pairs={{0,8},{4,12},{8,0},{12,4},{16,24},{20,28},{24,16},{28,20},{32,40},... | collective-permute-start | bytes 307208 | tf_op jit(solution)/shard_map/ppermute | solution.py:420
  49.3 3.5 %collective-permute-start.14 = (s16[25,16,128]{2,1,0:T(8,128)(2,1)S(1)}, s16[25,16,128]{2,1,0:T(8,128)(2,1)S(1)}, u32[]{:S(2)}, u32[]{:S(2)}) collective-permute-start(s16[25,16,128]{2,1,0:T(8,128)(2,1)S(1)} %get-tuple-element.51), channel_id=1, source_target_pairs={{0,12},{4,0},{8,4},{12,8},{16,28},{20,16},{24,20},{28,24},{32,44},... | collective-permute-start | bytes 307208 | tf_op jit(solution)/shard_map/ppermute | solution.py:420
  54.3 6.0 %collective-permute-start.15 = (s16[17,16,128]{2,1,0:T(8,128)(2,1)S(1)}, s16[17,16,128]{2,1,0:T(8,128)(2,1)S(1)}, u32[]{:S(2)}, u32[]{:S(2)}) collective-permute-start(s16[17,16,128]{2,1,0:T(8,128)(2,1)S(1)} %get-tuple-element.53), channel_id=1, source_target_pairs={{0,32},{4,36},{8,40},{12,44},{16,48},{20,52},{24,56},{28,60},{32,6... | collective-permute-start | bytes 208904 | tf_op jit(solution)/shard_map/ppermute | solution.py:420
  54.5 7.1 %collective-permute-start.16 = (s16[17,16,128]{2,1,0:T(8,128)(2,1)S(1)}, s16[17,16,128]{2,1,0:T(8,128)(2,1)S(1)}, u32[]{:S(2)}, u32[]{:S(2)}) collective-permute-start(s16[17,16,128]{2,1,0:T(8,128)(2,1)S(1)} %get-tuple-element.54), channel_id=1, source_target_pairs={{0,64},{4,68},{8,72},{12,76},{16,80},{20,84},{24,88},{28,92},{32,9... | collective-permute-start | bytes 208904 | tf_op jit(solution)/shard_map/ppermute | solution.py:420
  57.3 6.0 %collective-permute-start.17 = (s16[17,16,128]{2,1,0:T(8,128)(2,1)S(1)}, s16[17,16,128]{2,1,0:T(8,128)(2,1)S(1)}, u32[]{:S(2)}, u32[]{:S(2)}) collective-permute-start(s16[17,16,128]{2,1,0:T(8,128)(2,1)S(1)} %get-tuple-element.55), channel_id=1, source_target_pairs={{0,96},{4,100},{8,104},{12,108},{16,112},{20,116},{24,120},{28,124... | collective-permute-start | bytes 208904 | tf_op jit(solution)/shard_map/ppermute | solution.py:420
  64.5 21.4 %all-to-all-start = ((bf16[32,16,128]{2,1,0:T(8,128)(2,1)}), bf16[32,16,128]{2,1,0:T(8,128)(2,1)S(1)}, u32[]{:S(2)}, u32[]{:S(2)}) async-start(bf16[32,16,128]{2,1,0:T(8,128)(2,1)} %get-tuple-element.61), calls=%async_computation | async-start | bytes 262144 | tf_op jit(solution)/shard_map/all_to_all | solution.py:405

commit v6 on v5

--- a/solution.py
+++ b/solution.py
@@ -434,12 +434,14 @@
     near0, near1 = send(near0, PAIR[0]), send(near1, PAIR[1])
     steps = along_x(*inputs, crossed, there0, there1)
     kept, _ = lax.optimization_barrier((kept, steps[0]))
-    steps = [send(steps[0], UP), send(steps[1], TWO), send(steps[2], DOWN)]
+    two = send(steps[1], TWO)
+    steps = [send(steps[0], UP), two, send(steps[2], DOWN)]
     across, rest = pair_codes(kept, near0, near1)
     across = send(across, ACROSS)
     own = own_b(*inputs, crossed, there0, there1, *steps)
     codes = join(rest, across, own)
-    codes = [codes[0]] + [send(codes[k], z_shift(k)) for k in range(1, 4)]
+    far = send(codes[2], z_shift(2))
+    codes = [codes[0], send(codes[1], z_shift(1)), far, send(codes[3], z_shift(3))]
     *state, weights = adam(codes, master, m_codes, m_scale, v_codes, v_scale)
     return (*state, push_weights(weights))
 

time: 94.3 us -> 94.3 us (level)
  no operation moved by 1% of the time
where the time goes in v6:
time: 94.3 us; the launch traced here: 94.1 us
  starting transfers between devices  48.9 us (52%)
  waiting for transfers between devices  20.4 us (22%)
  Pallas kernels  15.8 us (17%)
  blocking collectives  7.29 us (8%)
    ppermute x18, starting transfers between devices, send(): return lax.ppermute(codes, 'dp', pairs)  33.8 us
    all_to_all x1, starting transfers between devices, push_weights(): lax.all_to_all(weights, ('dp', 'group'), 0, 0, axis_index_groups=swap_gro...  15.1 us
    pallas_call x10, Pallas kernels, call(): pl.pallas_call(kernel, in_specs=SPECS[:inputs] + [VMEM] * (len(ins) - inp...  14.6 us
    ppermute x18, waiting for transfers between devices, send(): return lax.ppermute(codes, 'dp', pairs)  14.1 us
    all_gather x1, blocking collectives, push_weights(): return lax.all_gather(slab, 'group', axis=1, tiled=True)  7.29 us
    all_to_all x1, waiting for transfers between devices, push_weights(): lax.all_to_all(weights, ('dp', 'group'), 0, 0, axis_index_groups=swap_gro...  6.31 us
  transfers between devices with their start and end apart: 19, of which 12 were waited for; matrix products, arithmetic and copies ran while one was open for 0% of the time, Pallas kernels for 11%

profile of v6, /device:TPU:1, one launch (start us, length us, event | category | flops | bytes accessed | tf_op | source)
XLA Modules:
  0.0 94.1 jit_solution(4786895368590587063)
XLA Ops:
  0.7 3.4 %shard_map.118 = s16[193,16,128]{2,1,0:T(8,128)(2,1)} custom-call(s32[1]{0:T(128)} %bitcast.me_ref, bf16[2,256,256]{2,1,0:T(8,128)(2,1)} %acts_ref.12, bf16[2,256,4096]{2,1,0:T(8,128)(2,1)} %grads_ref.15), custom_call_target="tpu_custom_call" | custom-call | flops 268435456 | bytes 6291456 | tf_op jit(solution)/shard_map/pallas_call | solution.py:219
  4.0 3.8 %collective-permute-start = (s16[193,16,128]{2,1,0:T(8,128)(2,1)}, s16[193,16,128]{2,1,0:T(8,128)(2,1)S(1)}, u32[]{:S(2)}, u32[]{:S(2)}) collective-permute-start(s16[193,16,128]{2,1,0:T(8,128)(2,1)} %shard_map.118), channel_id=1, source_target_pairs={{0,128},{4,132},{8,136},{12,140},{16,144},{20,148},{24,152},{28,15... | collective-permute-start | bytes 2371592 | tf_op jit(solution)/shard_map/ppermute | solution.py:420
  7.9 1.7 %shard_map.121 = (s16[81,16,128]{2,1,0:T(8,128)(2,1)S(1)}, s16[81,16,128]{2,1,0:T(8,128)(2,1)S(1)}) custom-call(s32[1]{0:T(128)} %bitcast.me_ref, bf16[2,256,256]{2,1,0:T(8,128)(2,1)S(1)} %copy-done.1, bf16[2,256,4096]{2,1,0:T(8,128)(2,1)S(1)} %copy-done), custom_call_target="tpu_custom_call" | custom-call | flops 268435456 | bytes 6291456 | tf_op jit(solution)/shard_map/pallas_call | solution.py:219
  9.5 1.3 %collective-permute-start.2 = (s16[81,16,128]{2,1,0:T(8,128)(2,1)S(1)}, s16[81,16,128]{2,1,0:T(8,128)(2,1)S(1)}, u32[]{:S(2)}, u32[]{:S(2)}) collective-permute-start(s16[81,16,128]{2,1,0:T(8,128)(2,1)S(1)} %get-tuple-element.37), channel_id=1, source_target_pairs={{0,4},{4,8},{8,12},{12,0},{16,20},{20,24},{24,28},{28,16},{32,36},... | collective-permute-start | bytes 995336 | tf_op jit(solution)/shard_map/ppermute | solution.py:420
  10.8 1.5 %collective-permute-start.3 = (s16[81,16,128]{2,1,0:T(8,128)(2,1)S(1)}, s16[81,16,128]{2,1,0:T(8,128)(2,1)S(1)}, u32[]{:S(2)}, u32[]{:S(2)}) collective-permute-start(s16[81,16,128]{2,1,0:T(8,128)(2,1)S(1)} %get-tuple-element.38), channel_id=1, source_target_pairs={{0,12},{4,0},{8,4},{12,8},{16,28},{20,16},{24,20},{28,24},{32,44},... | collective-permute-start | bytes 995336 | tf_op jit(solution)/shard_map/ppermute | solution.py:420
  12.3 1.7 %shard_map.120 = (s16[81,16,128]{2,1,0:T(8,128)(2,1)S(1)}, s16[81,16,128]{2,1,0:T(8,128)(2,1)S(1)}) custom-call(s32[1]{0:T(128)} %bitcast.me_ref, bf16[2,256,256]{2,1,0:T(8,128)(2,1)S(1)} %copy-done.1, bf16[2,256,4096]{2,1,0:T(8,128)(2,1)S(1)} %copy-done), custom_call_target="tpu_custom_call" | custom-call | flops 268435456 | bytes 6291456 | tf_op jit(solution)/shard_map/pallas_call | solution.py:219
  14.0 1.4 %collective-permute-start.1 = (s16[81,16,128]{2,1,0:T(8,128)(2,1)S(1)}, s16[81,16,128]{2,1,0:T(8,128)(2,1)S(1)}, u32[]{:S(2)}, u32[]{:S(2)}) collective-permute-start(s16[81,16,128]{2,1,0:T(8,128)(2,1)S(1)} %get-tuple-element.36), channel_id=1, source_target_pairs={{0,12},{4,0},{8,4},{12,8},{16,28},{20,16},{24,20},{28,24},{32,44},... | collective-permute-start | bytes 995336 | tf_op jit(solution)/shard_map/ppermute | solution.py:420
  15.3 0.2 collective-permute-start.5
  15.5 3.6 %collective-permute-done.2.rest_0_ = s16[81,16,128]{2,1,0:T(8,128)(2,1)S(1)} collective-permute-done((s16[81,16,128]{2,1,0:T(8,128)(2,1)S(1)}, s16[81,16,128]{2,1,0:T(8,128)(2,1)S(1)}, u32[]{:S(2)}, u32[]{:S(2)}) %collective-permute-start.2) | collective-permute-done | bytes 331808 | tf_op jit(solution)/shard_map/ppermute | solution.py:420
  19.2 1.7 %shard_map.122 = (s16[81,16,128]{2,1,0:T(8,128)(2,1)S(1)}, s16[81,16,128]{2,1,0:T(8,128)(2,1)S(1)}) custom-call(s32[1]{0:T(128)} %bitcast.me_ref, bf16[2,256,256]{2,1,0:T(8,128)(2,1)S(1)} %copy-done.1, bf16[2,256,4096]{2,1,0:T(8,128)(2,1)S(1)} %copy-done, s16[81,16,128]{2,1,0:T(8,128)(2,1)S(1)} %collective-permute-done.2.rest_0_, ...), custom_call_target="tpu_custom_call" | custom-call | flops 268435456 | bytes 6291456 | tf_op jit(solution)/shard_map/pallas_call | solution.py:219
  20.9 1.0 %collective-permute-start.4 = (s16[81,16,128]{2,1,0:T(8,128)(2,1)S(1)}, s16[81,16,128]{2,1,0:T(8,128)(2,1)S(1)}, u32[]{:S(2)}, u32[]{:S(2)}) collective-permute-start(s16[81,16,128]{2,1,0:T(8,128)(2,1)S(1)} %get-tuple-element.39), channel_id=1, source_target_pairs={{0,4},{4,8},{8,12},{12,0},{16,20},{20,24},{24,28},{28,16},{32,36},... | collective-permute-start | bytes 995336 | tf_op jit(solution)/shard_map/ppermute | solution.py:420
  21.9 1.8 %collective-permute-start.6 = (s16[81,16,128]{2,1,0:T(8,128)(2,1)S(1)}, s16[81,16,128]{2,1,0:T(8,128)(2,1)S(1)}, u32[]{:S(2)}, u32[]{:S(2)}) collective-permute-start(s16[81,16,128]{2,1,0:T(8,128)(2,1)S(1)} %get-tuple-element.41), channel_id=1, source_target_pairs={{0,12},{4,0},{8,4},{12,8},{16,28},{20,16},{24,20},{28,24},{32,44},... | collective-permute-start | bytes 995336 | tf_op jit(solution)/shard_map/ppermute | solution.py:420
  23.6 0.8 collective-permute-done.got
  24.5 1.4 %shard_map.119 = (s16[49,16,128]{2,1,0:T(8,128)(2,1)S(1)}, s16[49,16,128]{2,1,0:T(8,128)(2,1)S(1)}) custom-call(s32[1]{0:T(128)} %bitcast.me_ref, bf16[2,256,256]{2,1,0:T(8,128)(2,1)S(1)} %copy-done.1, bf16[2,256,4096]{2,1,0:T(8,128)(2,1)S(1)} %copy-done, s16[193,16,128]{2,1,0:T(8,128)(2,1)S(1)} %collective-permute-done.got), custom_call_target="tpu_custom_call" | custom-call | flops 268435456 | bytes 6291456 | tf_op jit(solution)/shard_map/pallas_call | solution.py:219
  25.9 2.4 %collective-permute-start.7 = (s16[49,16,128]{2,1,0:T(8,128)(2,1)S(1)}, s16[49,16,128]{2,1,0:T(8,128)(2,1)S(1)}, u32[]{:S(2)}, u32[]{:S(2)}) collective-permute-start(s16[49,16,128]{2,1,0:T(8,128)(2,1)S(1)} %get-tuple-element.34), channel_id=1, source_target_pairs={{0,16},{4,20},{8,24},{12,28},{16,0},{20,4},{24,8},{28,12},{32,48},... | collective-permute-start | bytes 602120 | tf_op jit(solution)/shard_map/ppermute | solution.py:420
  28.3 4.7 %collective-permute-start.8 = (s16[49,16,128]{2,1,0:T(8,128)(2,1)S(1)}, s16[49,16,128]{2,1,0:T(8,128)(2,1)S(1)}, u32[]{:S(2)}, u32[]{:S(2)}) collective-permute-start(s16[49,16,128]{2,1,0:T(8,128)(2,1)S(1)} %get-tuple-element.43), channel_id=1, source_target_pairs={{0,112},{4,116},{8,120},{12,124},{16,32},{20,36},{24,40},{28,44},{... | collective-permute-start | bytes 602120 | tf_op jit(solution)/shard_map/ppermute | solution.py:420
  33.0 0.6 collective-permute-done.4.b0
  33.5 1.7 %shard_map.123 = (s16[41,16,128]{2,1,0:T(8,128)(2,1)S(1)}, s16[41,16,128]{2,1,0:T(8,128)(2,1)S(1)}, f32[2,32,2560]{2,1,0:T(8,128)S(1)}) custom-call(s32[1]{0:T(128)} %bitcast.me_ref, bf16[2,256,256]{2,1,0:T(8,128)(2,1)S(1)} %copy-done.1, bf16[2,256,4096]{2,1,0:T(8,128)(2,1)S(1)} %copy-done, s16[81,16,128]{2,1,0:T(8,128)(2,1)S(1)} %collective-permute-done.1.a0, ...), custom_call_target="tpu_custom_call" | custom-call | flops 268435456 | bytes 6291456 | tf_op jit(solution)/shard_map/pallas_call | solution.py:219
  35.2 5.7 %collective-permute-start.10 = (s16[41,16,128]{2,1,0:T(8,128)(2,1)S(1)}, s16[41,16,128]{2,1,0:T(8,128)(2,1)S(1)}, u32[]{:S(2)}, u32[]{:S(2)}) collective-permute-start(s16[41,16,128]{2,1,0:T(8,128)(2,1)S(1)} %get-tuple-element.47), channel_id=1, source_target_pairs={{0,112},{4,116},{8,120},{12,124},{16,32},{20,36},{24,40},{28,44},{... | collective-permute-start | bytes 503816 | tf_op jit(solution)/shard_map/ppermute | solution.py:420
  40.9 1.4 %shard_map.124 = (s16[25,16,128]{2,1,0:T(8,128)(2,1)S(1)}, s16[25,16,128]{2,1,0:T(8,128)(2,1)S(1)}, s16[25,16,128]{2,1,0:T(8,128)(2,1)S(1)}) custom-call(s32[1]{0:T(128)} %bitcast.me_ref, bf16[2,256,256]{2,1,0:T(8,128)(2,1)S(1)} %copy-done.1, bf16[2,256,4096]{2,1,0:T(8,128)(2,1)S(1)} %copy-done, s16[193,16,128]{2,1,0:T(8,128)(2,1)S(1)} %collective-permute-done.got, ...), custom_call_target="tpu_custom_call" | custom-call | flops 268435456 | bytes 6291456 | tf_op jit(solution)/shard_map/pallas_call | solution.py:219
  42.3 0.0 copy-start.2
  42.3 0.0 copy-start.3
  42.3 0.0 copy-start.4
  42.3 0.0 copy-start.5
  42.4 1.3 %collective-permute-done.10.got1 = s16[41,16,128]{2,1,0:T(8,128)(2,1)S(1)} collective-permute-done((s16[41,16,128]{2,1,0:T(8,128)(2,1)S(1)}, s16[41,16,128]{2,1,0:T(8,128)(2,1)S(1)}, u32[]{:S(2)}, u32[]{:S(2)}) %collective-permute-start.10) | collective-permute-done | bytes 167968 | tf_op jit(solution)/shard_map/ppermute | solution.py:420
  43.7 1.8 %collective-permute-done.9.got0 = s16[41,16,128]{2,1,0:T(8,128)(2,1)S(1)} collective-permute-done((s16[41,16,128]{2,1,0:T(8,128)(2,1)S(1)}, s16[41,16,128]{2,1,0:T(8,128)(2,1)S(1)}, u32[]{:S(2)}, u32[]{:S(2)}) %collective-permute-start.9) | collective-permute-done | bytes 167968 | tf_op jit(solution)/shard_map/ppermute | solution.py:420
  45.4 0.3 shard_map.125
  45.7 0.1 collective-permute-start.11
  45.8 0.8 collective-permute-start.12
  46.6 2.6 %collective-permute-start.13 = (s16[25,16,128]{2,1,0:T(8,128)(2,1)S(1)}, s16[25,16,128]{2,1,0:T(8,128)(2,1)S(1)}, u32[]{:S(2)}, u32[]{:S(2)}) collective-permute-start(s16[25,16,128]{2,1,0:T(8,128)(2,1)S(1)} %get-tuple-element.50), channel_id=1, source_target_pairs={{0,8},{4,12},{8,0},{12,4},{16,24},{20,28},{24,16},{28,20},{32,40},... | collective-permute-start | bytes 307208 | tf_op jit(solution)/shard_map/ppermute | solution.py:420
  49.3 0.7 collective-permute-start.14
  49.9 0.6 collective-permute-done.12.r1
  50.6 1.9 %collective-permute-done.13.r2 = s16[25,16,128]{2,1,0:T(8,128)(2,1)S(1)} collective-permute-done((s16[25,16,128]{2,1,0:T(8,128)(2,1)S(1)}, s16[25,16,128]{2,1,0:T(8,128)(2,1)S(1)}, u32[]{:S(2)}, u32[]{:S(2)}) %collective-permute-start.13) | collective-permute-done | bytes 102432 | tf_op jit(solution)/shard_map/ppermute | solution.py:420
  52.4 0.4 collective-permute-done.14.r3
  52.8 1.2 %shard_map.126.own = f32[2,16,1536]{2,1,0:T(8,128)S(1)} custom-call(s32[1]{0:T(128)} %bitcast.me_ref, bf16[2,256,256]{2,1,0:T(8,128)(2,1)S(1)} %copy-done.1, bf16[2,256,4096]{2,1,0:T(8,128)(2,1)S(1)} %copy-done, s16[193,16,128]{2,1,0:T(8,128)(2,1)S(1)} %collective-permute-done.got, s16[49,16,128]{2,1,0:T(8,128)(2,1)S(1)} %collective-permute-done.7.near0, ...), custom_call_target="tpu_custom_call" | custom-call | flops 268435456 | bytes 6291456 | tf_op jit(solution)/shard_map/pallas_call | solution.py:219
  54.0 0.3 shard_map.127
  54.3 0.2 collective-permute-start.15
  54.5 2.8 %collective-permute-start.16 = (s16[17,16,128]{2,1,0:T(8,128)(2,1)S(1)}, s16[17,16,128]{2,1,0:T(8,128)(2,1)S(1)}, u32[]{:S(2)}, u32[]{:S(2)}) collective-permute-start(s16[17,16,128]{2,1,0:T(8,128)(2,1)S(1)} %get-tuple-element.54), channel_id=1, source_target_pairs={{0,64},{4,68},{8,72},{12,76},{16,80},{20,84},{24,88},{28,92},{32,9... | collective-permute-start | bytes 208904 | tf_op jit(solution)/shard_map/ppermute | solution.py:420
  57.3 2.9 %collective-permute-start.17 = (s16[17,16,128]{2,1,0:T(8,128)(2,1)S(1)}, s16[17,16,128]{2,1,0:T(8,128)(2,1)S(1)}, u32[]{:S(2)}, u32[]{:S(2)}) collective-permute-start(s16[17,16,128]{2,1,0:T(8,128)(2,1)S(1)} %get-tuple-element.55), channel_id=1, source_target_pairs={{0,96},{4,100},{8,104},{12,108},{16,112},{20,116},{24,120},{28,124... | collective-permute-start | bytes 208904 | tf_op jit(solution)/shard_map/ppermute | solution.py:420
  60.2 0.1 collective-permute-done.15.c1
  60.3 1.3 %collective-permute-done.16.c2 = s16[17,16,128]{2,1,0:T(8,128)(2,1)S(1)} collective-permute-done((s16[17,16,128]{2,1,0:T(8,128)(2,1)S(1)}, s16[17,16,128]{2,1,0:T(8,128)(2,1)S(1)}, u32[]{:S(2)}, u32[]{:S(2)}) %collective-permute-start.16) | collective-permute-done | bytes 69664 | tf_op jit(solution)/shard_map/ppermute | solution.py:420
  61.6 1.7 %collective-permute-done.17.c3 = s16[17,16,128]{2,1,0:T(8,128)(2,1)S(1)} collective-permute-done((s16[17,16,128]{2,1,0:T(8,128)(2,1)S(1)}, s16[17,16,128]{2,1,0:T(8,128)(2,1)S(1)}, u32[]{:S(2)}, u32[]{:S(2)}) %collective-permute-start.17) | collective-permute-done | bytes 69664 | tf_op jit(solution)/shard_map/ppermute | solution.py:420
  63.4 1.1 %shard_map.128 = (f32[2,4,4096]{2,1,0:T(4,128)}, f32[2,4,4096]{2,1,0:T(4,128)}, f32[2,2,4]{2,1,0:T(2,128)}, f32[2,4,4096]{2,1,0:T(4,128)}, f32[2,2,4]{2,1,0:T(2,128)}, /*index=5*/bf16[32,16,128]{2,1,0:T(8,128)(2,1)}) custom-call(s16[17,16,128]{2,1,0:T(8,128)(2,1)S(1)} %get-tuple-element.52.c0, s16[17,16,128]{2,1,0:T(8,128)(2,1)S(1)} %collective-permute-done.15.c1, ...), custom_call_target="tpu_custom_call" | custom-call | flops 1310720 | bytes 2097152 | tf_op jit(solution)/shard_map/pallas_call | solution.py:393
  64.5 15.1 %all-to-all-start = ((bf16[32,16,128]{2,1,0:T(8,128)(2,1)}), bf16[32,16,128]{2,1,0:T(8,128)(2,1)S(1)}, u32[]{:S(2)}, u32[]{:S(2)}) async-start(bf16[32,16,128]{2,1,0:T(8,128)(2,1)} %get-tuple-element.61), calls=%async_computation | async-start | bytes 262144 | tf_op jit(solution)/shard_map/all_to_all | solution.py:405
  79.7 6.3 %all-to-all-done = bf16[32,16,128]{2,1,0:T(8,128)(2,1)S(1)} async-done(((bf16[32,16,128]{2,1,0:T(8,128)(2,1)}), bf16[32,16,128]{2,1,0:T(8,128)(2,1)S(1)}, u32[]{:S(2)}, u32[]{:S(2)}) %all-to-all-start) | async-done | bytes 131104 | tf_op jit(solution)/shard_map/all_to_all | solution.py:405
  86.0 0.1 copy.13
  86.1 7.3 %all_gather.3 = bf16[2,256,256]{2,1,0:T(8,128)(2,1)S(1)} all-gather(bf16[2,64,256]{2,1,0:T(8,128)(2,1)S(1)} %reshape.23), channel_id=1, replica_groups=mesh['dp'=64,'group'=4] {'group'}, dimensions={1}, use_global_device_ids=true | all-gather | bytes 327680 | tf_op jit(solution)/shard_map/all_gather | solution.py:411
  93.4 0.7 copy.15
  (20 shorter events, 0.1 us)
Async XLA Ops:
  0.6 7.2 %copy-start.1 = (bf16[2,256,256]{2,1,0:T(8,128)(2,1)S(1)}, bf16[2,256,256]{2,1,0:T(8,128)(2,1)}, u32[]{:S(2)}) copy-start(bf16[2,256,256]{2,1,0:T(8,128)(2,1)} %acts_ref.12) | copy-start | bytes 786436
  0.6 7.2 %copy-start = (bf16[2,256,4096]{2,1,0:T(8,128)(2,1)S(1)}, bf16[2,256,4096]{2,1,0:T(8,128)(2,1)}, u32[]{:S(2)}) copy-start(bf16[2,256,4096]{2,1,0:T(8,128)(2,1)} %grads_ref.15) | copy-start | bytes 12582916
  4.0 20.4 %collective-permute-start = (s16[193,16,128]{2,1,0:T(8,128)(2,1)}, s16[193,16,128]{2,1,0:T(8,128)(2,1)S(1)}, u32[]{:S(2)}, u32[]{:S(2)}) collective-permute-start(s16[193,16,128]{2,1,0:T(8,128)(2,1)} %shard_map.118), channel_id=1, source_target_pairs={{0,128},{4,132},{8,136},{12,140},{16,144},{20,148},{24,152},{28,15... | collective-permute-start | bytes 2371592 | tf_op jit(solution)/shard_map/ppermute | solution.py:420
  9.5 9.6 %collective-permute-start.2 = (s16[81,16,128]{2,1,0:T(8,128)(2,1)S(1)}, s16[81,16,128]{2,1,0:T(8,128)(2,1)S(1)}, u32[]{:S(2)}, u32[]{:S(2)}) collective-permute-start(s16[81,16,128]{2,1,0:T(8,128)(2,1)S(1)} %get-tuple-element.37), channel_id=1, source_target_pairs={{0,4},{4,8},{8,12},{12,0},{16,20},{20,24},{24,28},{28,16},{32,36},... | collective-permute-start | bytes 995336 | tf_op jit(solution)/shard_map/ppermute | solution.py:420
  10.8 8.3 %collective-permute-start.3 = (s16[81,16,128]{2,1,0:T(8,128)(2,1)S(1)}, s16[81,16,128]{2,1,0:T(8,128)(2,1)S(1)}, u32[]{:S(2)}, u32[]{:S(2)}) collective-permute-start(s16[81,16,128]{2,1,0:T(8,128)(2,1)S(1)} %get-tuple-element.38), channel_id=1, source_target_pairs={{0,12},{4,0},{8,4},{12,8},{16,28},{20,16},{24,20},{28,24},{32,44},... | collective-permute-start | bytes 995336 | tf_op jit(solution)/shard_map/ppermute | solution.py:420
  14.0 14.3 %collective-permute-start.1 = (s16[81,16,128]{2,1,0:T(8,128)(2,1)S(1)}, s16[81,16,128]{2,1,0:T(8,128)(2,1)S(1)}, u32[]{:S(2)}, u32[]{:S(2)}) collective-permute-start(s16[81,16,128]{2,1,0:T(8,128)(2,1)S(1)} %get-tuple-element.36), channel_id=1, source_target_pairs={{0,12},{4,0},{8,4},{12,8},{16,28},{20,16},{24,20},{28,24},{32,44},... | collective-permute-start | bytes 995336 | tf_op jit(solution)/shard_map/ppermute | solution.py:420
  15.3 17.6 %collective-permute-start.5 = (s16[81,16,128]{2,1,0:T(8,128)(2,1)S(1)}, s16[81,16,128]{2,1,0:T(8,128)(2,1)S(1)}, u32[]{:S(2)}, u32[]{:S(2)}) collective-permute-start(s16[81,16,128]{2,1,0:T(8,128)(2,1)S(1)} %get-tuple-element.40), channel_id=1, source_target_pairs={{0,4},{4,8},{8,12},{12,0},{16,20},{20,24},{24,28},{28,16},{32,36},... | collective-permute-start | bytes 995336 | tf_op jit(solution)/shard_map/ppermute | solution.py:420
  20.9 12.7 %collective-permute-start.4 = (s16[81,16,128]{2,1,0:T(8,128)(2,1)S(1)}, s16[81,16,128]{2,1,0:T(8,128)(2,1)S(1)}, u32[]{:S(2)}, u32[]{:S(2)}) collective-permute-start(s16[81,16,128]{2,1,0:T(8,128)(2,1)S(1)} %get-tuple-element.39), channel_id=1, source_target_pairs={{0,4},{4,8},{8,12},{12,0},{16,20},{20,24},{24,28},{28,16},{32,36},... | collective-permute-start | bytes 995336 | tf_op jit(solution)/shard_map/ppermute | solution.py:420
  21.9 11.7 %collective-permute-start.6 = (s16[81,16,128]{2,1,0:T(8,128)(2,1)S(1)}, s16[81,16,128]{2,1,0:T(8,128)(2,1)S(1)}, u32[]{:S(2)}, u32[]{:S(2)}) collective-permute-start(s16[81,16,128]{2,1,0:T(8,128)(2,1)S(1)} %get-tuple-element.41), channel_id=1, source_target_pairs={{0,12},{4,0},{8,4},{12,8},{16,28},{20,16},{24,20},{28,24},{32,44},... | collective-permute-start | bytes 995336 | tf_op jit(solution)/shard_map/ppermute | solution.py:420
  25.9 15.0 %collective-permute-start.7 = (s16[49,16,128]{2,1,0:T(8,128)(2,1)S(1)}, s16[49,16,128]{2,1,0:T(8,128)(2,1)S(1)}, u32[]{:S(2)}, u32[]{:S(2)}) collective-permute-start(s16[49,16,128]{2,1,0:T(8,128)(2,1)S(1)} %get-tuple-element.34), channel_id=1, source_target_pairs={{0,16},{4,20},{8,24},{12,28},{16,0},{20,4},{24,8},{28,12},{32,48},... | collective-permute-start | bytes 602120 | tf_op jit(solution)/shard_map/ppermute | solution.py:420
  28.3 12.6 %collective-permute-start.8 = (s16[49,16,128]{2,1,0:T(8,128)(2,1)S(1)}, s16[49,16,128]{2,1,0:T(8,128)(2,1)S(1)}, u32[]{:S(2)}, u32[]{:S(2)}) collective-permute-start(s16[49,16,128]{2,1,0:T(8,128)(2,1)S(1)} %get-tuple-element.43), channel_id=1, source_target_pairs={{0,112},{4,116},{8,120},{12,124},{16,32},{20,36},{24,40},{28,44},{... | collective-permute-start | bytes 602120 | tf_op jit(solution)/shard_map/ppermute | solution.py:420
  35.2 8.4 %collective-permute-start.10 = (s16[41,16,128]{2,1,0:T(8,128)(2,1)S(1)}, s16[41,16,128]{2,1,0:T(8,128)(2,1)S(1)}, u32[]{:S(2)}, u32[]{:S(2)}) collective-permute-start(s16[41,16,128]{2,1,0:T(8,128)(2,1)S(1)} %get-tuple-element.47), channel_id=1, source_target_pairs={{0,112},{4,116},{8,120},{12,124},{16,32},{20,36},{24,40},{28,44},{... | collective-permute-start | bytes 503816 | tf_op jit(solution)/shard_map/ppermute | solution.py:420
  40.9 4.5 %collective-permute-start.9 = (s16[41,16,128]{2,1,0:T(8,128)(2,1)S(1)}, s16[41,16,128]{2,1,0:T(8,128)(2,1)S(1)}, u32[]{:S(2)}, u32[]{:S(2)}) collective-permute-start(s16[41,16,128]{2,1,0:T(8,128)(2,1)S(1)} %get-tuple-element.46), channel_id=1, source_target_pairs={{0,16},{4,20},{8,24},{12,28},{16,0},{20,4},{24,8},{28,12},{32,48},... | collective-permute-start | bytes 503816 | tf_op jit(solution)/shard_map/ppermute | solution.py:420
  42.3 21.1 %copy-start.2 = (f32[2,4,4096]{2,1,0:T(4,128)S(1)}, f32[2,4,4096]{2,1,0:T(4,128)}, u32[]{:S(2)}) copy-start(f32[2,4,4096]{2,1,0:T(4,128)} %master.1) | copy-start | bytes 393220
  42.3 21.1 %copy-start.3 = (s32[2,4,4096]{2,1,0:T(4,128)S(1)}, s32[2,4,4096]{2,1,0:T(4,128)}, u32[]{:S(2)}) copy-start(s32[2,4,4096]{2,1,0:T(4,128)} %m_codes.1) | copy-start | bytes 393220
  42.3 21.0 %copy-start.4 = (s32[2,4,4096]{2,1,0:T(4,128)S(1)}, s32[2,4,4096]{2,1,0:T(4,128)}, u32[]{:S(2)}) copy-start(s32[2,4,4096]{2,1,0:T(4,128)} %v_codes.1) | copy-start | bytes 393220
  42.3 21.0 %copy-start.5 = (f32[2,4,2]{1,2,0:T(2,128)S(1)}, f32[2,4,2]{1,2,0:T(2,128)}, u32[]{:S(2)}) copy-start(f32[2,4,2]{1,2,0:T(2,128)} %param.11) | copy-start | bytes 196
  42.4 21.0 %copy-start.6 = (f32[2,4,2]{1,2,0:T(2,128)S(1)}, f32[2,4,2]{1,2,0:T(2,128)}, u32[]{:S(2)}) copy-start(f32[2,4,2]{1,2,0:T(2,128)} %param.13) | copy-start | bytes 196
  45.7 8.3 %collective-permute-start.11 = (s16[41,16,128]{2,1,0:T(8,128)(2,1)S(1)}, s16[41,16,128]{2,1,0:T(8,128)(2,1)S(1)}, u32[]{:S(2)}, u32[]{:S(2)}) collective-permute-start(s16[41,16,128]{2,1,0:T(8,128)(2,1)S(1)} %get-tuple-element.49), channel_id=1, source_target_pairs={{0,128},{4,132},{8,136},{12,140},{16,144},{20,148},{24,152},{28,15... | collective-permute-start | bytes 503816 | tf_op jit(solution)/shard_map/ppermute | solution.py:420
  45.8 4.8 %collective-permute-start.12 = (s16[25,16,128]{2,1,0:T(8,128)(2,1)S(1)}, s16[25,16,128]{2,1,0:T(8,128)(2,1)S(1)}, u32[]{:S(2)}, u32[]{:S(2)}) collective-permute-start(s16[25,16,128]{2,1,0:T(8,128)(2,1)S(1)} %get-tuple-element.44), channel_id=1, source_target_pairs={{0,4},{4,8},{8,12},{12,0},{16,20},{20,24},{24,28},{28,16},{32,36},... | collective-permute-start | bytes 307208 | tf_op jit(solution)/shard_map/ppermute | solution.py:420
  46.6 5.8 %collective-permute-start.13 = (s16[25,16,128]{2,1,0:T(8,128)(2,1)S(1)}, s16[25,16,128]{2,1,0:T(8,128)(2,1)S(1)}, u32[]{:S(2)}, u32[]{:S(2)}) collective-permute-start(s16[25,16,128]{2,1,0:T(8,128)(2,1)S(1)} %get-tuple-element.50), channel_id=1, source_target_pairs={{0,8},{4,12},{8,0},{12,4},{16,24},{20,28},{24,16},{28,20},{32,40},... | collective-permute-start | bytes 307208 | tf_op jit(solution)/shard_map/ppermute | solution.py:420
  49.3 3.5 %collective-permute-start.14 = (s16[25,16,128]{2,1,0:T(8,128)(2,1)S(1)}, s16[25,16,128]{2,1,0:T(8,128)(2,1)S(1)}, u32[]{:S(2)}, u32[]{:S(2)}) collective-permute-start(s16[25,16,128]{2,1,0:T(8,128)(2,1)S(1)} %get-tuple-element.51), channel_id=1, source_target_pairs={{0,12},{4,0},{8,4},{12,8},{16,28},{20,16},{24,20},{28,24},{32,44},... | collective-permute-start | bytes 307208 | tf_op jit(solution)/shard_map/ppermute | solution.py:420
  54.3 6.0 %collective-permute-start.15 = (s16[17,16,128]{2,1,0:T(8,128)(2,1)S(1)}, s16[17,16,128]{2,1,0:T(8,128)(2,1)S(1)}, u32[]{:S(2)}, u32[]{:S(2)}) collective-permute-start(s16[17,16,128]{2,1,0:T(8,128)(2,1)S(1)} %get-tuple-element.53), channel_id=1, source_target_pairs={{0,32},{4,36},{8,40},{12,44},{16,48},{20,52},{24,56},{28,60},{32,6... | collective-permute-start | bytes 208904 | tf_op jit(solution)/shard_map/ppermute | solution.py:420
  54.5 7.1 %collective-permute-start.16 = (s16[17,16,128]{2,1,0:T(8,128)(2,1)S(1)}, s16[17,16,128]{2,1,0:T(8,128)(2,1)S(1)}, u32[]{:S(2)}, u32[]{:S(2)}) collective-permute-start(s16[17,16,128]{2,1,0:T(8,128)(2,1)S(1)} %get-tuple-element.54), channel_id=1, source_target_pairs={{0,64},{4,68},{8,72},{12,76},{16,80},{20,84},{24,88},{28,92},{32,9... | collective-permute-start | bytes 208904 | tf_op jit(solution)/shard_map/ppermute | solution.py:420
  57.3 6.0 %collective-permute-start.17 = (s16[17,16,128]{2,1,0:T(8,128)(2,1)S(1)}, s16[17,16,128]{2,1,0:T(8,128)(2,1)S(1)}, u32[]{:S(2)}, u32[]{:S(2)}) collective-permute-start(s16[17,16,128]{2,1,0:T(8,128)(2,1)S(1)} %get-tuple-element.55), channel_id=1, source_target_pairs={{0,96},{4,100},{8,104},{12,108},{16,112},{20,116},{24,120},{28,124... | collective-permute-start | bytes 208904 | tf_op jit(solution)/shard_map/ppermute | solution.py:420
  64.5 21.4 %all-to-all-start = ((bf16[32,16,128]{2,1,0:T(8,128)(2,1)}), bf16[32,16,128]{2,1,0:T(8,128)(2,1)S(1)}, u32[]{:S(2)}, u32[]{:S(2)}) async-start(bf16[32,16,128]{2,1,0:T(8,128)(2,1)} %get-tuple-element.61), calls=%async_computation | async-start | bytes 262144 | tf_op jit(solution)/shard_map/all_to_all | solution.py:405
